TPU v7x, 256 devices: a whole 4x4x8 slice. The times are simulated.
256 devices in a mesh: row: 32 (over x, z), col: 8 (over y, core).
Axes of the slice: x: 4, y: 4, z: 8, core: 2. Of those that a mesh axis runs over, the one named last changes fastest.
Arguments:
- tiles: bfloat16 [320, 2048, 2048], P('row', None, 'col')
- tile_row: int32 [320], P('row'), may hold values from 0 to 1
- tile_col: int32 [320], P('row'), may hold values from 0 to 63, as said below
- tile_count: int32 [32], P('row'), may hold values from 1 to 10, as said below
- block_vectors: bfloat16 [64, 2048, 64], P('row', 'col')
Outputs:
- basis_out: float32 [64, 2048, 64], P('row', 'col')
Inputs may be any that keep to these rules, and one draw needn't show every extreme that they name: Index r of row uses its first tile_count[r] slots; its other slots hold unused tiles. The most, 10, is reached on some index of row in every draw. `tile_col`: the live slots of index r of row name column blocks from 2 * (r - 4) to 2 * (r + 4) - 1, and distinct pairs of row block and column block.
All inputs are finite; a program needn't handle non-finite values.
Results may differ from a plain program's by a relative error of at most 0.0035.
Values may be sent and summed in bfloat16 or wider, within the bound.
No kernel may reach another device: no remote copies, remote signals or barrier semaphores. Data moves between devices by JAX's collectives and lax.ppermute only.
A program may use at most 64 MiB of HBM per device.

v0:
```python
import math

import jax
import jax.numpy as jnp
from jax import lax
from jax.sharding import PartitionSpec as P

REACH = 4


def passed_along(value, axis, steps):
    count = lax.axis_size(axis)
    leading, last = (max(0, -steps), min(count, count - steps))
    return lax.ppermute(value, axis, [(source, source + steps) for source in range(leading, last)])


def on_device(tiles, tile_row, tile_col, tile_count, block_vectors):
    blocks, col_width, vector_count = block_vectors.shape
    tile_rows = tiles.shape[1]
    window_base = (lax.axis_index("row") - REACH) * blocks
    live_count = tile_count[0]

    def window(panel_rows):
        pieces = []
        for offset in range(REACH, -REACH, -1):
            if offset == 0:
                pieces.append(panel_rows)
            else:
                pieces.append(passed_along(panel_rows, "row", offset))
        return jnp.concatenate(pieces, axis=0)

    def apply_graph(panel_rows):
        window_rows = window(panel_rows)

        def add_tile(slot_index, running):
            tile_piece = lax.dynamic_index_in_dim(tiles, slot_index, 0, keepdims=False)
            local_index = tile_col[slot_index] - window_base
            vector_piece = lax.dynamic_index_in_dim(window_rows, local_index, 0, keepdims=False)
            product_term = jnp.dot(tile_piece, vector_piece, preferred_element_type=jnp.float32)
            row_block = tile_row[slot_index]
            current = lax.dynamic_index_in_dim(running, row_block, 0, keepdims=False)
            return lax.dynamic_update_index_in_dim(running, current + product_term, row_block, 0)

        start = jnp.zeros((blocks, tile_rows, vector_count), jnp.float32)
        running = lax.fori_loop(0, live_count, add_tile, start)
        return lax.psum_scatter(running, "col", scatter_dimension=1, tiled=True)

    first_power = apply_graph(block_vectors)
    second_power = apply_graph(first_power.astype(jnp.bfloat16))
    third_power = apply_graph(second_power.astype(jnp.bfloat16))
    vectors_wide = block_vectors.astype(jnp.float32)
    highest = lax.Precision.HIGHEST
    spread_parts = lax.psum(
        (jnp.sum(first_power * first_power), jnp.sum(vectors_wide * vectors_wide)), ("row", "col")
    )
    spread = spread_parts[0] / spread_parts[1]
    filtered = 4.0 * third_power - 3.0 * spread * first_power
    flat_rows = filtered.reshape(-1, vector_count)
    local_gram = jnp.dot(
        flat_rows.T, flat_rows, precision=highest, preferred_element_type=jnp.float32
    )
    gram_matrix = lax.psum(local_gram, ("row", "col"))
    lower_factor = jnp.linalg.cholesky(gram_matrix)
    solved = jax.scipy.linalg.solve_triangular(lower_factor, flat_rows.T, lower=True)
    total_rows = blocks * col_width * lax.axis_size("row") * lax.axis_size("col")
    return (solved.T * math.sqrt(total_rows)).reshape(blocks, col_width, vector_count)


def solution(mesh):
    in_specs = (P("row", None, "col"), P("row"), P("row"), P("row"), P("row", "col", None))
    out_specs = P("row", "col", None)
    return jax.shard_map(
        on_device, mesh=mesh, in_specs=in_specs, out_specs=out_specs, check_vma=False
    )
```

profile of v0, /device:TPU:8, one launch (start us, length us, event | category | flops | bytes accessed | tf_op | source)
XLA Modules:
  0.0 580.6 jit_solution(1864336827586316922)
XLA Ops:
  7.5 9.1 %collective-permute-start = (bf16[2,256,64]{2,1,0:T(8,128)(2,1)S(1)}, bf16[2,256,64]{2,1,0:T(8,128)(2,1)S(1)}, u32[]{:S(2)}, u32[]{:S(2)}) collective-permute-start(bf16[2,256,64]{2,1,0:T(8,128)(2,1)S(1)} %copy.19), channel_id=1, source_target_pairs={{0,32},{8,40},{16,48},{24,56},{32,64},{40,72},{48,80},{56,88},{64,... | collective-permute-start | bytes 196616 | tf_op jit(solution)/shard_map/ppermute | solution.py:14
  16.6 3.8 collective-permute-start.1
  22.0 3.8 collective-permute-start.3
  30.9 2.0 collective-permute-done.2
  32.9 6.2 %collective-permute-done.3 = bf16[2,256,64]{2,1,0:T(8,128)(2,1)S(1)} collective-permute-done((bf16[2,256,64]{2,1,0:T(8,128)(2,1)S(1)}, bf16[2,256,64]{2,1,0:T(8,128)(2,1)S(1)}, u32[]{:S(2)}, u32[]{:S(2)}) %collective-permute-start.3) | collective-permute-done | bytes 65568 | tf_op jit(solution)/shard_map/ppermute | solution.py:14
  39.1 2.5 collective-permute-done.5
  41.7 6.6 %collective-permute-done.6 = bf16[2,256,64]{2,1,0:T(8,128)(2,1)S(1)} collective-permute-done((bf16[2,256,64]{2,1,0:T(8,128)(2,1)S(1)}, bf16[2,256,64]{2,1,0:T(8,128)(2,1)S(1)}, u32[]{:S(2)}, u32[]{:S(2)}) %collective-permute-start.6) | collective-permute-done | bytes 65568 | tf_op jit(solution)/shard_map/ppermute | solution.py:14
  48.4 8.1 %while.30 = (s32[]{:T(128)}, f32[2,2048,64]{1,2,0:T(8,128)S(1)}, s32[]{:T(128)}, s32[10]{0:T(128)}, bf16[10,2048,256]{2,1,0:T(8,128)(2,1)}, /*index=5*/s32[10]{0...) while((s32[]{:T(128)}, f32[2,2048,64]{1,2,0:T(8,128)S(1)}, ...), condition=%wide.region_1.2_spmd, body=%wide.region_0.1_spmd.sunk | while | flops 67239944 | bytes 3211543 | solution.py:45
  54.2 1.7 fusion.39
  57.6 94.5 %reduce-scatter.4.cloned.1.call-done = f32[2,256,64]{1,2,0:T(8,128)} async-done(((f32[2,2048,64]{1,2,0:T(8,128)}), f32[2,256,64]{1,2,0:T(8,128)}) %reduce-scatter.4.cloned.1.call-update) | async-done | bytes 131088 | tf_op jit(solution)/shard_map/reduce_scatter | solution.py:46
  153.7 7.7 %collective-permute-start.7 = (bf16[2,256,64]{1,2,0:T(8,128)(2,1)S(1)}, bf16[2,256,64]{1,2,0:T(8,128)(2,1)S(1)}, u32[]{:S(2)}, u32[]{:S(2)}) collective-permute-start(bf16[2,256,64]{1,2,0:T(8,128)(2,1)S(1)} %get-tuple-element.203), channel_id=1, source_target_pairs={{0,32},{8,40},{16,48},{24,56},{32,64},{40,72},{48,80},{56,88},{64,... | collective-permute-start | bytes 196616 | tf_op jit(solution)/shard_map/ppermute | solution.py:14
  161.3 2.7 collective-permute-start.8
  164.1 3.7 collective-permute-start.9
  167.8 3.5 collective-permute-start.10
  175.3 2.1 collective-permute-done.11
  177.4 3.9 collective-permute-done.12
  181.4 4.8 collective-permute-done.13
  186.2 8.1 %while.31 = (s32[]{:T(128)}, f32[2,2048,64]{1,2,0:T(8,128)S(1)}, s32[]{:T(128)}, s32[10]{0:T(128)}, bf16[10,2048,256]{2,1,0:T(8,128)(2,1)}, /*index=5*/s32[10]{0...) while((s32[]{:T(128)}, f32[2,2048,64]{1,2,0:T(8,128)S(1)}, ...), condition=%wide.region_4.5_spmd, body=%wide.region_3.4_spmd.sunk | while | flops 67239944 | bytes 3178775 | solution.py:45
  194.4 1.9 copy.28
  196.4 98.3 %reduce-scatter.6.cloned.1.call-done = f32[2,256,64]{2,1,0:T(8,128)} async-done(((f32[2,2048,64]{2,1,0:T(8,128)}), f32[2,256,64]{2,1,0:T(8,128)}) %reduce-scatter.6.cloned.1.call-update) | async-done | bytes 131088 | tf_op jit(solution)/shard_map/reduce_scatter | solution.py:46
  295.6 7.8 %collective-permute-start.14 = (bf16[2,256,64]{2,1,0:T(8,128)(2,1)S(1)}, bf16[2,256,64]{2,1,0:T(8,128)(2,1)S(1)}, u32[]{:S(2)}, u32[]{:S(2)}) collective-permute-start(bf16[2,256,64]{2,1,0:T(8,128)(2,1)S(1)} %convert_element_type.10), channel_id=1, source_target_pairs={{0,32},{8,40},{16,48},{24,56},{32,64},{40,72},{48,80},{56,88},{64,... | collective-permute-start | bytes 196616 | tf_op jit(solution)/shard_map/ppermute | solution.py:14
  303.4 2.7 collective-permute-start.15
  306.2 3.8 collective-permute-start.16
  310.0 3.5 collective-permute-start.17
  318.9 2.0 collective-permute-done.16
  320.9 4.6 collective-permute-done.17
  327.9 6.7 %collective-permute-done.20 = bf16[2,256,64]{2,1,0:T(8,128)(2,1)S(1)} collective-permute-done((bf16[2,256,64]{2,1,0:T(8,128)(2,1)S(1)}, bf16[2,256,64]{2,1,0:T(8,128)(2,1)S(1)}, u32[]{:S(2)}, u32[]{:S(2)}) %collective-permute-start.20) | collective-permute-done | bytes 65568 | tf_op jit(solution)/shard_map/ppermute | solution.py:14
  334.7 8.1 %while.32 = (s32[]{:T(128)}, f32[2,2048,64]{1,2,0:T(8,128)S(1)}, s32[]{:T(128)}, s32[10]{0:T(128)}, bf16[10,2048,256]{2,1,0:T(8,128)(2,1)}, /*index=5*/s32[10]{0...) while((s32[]{:T(128)}, f32[2,2048,64]{1,2,0:T(8,128)S(1)}, ...), condition=%wide.region_7.8_spmd, body=%wide.region_6.7_spmd.sunk | while | flops 67239944 | bytes 3211543 | solution.py:45
  344.6 138.8 %all-reduce = (f32[]{:T(128)}, f32[]{:T(128)}) all-reduce(f32[]{:T(128)} %get-tuple-element.204, f32[]{:T(128)} %multiply_reduce_fusion), channel_id=1, replica_groups=mesh['row'=32,'col'=8] {'row','col'}, use_global_device_ids=true, to_apply=%region_10.11 | all-reduce | flops 2 | bytes 16 | tf_op jit(solution)/shard_map/psum | solution.py:53
  486.0 74.0 %psum.23 = f32[64,64]{0,1:T(8,128)S(1)} all-reduce(f32[64,64]{0,1:T(8,128)S(1)} %convolution_bitcast_fusion), channel_id=1, replica_groups=mesh['row'=32,'col'=8] {'row','col'}, use_global_device_ids=true, to_apply=%region_13.14 | all-reduce | flops 4096 | bytes 32768 | tf_op jit(solution)/shard_map/psum | solution.py:62
  560.1 5.8 %cholesky.16 = f32[64,64]{1,0:T(8,128)S(1)} custom-call(f32[64,64]{1,0:T(8,128)S(1)} %fusion.24), custom_call_target="Cholesky" | custom-call | tf_op jit(solution)/shard_map/jit(cholesky)/cholesky | solution.py:63
  567.2 4.9 custom-call.7
  (88 shorter events, 40.7 us)
Async XLA Ops:
  6.5 145.5 %reduce-scatter.4.cloned.1.call-start = ((), (), s32[]{:S(2)}) async-start(), calls=%async_computation.3 | async-start | bytes 1179648 | tf_op jit(solution)/shard_map/reduce_scatter | solution.py:46
  7.5 19.7 %collective-permute-start = (bf16[2,256,64]{2,1,0:T(8,128)(2,1)S(1)}, bf16[2,256,64]{2,1,0:T(8,128)(2,1)S(1)}, u32[]{:S(2)}, u32[]{:S(2)}) collective-permute-start(bf16[2,256,64]{2,1,0:T(8,128)(2,1)S(1)} %copy.19), channel_id=1, source_target_pairs={{0,32},{8,40},{16,48},{24,56},{32,64},{40,72},{48,80},{56,88},{64,... | collective-permute-start | bytes 196616 | tf_op jit(solution)/shard_map/ppermute | solution.py:14
  16.6 13.0 %collective-permute-start.1 = (bf16[2,256,64]{2,1,0:T(8,128)(2,1)S(1)}, bf16[2,256,64]{2,1,0:T(8,128)(2,1)S(1)}, u32[]{:S(2)}, u32[]{:S(2)}) collective-permute-start(bf16[2,256,64]{2,1,0:T(8,128)(2,1)S(1)} %copy.19), channel_id=1, source_target_pairs={{0,24},{8,32},{16,40},{24,48},{32,56},{40,64},{48,72},{56,80},{64,... | collective-permute-start | bytes 196616 | tf_op jit(solution)/shard_map/ppermute | solution.py:14
  20.5 12.4 %collective-permute-start.2 = (bf16[2,256,64]{2,1,0:T(8,128)(2,1)S(1)}, bf16[2,256,64]{2,1,0:T(8,128)(2,1)S(1)}, u32[]{:S(2)}, u32[]{:S(2)}) collective-permute-start(bf16[2,256,64]{2,1,0:T(8,128)(2,1)S(1)} %copy.19), channel_id=1, source_target_pairs={{0,16},{8,24},{16,32},{24,40},{32,48},{40,56},{48,64},{56,72},{64,... | collective-permute-start | bytes 196616 | tf_op jit(solution)/shard_map/ppermute | solution.py:14
  22.0 17.0 %collective-permute-start.3 = (bf16[2,256,64]{2,1,0:T(8,128)(2,1)S(1)}, bf16[2,256,64]{2,1,0:T(8,128)(2,1)S(1)}, u32[]{:S(2)}, u32[]{:S(2)}) collective-permute-start(bf16[2,256,64]{2,1,0:T(8,128)(2,1)S(1)} %copy.19), channel_id=1, source_target_pairs={{0,8},{8,16},{16,24},{24,32},{32,40},{40,48},{48,56},{56,64},{64,7... | collective-permute-start | bytes 196616 | tf_op jit(solution)/shard_map/ppermute | solution.py:14
  25.9 13.2 %collective-permute-start.4 = (bf16[2,256,64]{2,1,0:T(8,128)(2,1)S(1)}, bf16[2,256,64]{2,1,0:T(8,128)(2,1)S(1)}, u32[]{:S(2)}, u32[]{:S(2)}) collective-permute-start(bf16[2,256,64]{2,1,0:T(8,128)(2,1)S(1)} %copy.19), channel_id=1, source_target_pairs={{8,0},{16,8},{24,16},{32,24},{40,32},{48,40},{56,48},{64,56},{72,6... | collective-permute-start | bytes 196616 | tf_op jit(solution)/shard_map/ppermute | solution.py:14
  27.2 14.5 %collective-permute-start.5 = (bf16[2,256,64]{2,1,0:T(8,128)(2,1)S(1)}, bf16[2,256,64]{2,1,0:T(8,128)(2,1)S(1)}, u32[]{:S(2)}, u32[]{:S(2)}) collective-permute-start(bf16[2,256,64]{2,1,0:T(8,128)(2,1)S(1)} %copy.19), channel_id=1, source_target_pairs={{16,0},{24,8},{32,16},{40,24},{48,32},{56,40},{64,48},{72,56},{80,... | collective-permute-start | bytes 196616 | tf_op jit(solution)/shard_map/ppermute | solution.py:14
  29.6 18.7 %collective-permute-start.6 = (bf16[2,256,64]{2,1,0:T(8,128)(2,1)S(1)}, bf16[2,256,64]{2,1,0:T(8,128)(2,1)S(1)}, u32[]{:S(2)}, u32[]{:S(2)}) collective-permute-start(bf16[2,256,64]{2,1,0:T(8,128)(2,1)S(1)} %copy.19), channel_id=1, source_target_pairs={{24,0},{32,8},{40,16},{48,24},{56,32},{64,40},{72,48},{80,56},{88,... | collective-permute-start | bytes 196616 | tf_op jit(solution)/shard_map/ppermute | solution.py:14
  56.5 1.0 copy-start.1
  57.5 237.1 %reduce-scatter.6.cloned.1.call-start = ((), (), s32[]{:S(2)}) async-start(), calls=%async_computation.4 | async-start | bytes 2359296 | tf_op jit(solution)/shard_map/reduce_scatter | solution.py:46
  153.7 18.9 %collective-permute-start.7 = (bf16[2,256,64]{1,2,0:T(8,128)(2,1)S(1)}, bf16[2,256,64]{1,2,0:T(8,128)(2,1)S(1)}, u32[]{:S(2)}, u32[]{:S(2)}) collective-permute-start(bf16[2,256,64]{1,2,0:T(8,128)(2,1)S(1)} %get-tuple-element.203), channel_id=1, source_target_pairs={{0,32},{8,40},{16,48},{24,56},{32,64},{40,72},{48,80},{56,88},{64,... | collective-permute-start | bytes 196616 | tf_op jit(solution)/shard_map/ppermute | solution.py:14
  161.3 12.5 %collective-permute-start.8 = (bf16[2,256,64]{1,2,0:T(8,128)(2,1)S(1)}, bf16[2,256,64]{1,2,0:T(8,128)(2,1)S(1)}, u32[]{:S(2)}, u32[]{:S(2)}) collective-permute-start(bf16[2,256,64]{1,2,0:T(8,128)(2,1)S(1)} %get-tuple-element.203), channel_id=1, source_target_pairs={{0,24},{8,32},{16,40},{24,48},{32,56},{40,64},{48,72},{56,80},{64,... | collective-permute-start | bytes 196616 | tf_op jit(solution)/shard_map/ppermute | solution.py:14
  164.1 11.1 %collective-permute-start.9 = (bf16[2,256,64]{1,2,0:T(8,128)(2,1)S(1)}, bf16[2,256,64]{1,2,0:T(8,128)(2,1)S(1)}, u32[]{:S(2)}, u32[]{:S(2)}) collective-permute-start(bf16[2,256,64]{1,2,0:T(8,128)(2,1)S(1)} %get-tuple-element.203), channel_id=1, source_target_pairs={{0,16},{8,24},{16,32},{24,40},{32,48},{40,56},{48,64},{56,72},{64,... | collective-permute-start | bytes 196616 | tf_op jit(solution)/shard_map/ppermute | solution.py:14
  167.8 7.4 %collective-permute-start.10 = (bf16[2,256,64]{1,2,0:T(8,128)(2,1)S(1)}, bf16[2,256,64]{1,2,0:T(8,128)(2,1)S(1)}, u32[]{:S(2)}, u32[]{:S(2)}) collective-permute-start(bf16[2,256,64]{1,2,0:T(8,128)(2,1)S(1)} %get-tuple-element.203), channel_id=1, source_target_pairs={{0,8},{8,16},{16,24},{24,32},{32,40},{40,48},{48,56},{56,64},{64,7... | collective-permute-start | bytes 196616 | tf_op jit(solution)/shard_map/ppermute | solution.py:14
  171.2 6.2 %collective-permute-start.11 = (bf16[2,256,64]{1,2,0:T(8,128)(2,1)S(1)}, bf16[2,256,64]{1,2,0:T(8,128)(2,1)S(1)}, u32[]{:S(2)}, u32[]{:S(2)}) collective-permute-start(bf16[2,256,64]{1,2,0:T(8,128)(2,1)S(1)} %get-tuple-element.203), channel_id=1, source_target_pairs={{8,0},{16,8},{24,16},{32,24},{40,32},{48,40},{56,48},{64,56},{72,6... | collective-permute-start | bytes 196616 | tf_op jit(solution)/shard_map/ppermute | solution.py:14
  172.6 8.8 %collective-permute-start.12 = (bf16[2,256,64]{1,2,0:T(8,128)(2,1)S(1)}, bf16[2,256,64]{1,2,0:T(8,128)(2,1)S(1)}, u32[]{:S(2)}, u32[]{:S(2)}) collective-permute-start(bf16[2,256,64]{1,2,0:T(8,128)(2,1)S(1)} %get-tuple-element.203), channel_id=1, source_target_pairs={{16,0},{24,8},{32,16},{40,24},{48,32},{56,40},{64,48},{72,56},{80,... | collective-permute-start | bytes 196616 | tf_op jit(solution)/shard_map/ppermute | solution.py:14
  173.9 12.2 %collective-permute-start.13 = (bf16[2,256,64]{1,2,0:T(8,128)(2,1)S(1)}, bf16[2,256,64]{1,2,0:T(8,128)(2,1)S(1)}, u32[]{:S(2)}, u32[]{:S(2)}) collective-permute-start(bf16[2,256,64]{1,2,0:T(8,128)(2,1)S(1)} %get-tuple-element.203), channel_id=1, source_target_pairs={{24,0},{32,8},{40,16},{48,24},{56,32},{64,40},{72,48},{80,56},{88,... | collective-permute-start | bytes 196616 | tf_op jit(solution)/shard_map/ppermute | solution.py:14
  196.3 147.5 %copy-start.3 = (bf16[2,256,64]{1,2,0:T(8,128)(2,1)S(1)}, bf16[2,256,64]{1,2,0:T(8,128)(2,1)}, u32[]{:S(2)}) copy-start(bf16[2,256,64]{1,2,0:T(8,128)(2,1)} %param.15) | copy-start | bytes 196612
  196.4 288.4 %reduce-scatter.8.cloned.1.call-start = ((), (), s32[]{:S(2)}) async-start(), calls=%async_computation.5 | async-start | bytes 1179648 | tf_op jit(solution)/shard_map/reduce_scatter | solution.py:46
  295.6 189.1 %copy-start.2 = (f32[2,256,64]{1,2,0:T(8,128)S(1)}, f32[2,256,64]{1,2,0:T(8,128)}, u32[]{:S(2)}) copy-start(f32[2,256,64]{1,2,0:T(8,128)} %reduce-scatter.4.cloned.1.call-done) | copy-start | bytes 393220
  295.6 19.1 %collective-permute-start.14 = (bf16[2,256,64]{2,1,0:T(8,128)(2,1)S(1)}, bf16[2,256,64]{2,1,0:T(8,128)(2,1)S(1)}, u32[]{:S(2)}, u32[]{:S(2)}) collective-permute-start(bf16[2,256,64]{2,1,0:T(8,128)(2,1)S(1)} %convert_element_type.10), channel_id=1, source_target_pairs={{0,32},{8,40},{16,48},{24,56},{32,64},{40,72},{48,80},{56,88},{64,... | collective-permute-start | bytes 196616 | tf_op jit(solution)/shard_map/ppermute | solution.py:14
  303.4 14.2 %collective-permute-start.15 = (bf16[2,256,64]{2,1,0:T(8,128)(2,1)S(1)}, bf16[2,256,64]{2,1,0:T(8,128)(2,1)S(1)}, u32[]{:S(2)}, u32[]{:S(2)}) collective-permute-start(bf16[2,256,64]{2,1,0:T(8,128)(2,1)S(1)} %convert_element_type.10), channel_id=1, source_target_pairs={{0,24},{8,32},{16,40},{24,48},{32,56},{40,64},{48,72},{56,80},{64,... | collective-permute-start | bytes 196616 | tf_op jit(solution)/shard_map/ppermute | solution.py:14
  306.2 14.7 %collective-permute-start.16 = (bf16[2,256,64]{2,1,0:T(8,128)(2,1)S(1)}, bf16[2,256,64]{2,1,0:T(8,128)(2,1)S(1)}, u32[]{:S(2)}, u32[]{:S(2)}) collective-permute-start(bf16[2,256,64]{2,1,0:T(8,128)(2,1)S(1)} %convert_element_type.10), channel_id=1, source_target_pairs={{0,16},{8,24},{16,32},{24,40},{32,48},{40,56},{48,64},{56,72},{64,... | collective-permute-start | bytes 196616 | tf_op jit(solution)/shard_map/ppermute | solution.py:14
  310.0 15.6 %collective-permute-start.17 = (bf16[2,256,64]{2,1,0:T(8,128)(2,1)S(1)}, bf16[2,256,64]{2,1,0:T(8,128)(2,1)S(1)}, u32[]{:S(2)}, u32[]{:S(2)}) collective-permute-start(bf16[2,256,64]{2,1,0:T(8,128)(2,1)S(1)} %convert_element_type.10), channel_id=1, source_target_pairs={{0,8},{8,16},{16,24},{24,32},{32,40},{40,48},{48,56},{56,64},{64,7... | collective-permute-start | bytes 196616 | tf_op jit(solution)/shard_map/ppermute | solution.py:14
  313.5 13.1 %collective-permute-start.18 = (bf16[2,256,64]{2,1,0:T(8,128)(2,1)S(1)}, bf16[2,256,64]{2,1,0:T(8,128)(2,1)S(1)}, u32[]{:S(2)}, u32[]{:S(2)}) collective-permute-start(bf16[2,256,64]{2,1,0:T(8,128)(2,1)S(1)} %convert_element_type.10), channel_id=1, source_target_pairs={{8,0},{16,8},{24,16},{32,24},{40,32},{48,40},{56,48},{64,56},{72,6... | collective-permute-start | bytes 196616 | tf_op jit(solution)/shard_map/ppermute | solution.py:14
  314.8 13.1 %collective-permute-start.19 = (bf16[2,256,64]{2,1,0:T(8,128)(2,1)S(1)}, bf16[2,256,64]{2,1,0:T(8,128)(2,1)S(1)}, u32[]{:S(2)}, u32[]{:S(2)}) collective-permute-start(bf16[2,256,64]{2,1,0:T(8,128)(2,1)S(1)} %convert_element_type.10), channel_id=1, source_target_pairs={{16,0},{24,8},{32,16},{40,24},{48,32},{56,40},{64,48},{72,56},{80,... | collective-permute-start | bytes 196616 | tf_op jit(solution)/shard_map/ppermute | solution.py:14
  317.6 17.0 %collective-permute-start.20 = (bf16[2,256,64]{2,1,0:T(8,128)(2,1)S(1)}, bf16[2,256,64]{2,1,0:T(8,128)(2,1)S(1)}, u32[]{:S(2)}, u32[]{:S(2)}) collective-permute-start(bf16[2,256,64]{2,1,0:T(8,128)(2,1)S(1)} %convert_element_type.10), channel_id=1, source_target_pairs={{24,0},{32,8},{40,16},{48,24},{56,32},{64,40},{72,48},{80,56},{88,... | collective-permute-start | bytes 196616 | tf_op jit(solution)/shard_map/ppermute | solution.py:14
  342.9 1.0 copy-start
Sparse Core Ops, SparseCore 0:
  57.6 94.3 reduce-scatter.3
  196.5 98.1 reduce-scatter.5
  344.0 95.4 reduce-scatter.7
where the time goes:
time: 587 us; the launch traced here: 581 us
  waiting for transfers between devices  238 us (41%)
  blocking collectives  213 us (36%)
  starting transfers between devices  65.4 us (11%)
  other arithmetic  17.3 us (3%)
  between operations  14.9 us (3%)
  local copies, waits for them, and re-layouts  13.9 us (2%)
  loops' own time  11.7 us (2%)
  matrix products  6.59 us (1%)
    reduce_scatter x3, waiting for transfers between devices, apply_graph(): return lax.psum_scatter(running, 'col', scatter_dimension=1, tiled=True)  193 us
    psum x1, blocking collectives, on_device(): lax.psum((jnp.sum(first_power * first_power), jnp.sum(vectors_wide * vect...  139 us
    psum x1, blocking collectives, on_device(): gram_matrix = lax.psum(local_gram, ('row', 'col'))  74 us
    ppermute x21, starting transfers between devices, passed_along(): lax.ppermute(value, axis, [(source, source + steps) for source in range(l...  65.3 us
    ppermute x21, waiting for transfers between devices, passed_along(): lax.ppermute(value, axis, [(source, source + steps) for source in range(l...  45.3 us
  transfers between devices with their start and end apart: 24, of which 15 were waited for; matrix products, arithmetic and copies ran while one was open for 0% of the time, Pallas kernels for 0%

commit v1 on v0

v1 whole, which is shorter than its diff:
```python
import functools
import math

import jax
import jax.numpy as jnp
from jax import lax
from jax.experimental import pallas as pl
from jax.experimental.pallas import tpu as pltpu
from jax.sharding import Mesh, PartitionSpec as P

X, Z, Y, CORE = 4, 8, 4, 2
ALL = ("x", "z", "y", "core")
SLICE = 256
LANES = 128
HIGHEST = lax.Precision.HIGHEST
VMEM = pl.BlockSpec(memory_space=pltpu.VMEM)
SMEM = pl.BlockSpec(memory_space=pltpu.SMEM)


def x_neighbour_pairs():
    pairs = []
    for x in range(X):
        for z in range(Z):
            to = (x + 1) % X if z >= Z // 2 else (x - 1) % X
            for c in range(Y * CORE):
                pairs.append(((x * Z + z) * Y * CORE + c, (to * Z + z) * Y * CORE + c))
    return pairs


def window(own):
    z = lax.axis_index("z")
    other = lax.ppermute(own, ALL, x_neighbour_pairs())
    target = lax.broadcasted_iota(jnp.int32, (Z, 1, 1), 0)
    half = Z // 2
    use_other = jnp.where(z < half, target >= z + half + 1, target <= z - half)
    pieces = jnp.where(use_other, other[None], own[None])
    return lax.all_to_all(pieces, "z", 0, 0)


def apply_kernel(meta, tiles, slots, out, rhs):
    count = tiles.shape[0]
    lane = lax.broadcasted_iota(jnp.int32, (SLICE, LANES), 1)
    half = LANES // 2
    for t in range(count):
        slot, parity, block, live = (meta[1 + 4 * t + i] for i in range(4))
        vectors = slots[slot].astype(jnp.float32)
        turned = pltpu.roll(vectors, half, axis=1)
        vectors = jnp.where(parity == block, vectors, turned)
        first = block * half
        keep = (lane >= first) & (lane < first + half) & (live > 0)
        rhs[t] = jnp.where(keep, vectors, 0.0).astype(jnp.bfloat16)

    def one(y, carry):
        start = pl.multiple_of((y * CORE + meta[0]) * SLICE, SLICE)
        total = jnp.zeros((SLICE, LANES), jnp.float32)
        for t in range(count):
            total = total + jnp.dot(
                tiles[t, pl.ds(start, SLICE), :], rhs[t], preferred_element_type=jnp.float32
            )
        out[y] = total
        return carry

    lax.fori_loop(0, Y, one, 0)


def apply_half(meta, tiles, slots):
    count = tiles.shape[0]
    return pl.pallas_call(
        apply_kernel,
        out_shape=jax.ShapeDtypeStruct((Y, SLICE, LANES), jnp.float32),
        in_specs=[SMEM, VMEM, VMEM],
        out_specs=VMEM,
        scratch_shapes=[pltpu.VMEM((count, SLICE, LANES), jnp.bfloat16)],
        cost_estimate=pl.CostEstimate(
            flops=2 * count * Y * SLICE * SLICE * LANES * 2,
            bytes_accessed=count * Y * SLICE * SLICE * 2,
            transcendentals=0,
        ),
    )(meta, tiles, slots)


def summed_over_col(meta_send, meta_keep, tiles, slots):
    sent = apply_half(meta_send, tiles, slots)
    received = lax.ppermute(sent, "core", [(0, 1), (1, 0)])
    kept = apply_half(meta_keep, tiles, slots)
    pieces = lax.all_to_all(kept + received, "y", 0, 0)
    return jnp.sum(pieces, axis=0)


def total_over_all(value):
    value = value + lax.ppermute(value, "core", [(0, 1), (1, 0)])
    for axes, size in ((("x", "y"), X * Y), (("z",), Z)):
        copies = jnp.broadcast_to(value[None], (size,) + value.shape)
        value = jnp.sum(lax.all_to_all(copies, axes, 0, 0), axis=0)
    return value


def gram_kernel(spread, third, first, filtered, gram):
    value = 4.0 * third[...] - 3.0 * spread[0] * first[...]
    filtered[...] = value
    full = lax.dot_general(
        value, value, (((0,), (0,)), ((), ())), precision=HIGHEST, preferred_element_type=jnp.float32
    )
    half = LANES // 2
    gram64 = full[:half, :half] + full[half:, half:]
    gram[...] = jnp.concatenate([gram64[: half // 2], gram64[half // 2 :]], axis=1)


def finish_kernel(scale, gram, filtered, out):
    half = LANES // 2
    packed = gram[...]
    square = jnp.concatenate([packed[:, :half], packed[:, half:]], axis=0)
    row = lax.broadcasted_iota(jnp.int32, (half, LANES), 0)
    lane = lax.broadcasted_iota(jnp.int32, (half, LANES), 1)
    unit = jnp.where(lane - half == row, 1.0, 0.0)
    work = jnp.where(lane < half, jnp.concatenate([square, square], axis=1), unit)
    rows = lax.broadcasted_iota(jnp.int32, (half, 1), 0)
    pivots = jnp.zeros((half, 1), jnp.float32)
    for k in range(half):
        column = work[:, k : k + 1]
        pivot = work[k : k + 1, k : k + 1]
        pivots = jnp.where(rows == k, pivot, pivots)
        factor = jnp.where(rows > k, column / pivot, 0.0)
        work = work - factor * work[k : k + 1, :]
    inverse = work[:, half:] * (scale / jnp.sqrt(pivots))
    for block in range(2):
        out[block] = lax.dot_general(
            inverse,
            filtered[:, block * half : (block + 1) * half],
            (((1,), (1,)), ((), ())),
            precision=HIGHEST,
            preferred_element_type=jnp.float32,
        )


def on_device(tiles, tile_row, tile_col, tile_count, block_vectors):
    blocks, rows, vectors = block_vectors.shape
    count = tiles.shape[0]
    core = lax.axis_index("core")
    live = (jnp.arange(count, dtype=jnp.int32) < tile_count[0]).astype(jnp.int32)
    per_tile = jnp.stack([(tile_col // 2) % Z, tile_col % 2, tile_row, live], axis=1).reshape(-1)
    meta_keep = jnp.concatenate([core[None], per_tile])
    meta_send = jnp.concatenate([1 - core[None], per_tile])

    packed = block_vectors.transpose(1, 0, 2).reshape(rows, blocks * vectors)
    apply = functools.partial(summed_over_col, meta_send, meta_keep, tiles)
    first = apply(window(packed))
    second = apply(window(first.astype(jnp.bfloat16)))
    wide = packed.astype(jnp.float32)
    sums = jnp.stack([jnp.sum(first * first, axis=0), jnp.sum(wide * wide, axis=0)])
    sums = total_over_all(jnp.concatenate([sums, jnp.zeros((6, LANES), jnp.float32)]))
    spread = jnp.sum(sums[0]) / jnp.sum(sums[1])
    third = apply(window(second.astype(jnp.bfloat16)))

    filtered, gram = pl.pallas_call(
        gram_kernel,
        out_shape=(
            jax.ShapeDtypeStruct((rows, LANES), jnp.float32),
            jax.ShapeDtypeStruct((vectors // 2, LANES), jnp.float32),
        ),
        in_specs=[SMEM, VMEM, VMEM],
        out_specs=(VMEM, VMEM),
    )(spread[None], third, first)
    gram = total_over_all(gram)
    total_rows = blocks * rows * X * Z * Y * CORE
    out = pl.pallas_call(
        functools.partial(finish_kernel, math.sqrt(total_rows)),
        out_shape=jax.ShapeDtypeStruct((blocks, vectors, rows), jnp.float32),
        in_specs=[VMEM, VMEM],
        out_specs=VMEM,
    )(gram, filtered)
    return out.transpose(0, 2, 1)


def solution(mesh):
    grid = Mesh(mesh.devices.reshape(X, Z, Y, CORE), ALL)
    row, col = ("x", "z"), ("y", "core")
    in_specs = (P(row, None, col), P(row), P(row), P(row), P(row, col, None))
    return jax.shard_map(
        on_device, mesh=grid, in_specs=in_specs, out_specs=P(row, col, None), check_vma=False
    )
```

time: 587 us -> 229 us (0.39)
  waiting for transfers between devices: 238 us -> 44 us
  blocking collectives: 213 us -> 85.8 us
  Pallas kernels: 0 us -> 52.6 us
  starting transfers between devices: 65.4 us -> 28.8 us
  between operations: 14.9 us -> 2.15 us
  loops' own time: 11.7 us -> 0 us
  local copies, waits for them, and re-layouts: 13.9 us -> 3.53 us
  matrix products: 6.59 us -> 0 us
  other arithmetic: 17.3 us -> 11.1 us
    psum x2 -> x0, blocking collectives: 213 us -> none  [the longest x1 139 us: on_device(): lax.psum((jnp.sum(first_power * first_power), jnp.sum(vectors_wide * vect...]
    reduce_scatter x3 -> x0, waiting for transfers between devices: 193 us -> none  [apply_graph(): return lax.psum_scatter(running, 'col', scatter_dimension=1, tiled=True)]
    all_to_all x0 -> x6, blocking collectives: none -> 85.8 us  [the longest x3 40.3 us: total_over_all(): value = jnp.sum(lax.all_to_all(copies, axes, 0, 0), axis=0)]
    ppermute x21 -> x8, starting transfers between devices: 65.3 us -> 7.83 us  [the longest x3 7.28 us: window(): other = lax.ppermute(own, ALL, x_neighbour_pairs())]
    pallas_call x0 -> x8, Pallas kernels: none -> 52.6 us  [the longest x6 42.7 us: apply_half(): pl.pallas_call(apply_kernel, out_shape=jax.ShapeDtypeStruct((Y, SLICE, LA...]
    ppermute x21 -> x8, waiting for transfers between devices: 45.3 us -> 9.23 us  [the longest x3 6.52 us: window(): other = lax.ppermute(own, ALL, x_neighbour_pairs())]
    all_to_all x0 -> x4, waiting for transfers between devices: none -> 34.7 us  [the longest x2 29.6 us: window(): return lax.all_to_all(pieces, 'z', 0, 0)]
    all_to_all x0 -> x4, starting transfers between devices: none -> 21 us  [the longest x2 12.8 us: window(): return lax.all_to_all(pieces, 'z', 0, 0)]
  transfers between devices with their start and end apart: 24 -> 12, of which waited for: 15 -> 8; matrix products, arithmetic and copies ran while one was open for 0% -> 3% of each run, Pallas kernels for 0% -> 9%
where the time goes in v1:
time: 229 us; the launch traced here: 228 us
  blocking collectives  85.8 us (37%)
  Pallas kernels  52.6 us (23%)
  waiting for transfers between devices  44 us (19%)
  starting transfers between devices  28.8 us (13%)
  other arithmetic  11.1 us (5%)
  local copies, waits for them, and re-layouts  3.53 us (2%)
    pallas_call x6, Pallas kernels, apply_half(): pl.pallas_call(apply_kernel, out_shape=jax.ShapeDtypeStruct((Y, SLICE, LA...  42.7 us
    all_to_all x3, blocking collectives, total_over_all(): value = jnp.sum(lax.all_to_all(copies, axes, 0, 0), axis=0)  40.3 us
    all_to_all x2, waiting for transfers between devices, window(): return lax.all_to_all(pieces, 'z', 0, 0)  29.6 us
    all_to_all x2, blocking collectives, summed_over_col(): pieces = lax.all_to_all(kept + received, 'y', 0, 0)  26.2 us
    all_to_all x1, blocking collectives, window(): return lax.all_to_all(pieces, 'z', 0, 0)  19.3 us
    all_to_all x2, starting transfers between devices, window(): return lax.all_to_all(pieces, 'z', 0, 0)  12.8 us
    pallas_call x1, Pallas kernels, on_device(): pl.pallas_call(functools.partial(finish_kernel, math.sqrt(total_rows)), o...  7.93 us
    ppermute x3, starting transfers between devices, window(): other = lax.ppermute(own, ALL, x_neighbour_pairs())  7.28 us
  transfers between devices with their start and end apart: 12, of which 8 were waited for; matrix products, arithmetic and copies ran while one was open for 3% of the time, Pallas kernels for 9%

profile of v1, /device:TPU:8, one launch (start us, length us, event | category | flops | bytes accessed | tf_op | source)
XLA Modules:
  0.0 228.0 jit_solution(1697848525950481318)
XLA Ops:
  1.0 2.8 %collective-permute-start = (bf16[256,128]{1,0:T(8,128)(2,1)S(1)}, bf16[256,128]{1,0:T(8,128)(2,1)S(1)}, u32[]{:S(2)}, u32[]{:S(2)}) collective-permute-start(bf16[256,128]{1,0:T(8,128)(2,1)S(1)} %copy.13), channel_id=1, source_target_pairs={{0,192},{1,193},{2,194},{3,195},{4,196},{5,197},{6,198},{7,199},{8... | collective-permute-start | bytes 196616 | tf_op jit(solution)/shard_map/ppermute | solution.py:32
  3.8 1.9 collective-permute-done
  6.6 9.3 %all-to-all-start = ((bf16[8,256,128]{2,1,0:T(8,128)(2,1)}), bf16[8,256,128]{2,1,0:T(8,128)(2,1)S(1)}, u32[]{:S(2)}, u32[]{:S(2)}) async-start(bf16[8,256,128]{2,1,0:T(8,128)(2,1)} %broadcast_select_fusion.2), calls=%async_computation | async-start | bytes 1048576 | tf_op jit(solution)/shard_map/all_to_all | solution.py:37
  18.7 13.5 %all-to-all-done.slots = bf16[8,256,128]{2,1,0:T(8,128)(2,1)S(1)} async-done(((bf16[8,256,128]{2,1,0:T(8,128)(2,1)}), bf16[8,256,128]{2,1,0:T(8,128)(2,1)S(1)}, u32[]{:S(2)}, u32[]{:S(2)}) %all-to-all-start) | async-done | bytes 524320 | tf_op jit(solution)/shard_map/all_to_all | solution.py:37
  33.0 7.1 %shard_map.56 = f32[4,256,128]{2,1,0:T(8,128)} custom-call(s32[41]{0:T(128)} %get-tuple-element.13.meta, bf16[10,2048,256]{2,1,0:T(8,128)(2,1)} %tiles.11, bf16[8,256,128]{2,1,0:T(8,128)(2,1)} %copy-done.1), custom_call_target="tpu_custom_call" | custom-call | flops 1342177280 | bytes 5242880 | tf_op jit(solution)/shard_map/pallas_call | solution.py:68
  40.1 7.1 %shard_map.55 = f32[4,256,128]{2,1,0:T(8,128)} custom-call(s32[41]{0:T(128)} %get-tuple-element.14.meta, bf16[10,2048,256]{2,1,0:T(8,128)(2,1)} %tiles.11, bf16[8,256,128]{2,1,0:T(8,128)(2,1)} %copy-done.1), custom_call_target="tpu_custom_call" | custom-call | flops 1342177280 | bytes 5242880 | tf_op jit(solution)/shard_map/pallas_call | solution.py:68
  47.2 1.1 add.40
  48.3 13.4 %all_to_all.50 = f32[4,256,128]{2,1,0:T(8,128)S(1)} all-to-all(f32[4,256,128]{2,1,0:T(8,128)S(1)} %add.40), channel_id=1, replica_groups=mesh['x'=4,'z'=8,'y'=4,'core'=2] {'y'}, dimensions={0} | all-to-all | bytes 1048576 | tf_op jit(solution)/shard_map/all_to_all | solution.py:86
  61.8 1.6 collective-permute-start.3
  63.4 2.7 %collective-permute-done.3 = bf16[256,128]{1,0:T(8,128)(2,1)S(1)} collective-permute-done((bf16[256,128]{1,0:T(8,128)(2,1)S(1)}, bf16[256,128]{1,0:T(8,128)(2,1)S(1)}, u32[]{:S(2)}, u32[]{:S(2)}) %collective-permute-start.3) | collective-permute-done | bytes 65568 | tf_op jit(solution)/shard_map/ppermute | solution.py:32
  66.3 19.3 %all_to_all.51.slots = bf16[8,256,128]{2,1,0:T(8,128)(2,1)} all-to-all(bf16[8,256,128]{2,1,0:T(8,128)(2,1)S(1)} %broadcast_select_fusion.1), channel_id=1, replica_groups=mesh['x'=4,'z'=8,'y'=4,'core'=2] {'z'}, dimensions={0} | all-to-all | bytes 1048576 | tf_op jit(solution)/shard_map/all_to_all | solution.py:37
  85.5 7.1 %shard_map.58 = f32[4,256,128]{2,1,0:T(8,128)} custom-call(s32[41]{0:T(128)} %get-tuple-element.13.meta, bf16[10,2048,256]{2,1,0:T(8,128)(2,1)} %tiles.11, bf16[8,256,128]{2,1,0:T(8,128)(2,1)} %all_to_all.51.slots), custom_call_target="tpu_custom_call" | custom-call | flops 1342177280 | bytes 5242880 | tf_op jit(solution)/shard_map/pallas_call | solution.py:68
  92.7 7.1 %shard_map.57 = f32[4,256,128]{2,1,0:T(8,128)} custom-call(s32[41]{0:T(128)} %get-tuple-element.14.meta, bf16[10,2048,256]{2,1,0:T(8,128)(2,1)} %tiles.11, bf16[8,256,128]{2,1,0:T(8,128)(2,1)} %all_to_all.51.slots), custom_call_target="tpu_custom_call" | custom-call | flops 1342177280 | bytes 5242880 | tf_op jit(solution)/shard_map/pallas_call | solution.py:68
  99.8 1.1 add.42
  100.9 12.8 %all_to_all.52 = f32[4,256,128]{2,1,0:T(8,128)S(1)} all-to-all(f32[4,256,128]{2,1,0:T(8,128)S(1)} %add.42), channel_id=1, replica_groups=mesh['x'=4,'z'=8,'y'=4,'core'=2] {'y'}, dimensions={0} | all-to-all | bytes 1048576 | tf_op jit(solution)/shard_map/all_to_all | solution.py:86
  113.7 2.8 %collective-permute-start.5 = (bf16[256,128]{1,0:T(8,128)(2,1)S(1)}, bf16[256,128]{1,0:T(8,128)(2,1)S(1)}, u32[]{:S(2)}, u32[]{:S(2)}) collective-permute-start(bf16[256,128]{1,0:T(8,128)(2,1)S(1)} %reduce_sum.106), channel_id=1, source_target_pairs={{0,192},{1,193},{2,194},{3,195},{4,196},{5,197},{6,198},{7,199},{8... | collective-permute-start | bytes 196616 | tf_op jit(solution)/shard_map/ppermute | solution.py:32
  116.6 1.9 collective-permute-done.5
  119.4 3.5 %all-to-all-start.6 = ((bf16[8,256,128]{2,1,0:T(8,128)(2,1)}), bf16[8,256,128]{2,1,0:T(8,128)(2,1)S(1)}, u32[]{:S(2)}, u32[]{:S(2)}) async-start(bf16[8,256,128]{2,1,0:T(8,128)(2,1)} %broadcast_select_fusion), calls=%async_computation.6 | async-start | bytes 1048576 | tf_op jit(solution)/shard_map/all_to_all | solution.py:37
  123.1 16.1 %all-to-all-done.6.slots = bf16[8,256,128]{2,1,0:T(8,128)(2,1)S(1)} async-done(((bf16[8,256,128]{2,1,0:T(8,128)(2,1)}), bf16[8,256,128]{2,1,0:T(8,128)(2,1)S(1)}, u32[]{:S(2)}, u32[]{:S(2)}) %all-to-all-start.6) | async-done | bytes 524320 | tf_op jit(solution)/shard_map/all_to_all | solution.py:37
  140.0 7.1 %shard_map.60 = f32[4,256,128]{2,1,0:T(8,128)} custom-call(s32[41]{0:T(128)} %get-tuple-element.13.meta, bf16[10,2048,256]{2,1,0:T(8,128)(2,1)} %tiles.11, bf16[8,256,128]{2,1,0:T(8,128)(2,1)} %copy-done), custom_call_target="tpu_custom_call" | custom-call | flops 1342177280 | bytes 5242880 | tf_op jit(solution)/shard_map/pallas_call | solution.py:68
  147.8 1.3 collective-permute-done.2
  149.1 12.7 %all_to_all.53 = f32[16,8,128]{2,1,0:T(8,128)S(1)} all-to-all(f32[16,8,128]{2,1,0:T(8,128)S(1)} %broadcast_in_dim.94), channel_id=1, replica_groups=mesh['x'=4,'z'=8,'y'=4,'core'=2] {'x','y'}, dimensions={0} | all-to-all | bytes 131072 | tf_op jit(solution)/shard_map/all_to_all | solution.py:94
  162.5 3.3 %all-to-all-start.3 = ((f32[8,8,128]{2,1,0:T(8,128)}), f32[8,8,128]{2,1,0:T(8,128)S(1)}, u32[]{:S(2)}, u32[]{:S(2)}) async-start(f32[8,8,128]{2,1,0:T(8,128)} %broadcast_in_dim.95), calls=%async_computation.3 | async-start | bytes 65536 | tf_op jit(solution)/shard_map/all_to_all | solution.py:94
  165.8 7.1 %shard_map.59 = f32[4,256,128]{2,1,0:T(8,128)} custom-call(s32[41]{0:T(128)} %get-tuple-element.14.meta, bf16[10,2048,256]{2,1,0:T(8,128)(2,1)} %tiles.11, bf16[8,256,128]{2,1,0:T(8,128)(2,1)} %copy-done), custom_call_target="tpu_custom_call" | custom-call | flops 1342177280 | bytes 5242880 | tf_op jit(solution)/shard_map/pallas_call | solution.py:68
  173.0 1.9 add.43
  174.9 4.9 %all-to-all-start.7 = ((f32[4,256,128]{2,1,0:T(8,128)}), f32[4,256,128]{2,1,0:T(8,128)S(1)}, u32[]{:S(2)}, u32[]{:S(2)}) async-start(f32[4,256,128]{2,1,0:T(8,128)} %add.43), calls=%async_computation.7 | async-start | bytes 1048576 | tf_op jit(solution)/shard_map/all_to_all | solution.py:86
  181.9 5.1 %all-to-all-done.7 = f32[4,256,128]{2,1,0:T(8,128)S(1)} async-done(((f32[4,256,128]{2,1,0:T(8,128)}), f32[4,256,128]{2,1,0:T(8,128)S(1)}, u32[]{:S(2)}, u32[]{:S(2)}) %all-to-all-start.7) | async-done | bytes 524320 | tf_op jit(solution)/shard_map/all_to_all | solution.py:86
  187.6 2.0 shard_map.61
  189.7 1.4 collective-permute-done.7
  191.8 11.9 %all_to_all.54 = f32[16,32,128]{2,1,0:T(8,128)S(1)} all-to-all(f32[16,32,128]{2,1,0:T(8,128)S(1)} %broadcast_in_dim.101), channel_id=1, replica_groups=mesh['x'=4,'z'=8,'y'=4,'core'=2] {'x','y'}, dimensions={0} | all-to-all | bytes 524288 | tf_op jit(solution)/shard_map/all_to_all | solution.py:94
  203.7 15.8 %all_to_all.55 = f32[8,32,128]{2,1,0:T(8,128)S(1)} all-to-all(f32[8,32,128]{2,1,0:T(8,128)S(1)} %broadcast_in_dim.102), channel_id=1, replica_groups=mesh['x'=4,'z'=8,'y'=4,'core'=2] {'z'}, dimensions={0} | all-to-all | bytes 262144 | tf_op jit(solution)/shard_map/all_to_all | solution.py:94
  220.1 7.9 %shard_map.62 = f32[2,64,256]{2,1,0:T(8,128)} custom-call(f32[32,128]{1,0:T(8,128)} %reduce_sum.109.gram, f32[256,128]{1,0:T(8,128)} %get-tuple-element.8.filtered), custom_call_target="tpu_custom_call" | custom-call | tf_op jit(solution)/shard_map/pallas_call | solution.py:166
  (48 shorter events, 11.1 us)
Async XLA Ops:
  1.0 4.7 %collective-permute-start = (bf16[256,128]{1,0:T(8,128)(2,1)S(1)}, bf16[256,128]{1,0:T(8,128)(2,1)S(1)}, u32[]{:S(2)}, u32[]{:S(2)}) collective-permute-start(bf16[256,128]{1,0:T(8,128)(2,1)S(1)} %copy.13), channel_id=1, source_target_pairs={{0,192},{1,193},{2,194},{3,195},{4,196},{5,197},{6,198},{7,199},{8... | collective-permute-start | bytes 196616 | tf_op jit(solution)/shard_map/ppermute | solution.py:32
  6.6 25.6 %all-to-all-start = ((bf16[8,256,128]{2,1,0:T(8,128)(2,1)}), bf16[8,256,128]{2,1,0:T(8,128)(2,1)S(1)}, u32[]{:S(2)}, u32[]{:S(2)}) async-start(bf16[8,256,128]{2,1,0:T(8,128)(2,1)} %broadcast_select_fusion.2), calls=%async_computation | async-start | bytes 1048576 | tf_op jit(solution)/shard_map/all_to_all | solution.py:37
  32.2 0.8 copy-start.1
  40.1 7.1 %collective-permute-start.1 = (f32[4,256,128]{2,1,0:T(8,128)}, f32[4,256,128]{2,1,0:T(8,128)S(1)}, u32[]{:S(2)}, u32[]{:S(2)}) collective-permute-start(f32[4,256,128]{2,1,0:T(8,128)} %shard_map.56), channel_id=1, source_target_pairs={{0,1},{1,0},{2,3},{3,2},{4,5},{5,4},{6,7},{7,6},{8,9},{9,8},{10,11... | collective-permute-start | bytes 1572872 | tf_op jit(solution)/shard_map/ppermute | solution.py:84
  61.8 38.0 %copy-start.2 = (f32[256,128]{1,0:T(8,128)}, f32[256,128]{1,0:T(8,128)S(1)}, u32[]{:S(2)}) copy-start(f32[256,128]{1,0:T(8,128)S(1)} %reduce_sum.99.first) | copy-start | bytes 393220
  61.8 4.3 %collective-permute-start.3 = (bf16[256,128]{1,0:T(8,128)(2,1)S(1)}, bf16[256,128]{1,0:T(8,128)(2,1)S(1)}, u32[]{:S(2)}, u32[]{:S(2)}) collective-permute-start(bf16[256,128]{1,0:T(8,128)(2,1)S(1)} %get-tuple-element.11), channel_id=1, source_target_pairs={{0,192},{1,193},{2,194},{3,195},{4,196},{5,197},{6,198},{7,199},{8... | collective-permute-start | bytes 196616 | tf_op jit(solution)/shard_map/ppermute | solution.py:32
  92.6 30.2 %copy-start.3 = (bf16[2,256,64]{1,2,0:T(8,128)(2,1)S(1)}, bf16[2,256,64]{1,2,0:T(8,128)(2,1)}, u32[]{:S(2)}) copy-start(bf16[2,256,64]{1,2,0:T(8,128)(2,1)} %param.9) | copy-start | bytes 196612
  92.6 7.1 %collective-permute-start.4 = (f32[4,256,128]{2,1,0:T(8,128)}, f32[4,256,128]{2,1,0:T(8,128)S(1)}, u32[]{:S(2)}, u32[]{:S(2)}) collective-permute-start(f32[4,256,128]{2,1,0:T(8,128)} %shard_map.58), channel_id=1, source_target_pairs={{0,1},{1,0},{2,3},{3,2},{4,5},{5,4},{6,7},{7,6},{8,9},{9,8},{10,11... | collective-permute-start | bytes 1572872 | tf_op jit(solution)/shard_map/ppermute | solution.py:84
  113.7 4.7 %collective-permute-start.5 = (bf16[256,128]{1,0:T(8,128)(2,1)S(1)}, bf16[256,128]{1,0:T(8,128)(2,1)S(1)}, u32[]{:S(2)}, u32[]{:S(2)}) collective-permute-start(bf16[256,128]{1,0:T(8,128)(2,1)S(1)} %reduce_sum.106), channel_id=1, source_target_pairs={{0,192},{1,193},{2,194},{3,195},{4,196},{5,197},{6,198},{7,199},{8... | collective-permute-start | bytes 196616 | tf_op jit(solution)/shard_map/ppermute | solution.py:32
  119.4 19.9 %all-to-all-start.6 = ((bf16[8,256,128]{2,1,0:T(8,128)(2,1)}), bf16[8,256,128]{2,1,0:T(8,128)(2,1)S(1)}, u32[]{:S(2)}, u32[]{:S(2)}) async-start(bf16[8,256,128]{2,1,0:T(8,128)(2,1)} %broadcast_select_fusion), calls=%async_computation.6 | async-start | bytes 1048576 | tf_op jit(solution)/shard_map/all_to_all | solution.py:37
  139.3 0.8 copy-start
  147.1 25.8 %collective-permute-start.6 = (f32[4,256,128]{2,1,0:T(8,128)}, f32[4,256,128]{2,1,0:T(8,128)S(1)}, u32[]{:S(2)}, u32[]{:S(2)}) collective-permute-start(f32[4,256,128]{2,1,0:T(8,128)} %shard_map.60), channel_id=1, source_target_pairs={{0,1},{1,0},{2,3},{3,2},{4,5},{5,4},{6,7},{7,6},{8,9},{9,8},{10,11... | collective-permute-start | bytes 1572872 | tf_op jit(solution)/shard_map/ppermute | solution.py:84
  147.2 1.8 collective-permute-start.2
  162.5 12.4 %all-to-all-start.3 = ((f32[8,8,128]{2,1,0:T(8,128)}), f32[8,8,128]{2,1,0:T(8,128)S(1)}, u32[]{:S(2)}, u32[]{:S(2)}) async-start(f32[8,8,128]{2,1,0:T(8,128)} %broadcast_in_dim.95), calls=%async_computation.3 | async-start | bytes 65536 | tf_op jit(solution)/shard_map/all_to_all | solution.py:94
  174.9 12.1 %all-to-all-start.7 = ((f32[4,256,128]{2,1,0:T(8,128)}), f32[4,256,128]{2,1,0:T(8,128)S(1)}, u32[]{:S(2)}, u32[]{:S(2)}) async-start(f32[4,256,128]{2,1,0:T(8,128)} %add.43), calls=%async_computation.7 | async-start | bytes 1048576 | tf_op jit(solution)/shard_map/all_to_all | solution.py:86
  189.7 1.4 collective-permute-start.7

commit v2 on v0

v2 whole, which is shorter than its diff:
```python
import functools
import math

import jax
import jax.numpy as jnp
from jax import lax
from jax.experimental import pallas as pl
from jax.experimental.pallas import tpu as pltpu
from jax.sharding import Mesh, PartitionSpec as P

X, Z, Y, CORE = 4, 8, 4, 2
ALL = ("x", "z", "y", "core")
SLICE = 256
LANES = 128
HALF = LANES // 2
EXT = 16
SUMS = 8
HIGHEST = lax.Precision.HIGHEST
VMEM = pl.BlockSpec(memory_space=pltpu.VMEM)
SMEM = pl.BlockSpec(memory_space=pltpu.SMEM)
F32, BF16 = jnp.float32, jnp.bfloat16


def call(kernel, outs, specs, *args, scratch=(), limit=8, flops=0, moved=0):
    single = not isinstance(outs[0][0], tuple)
    shapes = (outs,) if single else outs
    result = pl.pallas_call(
        kernel,
        out_shape=tuple(jax.ShapeDtypeStruct(*s) for s in shapes),
        in_specs=specs,
        out_specs=(VMEM,) * len(shapes),
        scratch_shapes=scratch,
        compiler_params=pltpu.CompilerParams(vmem_limit_bytes=limit << 20),
        cost_estimate=pl.CostEstimate(flops=flops, bytes_accessed=moved, transcendentals=0),
    )(*args)
    return result[0] if single else result


def x_neighbour_pairs():
    pairs = []
    for x in range(X):
        for z in range(Z):
            to = (x + 1) % X if z >= Z // 2 else (x - 1) % X
            for c in range(Y * CORE):
                pairs.append(((x * Z + z) * Y * CORE + c, (to * Z + z) * Y * CORE + c))
    return pairs


def split(value):
    high = value.astype(BF16).astype(F32)
    rest = value - high
    middle = rest.astype(BF16).astype(F32)
    return jnp.concatenate([high, middle, rest - middle], axis=0)


def joined(rows):
    return rows[0:2] + rows[2:4] + rows[4:6]


def pad_rows(value, count):
    return jnp.concatenate([value, jnp.zeros((count - value.shape[0], LANES), F32)], axis=0)


def pieces_kernel(stage, meta, own, other, *refs):
    out = refs[-1]
    z = meta[1]
    half = Z // 2
    for target in range(Z):
        use_other = jnp.where(z < half, z <= target - half - 1, z >= target + half)

        @pl.when(use_other)
        def _():
            out[target, :SLICE] = other[:SLICE]

        @pl.when(jnp.logical_not(use_other))
        def _():
            out[target, :SLICE] = own[:SLICE]

    if stage == 0:
        return
    theirs = other[SLICE:].astype(F32)
    if stage == 1:
        mine = own[SLICE:].astype(F32)
        extra = pad_rows(jnp.concatenate([mine[:6], theirs[:6]], axis=0), EXT)
    else:
        extra = pad_rows(split(refs[0][0:2] + joined(theirs)), EXT)
    extra = extra.astype(BF16)
    for target in range(Z):
        out[target, SLICE:] = extra


def window(stage, meta, own, *parts):
    other = lax.ppermute(own, ALL, x_neighbour_pairs())
    specs = [SMEM] + [VMEM] * (2 + len(parts))
    shape = (Z,) + own.shape
    pieces = call(functools.partial(pieces_kernel, stage), (shape, BF16), specs, meta, own, other, *parts)
    return lax.all_to_all(pieces, "z", 0, 0)


def multiply(meta, first_slice, tiles, rhs, out, sums):
    count = tiles.shape[0]
    for y in range(Y):
        start = pl.multiple_of((y * CORE + first_slice) * SLICE, SLICE)
        total = jnp.zeros((SLICE, LANES), F32)
        for t in range(count):
            total = total + jnp.dot(
                tiles[t, pl.ds(start, SLICE), :], rhs[t], preferred_element_type=F32
            )
        out[y, :SLICE] = total
        if sums is not None:
            out[y, SLICE:] = sums


def send_kernel(stage, meta, tiles, slots, out, rhs, *sums_ref):
    lane = lax.broadcasted_iota(jnp.int32, (SLICE, LANES), 1)
    for t in range(tiles.shape[0]):
        slot, parity, block, live = (meta[2 + 4 * t + i] for i in range(4))
        vectors = slots[slot, :SLICE].astype(F32)
        turned = pltpu.roll(vectors, HALF, axis=1)
        vectors = jnp.where(parity == block, vectors, turned)
        first = block * HALF
        keep = (lane >= first) & (lane < first + HALF) & (live > 0)
        rhs[t] = jnp.where(keep, vectors, 0.0).astype(BF16)
    sums = None
    if stage:
        extra = [slots[z, SLICE:].astype(F32) for z in range(Z)]
    if stage == 1:
        low, high = sum(extra[: Z // 2]), sum(extra[Z // 2 :])
        own_low, own_high = joined(low), joined(high)
        next_low, next_high = joined(low[6:12]), joined(high[6:12])
        upper = meta[1] >= Z // 2
        gathered = jnp.where(upper, own_high + next_high, own_low + next_low)
        passed = jnp.where(upper, next_high + own_low, next_low + own_high)
        sums = pad_rows(jnp.concatenate([gathered, passed], axis=0), SUMS)
        sums_ref[0][...] = sums
    if stage == 2:
        sums_ref[0][...] = pad_rows(joined(extra[0]) + joined(extra[Z // 2]), SUMS)
    multiply(meta, 1 - meta[0], tiles, rhs, out, sums)


def keep_kernel(stage, meta, tiles, rhs, *refs):
    sums = refs[0][...] if stage == 1 else None
    multiply(meta, meta[0], tiles, rhs, refs[-1], sums)


def apply_graph(stage, meta, tiles, slots):
    count = tiles.shape[0]
    rows = SLICE + (SUMS if stage == 1 else 0)
    work = dict(limit=20, flops=2 * count * Y * SLICE * SLICE * LANES, moved=count * Y * SLICE * SLICE * 2)
    outs = (((Y, rows, LANES), F32), ((count, SLICE, LANES), BF16))
    if stage:
        outs += (((SUMS, LANES), F32),)
    sent, rhs, *sums = call(
        functools.partial(send_kernel, stage), outs, [SMEM, VMEM, VMEM], meta, tiles, slots, **work
    )
    received = lax.ppermute(sent, "core", [(0, 1), (1, 0)])
    passed = sums if stage == 1 else []
    kept = call(
        functools.partial(keep_kernel, stage),
        outs[0],
        [SMEM] + [VMEM] * (2 + len(passed)),
        meta,
        tiles,
        rhs,
        *passed,
        **work,
    )
    return lax.all_to_all(kept + received, "y", 0, 0), sums


def first_kernel(pieces, vectors, first, payload):
    value = pieces[0] + pieces[1] + pieces[2] + pieces[3]
    first[...] = value
    payload[:SLICE] = value.astype(BF16)
    wide = vectors[...].astype(F32)
    sums = [jnp.sum(part * part, axis=0, keepdims=True) for part in (value, wide)]
    payload[SLICE:] = pad_rows(split(jnp.concatenate(sums, axis=0)), EXT).astype(BF16)


def second_kernel(pieces, payload, gathered):
    value = pieces[0] + pieces[1] + pieces[2] + pieces[3]
    payload[:SLICE] = value[:SLICE].astype(BF16)
    sums = value[SLICE:]
    gathered[...] = sums
    payload[SLICE:] = pad_rows(split(sums[2:4]), EXT).astype(BF16)


def gram_kernel(pieces, first, sums, filtered, gram):
    third = pieces[0] + pieces[1] + pieces[2] + pieces[3]
    totals = jnp.sum(sums[...], axis=1, keepdims=True)
    spread = totals[0:1] / totals[1:2]
    value = 4.0 * third - 3.0 * spread * first[...]
    filtered[...] = value
    full = lax.dot_general(
        value, value, (((0,), (0,)), ((), ())), precision=HIGHEST, preferred_element_type=F32
    )
    gram64 = full[:HALF, :HALF] + full[HALF:, HALF:]
    gram[...] = jnp.concatenate([gram64[: HALF // 2], gram64[HALF // 2 :]], axis=1)


def finish_kernel(scale, grams, filtered, out):
    packed = grams[0]
    for i in range(1, grams.shape[0]):
        packed = packed + grams[i]
    square = jnp.concatenate([packed[:, :HALF], packed[:, HALF:]], axis=0)
    row = lax.broadcasted_iota(jnp.int32, (HALF, LANES), 0)
    lane = lax.broadcasted_iota(jnp.int32, (HALF, LANES), 1)
    unit = jnp.where(lane - HALF == row, 1.0, 0.0)
    work = jnp.where(lane < HALF, jnp.concatenate([square, square], axis=1), unit)
    rows = lax.broadcasted_iota(jnp.int32, (HALF, 1), 0)
    for k in range(HALF - 1):
        scaled = work[k : k + 1, :] * (1.0 / work[k : k + 1, k : k + 1])
        column = jnp.where(rows > k, work[:, k : k + 1], 0.0)
        work = work - column * scaled
    pivots = jnp.sum(jnp.where(lane == row, work, 0.0), axis=1, keepdims=True)
    inverse = work[:, HALF:] * (scale / jnp.sqrt(pivots))
    for block in range(2):
        out[block] = lax.dot_general(
            inverse,
            filtered[:, block * HALF : (block + 1) * HALF],
            (((1,), (1,)), ((), ())),
            precision=HIGHEST,
            preferred_element_type=F32,
        )


def on_device(tiles, tile_row, tile_col, tile_count, block_vectors):
    blocks, rows, vectors = block_vectors.shape
    count = tiles.shape[0]
    place = jnp.stack([lax.axis_index("core"), lax.axis_index("z")])
    live = (jnp.arange(count, dtype=jnp.int32) < tile_count[0]).astype(jnp.int32)
    per_tile = jnp.stack([(tile_col // 2) % Z, tile_col % 2, tile_row, live], axis=1)
    meta = jnp.concatenate([place, per_tile.reshape(-1)])

    packed = block_vectors.transpose(1, 0, 2).reshape(rows, blocks * vectors)
    slice_shape, payload_shape = (rows, LANES), (rows + EXT, LANES)

    pieces, _ = apply_graph(0, meta, tiles, window(0, meta, packed))
    first, payload = call(
        first_kernel, ((slice_shape, F32), (payload_shape, BF16)), [VMEM, VMEM], pieces, packed
    )
    pieces, _ = apply_graph(1, meta, tiles, window(1, meta, payload))
    payload, gathered = call(
        second_kernel, ((payload_shape, BF16), ((SUMS, LANES), F32)), [VMEM], pieces
    )
    pieces, sums = apply_graph(2, meta, tiles, window(2, meta, payload, gathered))
    filtered, gram = call(
        gram_kernel,
        ((slice_shape, F32), ((vectors // 2, LANES), F32)),
        [VMEM] * 3,
        pieces,
        first,
        *sums,
    )

    gram = gram + lax.ppermute(gram, "core", [(0, 1), (1, 0)])
    grams = lax.all_to_all(jnp.broadcast_to(gram[None], (X * Y,) + gram.shape), ("x", "y"), 0, 0)
    gram = jnp.sum(grams, axis=0)
    grams = lax.all_to_all(jnp.broadcast_to(gram[None], (Z,) + gram.shape), "z", 0, 0)
    total_rows = blocks * rows * X * Z * Y * CORE
    out = call(
        functools.partial(finish_kernel, math.sqrt(total_rows)),
        ((blocks, vectors, rows), F32),
        [VMEM, VMEM],
        grams,
        filtered,
    )
    return out.transpose(0, 2, 1)


def solution(mesh):
    grid = Mesh(mesh.devices.reshape(X, Z, Y, CORE), ALL)
    row, col = ("x", "z"), ("y", "core")
    in_specs = (P(row, None, col), P(row), P(row), P(row), P(row, col, None))
    return jax.shard_map(
        on_device, mesh=grid, in_specs=in_specs, out_specs=P(row, col, None), check_vma=False
    )
```

time: 587 us -> 172 us (0.29); the launches traced: 581 us -> 172 us
  waiting for transfers between devices: 238 us -> 5.88 us
  blocking collectives: 213 us -> 129 us
  starting transfers between devices: 65.4 us -> 7.43 us
  Pallas kernels: 0 us -> 22.1 us
  other arithmetic: 17.3 us -> 1.65 us
  between operations: 14.9 us -> 0.81 us
  loops' own time: 11.7 us -> 0 us
  local copies, waits for them, and re-layouts: 13.9 us -> 5.14 us
  matrix products: 6.59 us -> 0 us
    psum x2 -> x0, blocking collectives: 213 us -> none  [the longest x1 139 us: on_device(): lax.psum((jnp.sum(first_power * first_power), jnp.sum(vectors_wide * vect...]
    reduce_scatter x3 -> x0, waiting for transfers between devices: 193 us -> none  [apply_graph(): return lax.psum_scatter(running, 'col', scatter_dimension=1, tiled=True)]
    all_to_all x0 -> x8, blocking collectives: none -> 129 us  [the longest x3 64.4 us: window(): return lax.all_to_all(pieces, 'z', 0, 0)]
    ppermute x21 -> x7, starting transfers between devices: 65.3 us -> 7.43 us  [the longest x3 7.1 us: window(): other = lax.ppermute(own, ALL, x_neighbour_pairs())]
    ppermute x21 -> x7, waiting for transfers between devices: 45.3 us -> 5.88 us  [the longest x3 4.7 us: window(): other = lax.ppermute(own, ALL, x_neighbour_pairs())]
    pallas_call x0 -> x13, Pallas kernels: none -> 22.1 us  [call(): pl.pallas_call(kernel, out_shape=tuple((jax.ShapeDtypeStruct(*s) for s in...]
    another operation x3 -> x0, loops' own time: 11.7 us -> none  [apply_graph(): running = lax.fori_loop(0, live_count, add_tile, start)]
    another operation x5 -> x2, other arithmetic: 12.1 us -> 1.34 us  [on_device(): jnp.stack([tile_col // 2 % Z, tile_col % 2, tile_row, live], axis=1)]
  transfers between devices with their start and end apart: 24 -> 7, of which waited for: 15 -> 3; matrix products, arithmetic and copies ran while one was open for 0% -> 1% of each run, Pallas kernels for 0% -> 4%
where the time goes in v2:
time: 172 us
  blocking collectives  129 us (75%)
  Pallas kernels  22.1 us (13%)
  starting transfers between devices  7.43 us (4%)
  waiting for transfers between devices  5.88 us (3%)
  local copies, waits for them, and re-layouts  5.14 us (3%)
    all_to_all x3, blocking collectives, window(): return lax.all_to_all(pieces, 'z', 0, 0)  64.4 us
    all_to_all x3, blocking collectives, apply_graph(): return (lax.all_to_all(kept + received, 'y', 0, 0), sums)  39.2 us
    pallas_call x13, Pallas kernels, call(): pl.pallas_call(kernel, out_shape=tuple((jax.ShapeDtypeStruct(*s) for s in...  22.1 us
    all_to_all x1, blocking collectives, on_device(): lax.all_to_all(jnp.broadcast_to(gram[None], (X * Y,) + gram.shape), ('x',...  13.7 us
    all_to_all x1, blocking collectives, on_device(): lax.all_to_all(jnp.broadcast_to(gram[None], (Z,) + gram.shape), 'z', 0, 0)  11.5 us
    ppermute x3, starting transfers between devices, window(): other = lax.ppermute(own, ALL, x_neighbour_pairs())  7.1 us
    ppermute x3, waiting for transfers between devices, window(): other = lax.ppermute(own, ALL, x_neighbour_pairs())  4.7 us
    unnamed x2, local copies, waits for them, and re-layouts  3.98 us
  transfers between devices with their start and end apart: 7, of which 3 were waited for; matrix products, arithmetic and copies ran while one was open for 1% of the time, Pallas kernels for 4%

profile of v2, /device:TPU:8, one launch (start us, length us, event | category | flops | bytes accessed | tf_op | source)
XLA Modules:
  0.0 171.7 jit_solution(12358031902174671860)
XLA Ops:
  0.0 0.9 copy.14.own.vectors
  1.0 2.8 %collective-permute-start = (bf16[256,128]{1,0:T(8,128)(2,1)S(1)}, bf16[256,128]{1,0:T(8,128)(2,1)S(1)}, u32[]{:S(2)}, u32[]{:S(2)}) collective-permute-start(bf16[256,128]{1,0:T(8,128)(2,1)S(1)} %copy.14.own.vectors), channel_id=1, source_target_pairs={{0,192},{1,193},{2,194},{3,195},{4,196},{5,197},{6,198},{7,199},{8... | collective-permute-start | bytes 196616 | tf_op jit(solution)/shard_map/ppermute | solution.py:93
  4.5 0.7 fusion
  5.1 0.7 pad_add_fusion
  5.8 0.1 copy.12
  6.1 0.6 shard_map.55
  6.7 25.1 %all_to_all.40.slots = bf16[8,256,128]{2,1,0:T(8,128)(2,1)S(1)} all-to-all(bf16[8,256,128]{2,1,0:T(8,128)(2,1)S(1)} %shard_map.55), channel_id=1, replica_groups=mesh['x'=4,'z'=8,'y'=4,'core'=2] {'z'}, dimensions={0} | all-to-all | bytes 1048576 | tf_op jit(solution)/shard_map/all_to_all | solution.py:97
  31.8 4.0 %copy-done = bf16[10,2048,256]{2,1,0:T(8,128)(2,1)S(1)} copy-done((bf16[10,2048,256]{2,1,0:T(8,128)(2,1)S(1)}, bf16[10,2048,256]{2,1,0:T(8,128)(2,1)}, u32[]{:S(2)}) %copy-start) | copy-done | bytes 10485784
  35.7 2.2 %shard_map.56 = (f32[4,256,128]{2,1,0:T(8,128)S(1)}, bf16[10,256,128]{2,1,0:T(8,128)(2,1)S(1)}) custom-call(s32[42]{0:T(128)S(1)} %pad_add_fusion.1.meta, bf16[10,2048,256]{2,1,0:T(8,128)(2,1)S(1)} %copy-done, bf16[8,256,128]{2,1,0:T(8,128)(2,1)S(1)} %all_to_all.40.slots), custom_call_target="tpu_custom_call" | custom-call | flops 671088640 | bytes 5242880 | tf_op jit(solution)/shard_map/pallas_call | solution.py:27
  38.0 0.1 collective-permute-start.1
  38.1 2.1 %shard_map.57 = f32[4,256,128]{2,1,0:T(8,128)S(1)} custom-call(s32[42]{0:T(128)S(1)} %pad_add_fusion.1.meta, bf16[10,2048,256]{2,1,0:T(8,128)(2,1)S(1)} %copy-done, bf16[10,256,128]{2,1,0:T(8,128)(2,1)S(1)} %get-tuple-element.19.rhs), custom_call_target="tpu_custom_call" | custom-call | flops 671088640 | bytes 5242880 | tf_op jit(solution)/shard_map/pallas_call | solution.py:27
  40.2 13.4 %all_to_all.41.pieces = f32[4,256,128]{2,1,0:T(8,128)S(1)} all-to-all(f32[4,256,128]{2,1,0:T(8,128)S(1)} %add.25), channel_id=1, replica_groups=mesh['x'=4,'z'=8,'y'=4,'core'=2] {'y'}, dimensions={0} | all-to-all | bytes 1048576 | tf_op jit(solution)/shard_map/all_to_all | solution.py:168
  53.7 1.6 collective-permute-start.2
  55.3 2.8 %collective-permute-done.2.other = bf16[272,128]{1,0:T(8,128)(2,1)S(1)} collective-permute-done((bf16[272,128]{1,0:T(8,128)(2,1)S(1)}, bf16[272,128]{1,0:T(8,128)(2,1)S(1)}, u32[]{:S(2)}, u32[]{:S(2)}) %collective-permute-start.2) | collective-permute-done | bytes 69664 | tf_op jit(solution)/shard_map/ppermute | solution.py:93
  58.1 0.6 shard_map.59
  58.7 19.5 %all_to_all.42.slots = bf16[8,272,128]{2,1,0:T(8,128)(2,1)S(1)} all-to-all(bf16[8,272,128]{2,1,0:T(8,128)(2,1)S(1)} %shard_map.59), channel_id=1, replica_groups=mesh['x'=4,'z'=8,'y'=4,'core'=2] {'z'}, dimensions={0} | all-to-all | bytes 1114112 | tf_op jit(solution)/shard_map/all_to_all | solution.py:97
  78.2 2.3 %shard_map.60 = (f32[4,264,128]{2,1,0:T(8,128)S(1)}, bf16[10,256,128]{2,1,0:T(8,128)(2,1)S(1)}, f32[8,128]{1,0:T(8,128)S(1)}) custom-call(s32[42]{0:T(128)S(1)} %pad_add_fusion.1.meta, bf16[10,2048,256]{2,1,0:T(8,128)(2,1)S(1)} %copy-done, bf16[8,272,128]{2,1,0:T(8,128)(2,1)S(1)} %all_to_all.42.slots), custom_call_target="tpu_custom_call" | custom-call | flops 671088640 | bytes 5242880 | tf_op jit(solution)/shard_map/pallas_call | solution.py:27
  80.4 0.1 collective-permute-start.3
  80.5 2.1 %shard_map.61 = f32[4,264,128]{2,1,0:T(8,128)S(1)} custom-call(s32[42]{0:T(128)S(1)} %pad_add_fusion.1.meta, bf16[10,2048,256]{2,1,0:T(8,128)(2,1)S(1)} %copy-done, bf16[10,256,128]{2,1,0:T(8,128)(2,1)S(1)} %get-tuple-element.22.rhs, f32[8,128]{1,0:T(8,128)S(1)} %get-tuple-element.23.refs_0_), custom_call_target="tpu_custom_call" | custom-call | flops 671088640 | bytes 5242880 | tf_op jit(solution)/shard_map/pallas_call | solution.py:27
  82.7 13.0 %all_to_all.43.pieces = f32[4,264,128]{2,1,0:T(8,128)S(1)} all-to-all(f32[4,264,128]{2,1,0:T(8,128)S(1)} %add.26), channel_id=1, replica_groups=mesh['x'=4,'z'=8,'y'=4,'core'=2] {'y'}, dimensions={0} | all-to-all | bytes 1081344 | tf_op jit(solution)/shard_map/all_to_all | solution.py:168
  95.7 2.6 %collective-permute-start.4 = (bf16[272,128]{1,0:T(8,128)(2,1)S(1)}, bf16[272,128]{1,0:T(8,128)(2,1)S(1)}, u32[]{:S(2)}, u32[]{:S(2)}) collective-permute-start(bf16[272,128]{1,0:T(8,128)(2,1)S(1)} %get-tuple-element.25.own), channel_id=1, source_target_pairs={{0,192},{1,193},{2,194},{3,195},{4,196},{5,197},{6,198},{7,199},{8... | collective-permute-start | bytes 208904 | tf_op jit(solution)/shard_map/ppermute | solution.py:93
  98.4 1.9 %collective-permute-done.4.other = bf16[272,128]{1,0:T(8,128)(2,1)S(1)} collective-permute-done((bf16[272,128]{1,0:T(8,128)(2,1)S(1)}, bf16[272,128]{1,0:T(8,128)(2,1)S(1)}, u32[]{:S(2)}, u32[]{:S(2)}) %collective-permute-start.4) | collective-permute-done | bytes 69664 | tf_op jit(solution)/shard_map/ppermute | solution.py:93
  100.3 0.7 shard_map.63
  101.0 19.9 %all_to_all.44.slots = bf16[8,272,128]{2,1,0:T(8,128)(2,1)S(1)} all-to-all(bf16[8,272,128]{2,1,0:T(8,128)(2,1)S(1)} %shard_map.63), channel_id=1, replica_groups=mesh['x'=4,'z'=8,'y'=4,'core'=2] {'z'}, dimensions={0} | all-to-all | bytes 1114112 | tf_op jit(solution)/shard_map/all_to_all | solution.py:97
  120.8 2.3 %shard_map.64 = (f32[4,256,128]{2,1,0:T(8,128)S(1)}, bf16[10,256,128]{2,1,0:T(8,128)(2,1)S(1)}, f32[8,128]{1,0:T(8,128)S(1)}) custom-call(s32[42]{0:T(128)S(1)} %pad_add_fusion.1.meta, bf16[10,2048,256]{2,1,0:T(8,128)(2,1)S(1)} %copy-done, bf16[8,272,128]{2,1,0:T(8,128)(2,1)S(1)} %all_to_all.44.slots), custom_call_target="tpu_custom_call" | custom-call | flops 671088640 | bytes 5242880 | tf_op jit(solution)/shard_map/pallas_call | solution.py:27
  123.2 2.1 %shard_map.65 = f32[4,256,128]{2,1,0:T(8,128)S(1)} custom-call(s32[42]{0:T(128)S(1)} %pad_add_fusion.1.meta, bf16[10,2048,256]{2,1,0:T(8,128)(2,1)S(1)} %copy-done, bf16[10,256,128]{2,1,0:T(8,128)(2,1)S(1)} %get-tuple-element.27.rhs), custom_call_target="tpu_custom_call" | custom-call | flops 671088640 | bytes 5242880 | tf_op jit(solution)/shard_map/pallas_call | solution.py:27
  125.3 12.8 %all_to_all.45.pieces = f32[4,256,128]{2,1,0:T(8,128)S(1)} all-to-all(f32[4,256,128]{2,1,0:T(8,128)S(1)} %add.27), channel_id=1, replica_groups=mesh['x'=4,'z'=8,'y'=4,'core'=2] {'y'}, dimensions={0} | all-to-all | bytes 1048576 | tf_op jit(solution)/shard_map/all_to_all | solution.py:168
  138.2 0.6 shard_map.66
  138.8 1.2 collective-permute-done.6
  140.0 13.7 %all_to_all.46 = f32[16,32,128]{2,1,0:T(8,128)S(1)} all-to-all(f32[16,32,128]{2,1,0:T(8,128)S(1)} %broadcast_in_dim.4), channel_id=1, replica_groups=mesh['x'=4,'z'=8,'y'=4,'core'=2] {'x','y'}, dimensions={0} | all-to-all | bytes 524288 | tf_op jit(solution)/shard_map/all_to_all | solution.py:257
  153.8 11.5 %all_to_all.47.grams = f32[8,32,128]{2,1,0:T(8,128)S(1)} all-to-all(f32[8,32,128]{2,1,0:T(8,128)S(1)} %broadcast_in_dim.5), channel_id=1, replica_groups=mesh['x'=4,'z'=8,'y'=4,'core'=2] {'z'}, dimensions={0} | all-to-all | bytes 262144 | tf_op jit(solution)/shard_map/all_to_all | solution.py:259
  165.2 6.5 %shard_map.67 = f32[2,64,256]{2,1,0:T(8,128)} custom-call(f32[8,32,128]{2,1,0:T(8,128)S(1)} %all_to_all.47.grams, f32[256,128]{1,0:T(8,128)S(1)} %get-tuple-element.32.filtered), custom_call_target="tpu_custom_call" | custom-call | tf_op jit(solution)/shard_map/pallas_call | solution.py:27
  (19 shorter events, 0.7 us)
Async XLA Ops:
  1.0 5.1 %collective-permute-start = (bf16[256,128]{1,0:T(8,128)(2,1)S(1)}, bf16[256,128]{1,0:T(8,128)(2,1)S(1)}, u32[]{:S(2)}, u32[]{:S(2)}) collective-permute-start(bf16[256,128]{1,0:T(8,128)(2,1)S(1)} %copy.14.own.vectors), channel_id=1, source_target_pairs={{0,192},{1,193},{2,194},{3,195},{4,196},{5,197},{6,198},{7,199},{8... | collective-permute-start | bytes 196616 | tf_op jit(solution)/shard_map/ppermute | solution.py:93
  31.8 4.0 %copy-start = (bf16[10,2048,256]{2,1,0:T(8,128)(2,1)S(1)}, bf16[10,2048,256]{2,1,0:T(8,128)(2,1)}, u32[]{:S(2)}) copy-start(bf16[10,2048,256]{2,1,0:T(8,128)(2,1)} %tiles.11) | copy-start | bytes 31457284
  38.0 2.2 %collective-permute-start.1 = (f32[4,256,128]{2,1,0:T(8,128)S(1)}, f32[4,256,128]{2,1,0:T(8,128)S(1)}, u32[]{:S(2)}, u32[]{:S(2)}) collective-permute-start(f32[4,256,128]{2,1,0:T(8,128)S(1)} %get-tuple-element.20), channel_id=1, source_target_pairs={{0,1},{1,0},{2,3},{3,2},{4,5},{5,4},{6,7},{7,6},{8,9},{9,8},{10,11... | collective-permute-start | bytes 1572872 | tf_op jit(solution)/shard_map/ppermute | solution.py:156
  53.7 4.4 %collective-permute-start.2 = (bf16[272,128]{1,0:T(8,128)(2,1)S(1)}, bf16[272,128]{1,0:T(8,128)(2,1)S(1)}, u32[]{:S(2)}, u32[]{:S(2)}) collective-permute-start(bf16[272,128]{1,0:T(8,128)(2,1)S(1)} %get-tuple-element.21.own), channel_id=1, source_target_pairs={{0,192},{1,193},{2,194},{3,195},{4,196},{5,197},{6,198},{7,199},{8... | collective-permute-start | bytes 208904 | tf_op jit(solution)/shard_map/ppermute | solution.py:93
  80.4 2.2 %collective-permute-start.3 = (f32[4,264,128]{2,1,0:T(8,128)S(1)}, f32[4,264,128]{2,1,0:T(8,128)S(1)}, u32[]{:S(2)}, u32[]{:S(2)}) collective-permute-start(f32[4,264,128]{2,1,0:T(8,128)S(1)} %get-tuple-element.24), channel_id=1, source_target_pairs={{0,1},{1,0},{2,3},{3,2},{4,5},{5,4},{6,7},{7,6},{8,9},{9,8},{10,11... | collective-permute-start | bytes 1622024 | tf_op jit(solution)/shard_map/ppermute | solution.py:156
  95.7 4.6 %collective-permute-start.4 = (bf16[272,128]{1,0:T(8,128)(2,1)S(1)}, bf16[272,128]{1,0:T(8,128)(2,1)S(1)}, u32[]{:S(2)}, u32[]{:S(2)}) collective-permute-start(bf16[272,128]{1,0:T(8,128)(2,1)S(1)} %get-tuple-element.25.own), channel_id=1, source_target_pairs={{0,192},{1,193},{2,194},{3,195},{4,196},{5,197},{6,198},{7,199},{8... | collective-permute-start | bytes 208904 | tf_op jit(solution)/shard_map/ppermute | solution.py:93
  123.1 2.2 %collective-permute-start.5 = (f32[4,256,128]{2,1,0:T(8,128)S(1)}, f32[4,256,128]{2,1,0:T(8,128)S(1)}, u32[]{:S(2)}, u32[]{:S(2)}) collective-permute-start(f32[4,256,128]{2,1,0:T(8,128)S(1)} %get-tuple-element.28), channel_id=1, source_target_pairs={{0,1},{1,0},{2,3},{3,2},{4,5},{5,4},{6,7},{7,6},{8,9},{9,8},{10,11... | collective-permute-start | bytes 1572872 | tf_op jit(solution)/shard_map/ppermute | solution.py:156
  138.7 1.2 collective-permute-start.6

commit v3 on v2

v3 whole, which is shorter than its diff:
```python
import functools
import math

import jax
import jax.numpy as jnp
from jax import lax
from jax.experimental import pallas as pl
from jax.experimental.pallas import tpu as pltpu
from jax.sharding import Mesh, PartitionSpec as P

X, Z, Y, CORE = 4, 8, 4, 2
ALL = ("x", "z", "y", "core")
SLICE = 256
LANES = 128
HALF = LANES // 2
EXT = 16
SUMS = 8
HIGHEST = lax.Precision.HIGHEST
VMEM = pl.BlockSpec(memory_space=pltpu.VMEM)
SMEM = pl.BlockSpec(memory_space=pltpu.SMEM)
F32, BF16 = jnp.float32, jnp.bfloat16


def call(kernel, outs, specs, *args, scratch=(), limit=8, flops=0, moved=0):
    single = not isinstance(outs[0][0], tuple)
    shapes = (outs,) if single else outs
    result = pl.pallas_call(
        kernel,
        out_shape=tuple(jax.ShapeDtypeStruct(*s) for s in shapes),
        in_specs=specs,
        out_specs=(VMEM,) * len(shapes),
        scratch_shapes=scratch,
        compiler_params=pltpu.CompilerParams(vmem_limit_bytes=limit << 20),
        cost_estimate=pl.CostEstimate(flops=flops, bytes_accessed=moved, transcendentals=0),
    )(*args)
    return result[0] if single else result


def x_neighbour_pairs():
    pairs = []
    for x in range(X):
        for z in range(Z):
            to = (x + 1) % X if z >= Z // 2 else (x - 1) % X
            for c in range(Y * CORE):
                pairs.append(((x * Z + z) * Y * CORE + c, (to * Z + z) * Y * CORE + c))
    return pairs


def split(value):
    high = value.astype(BF16).astype(F32)
    rest = value - high
    middle = rest.astype(BF16).astype(F32)
    return jnp.concatenate([high, middle, rest - middle], axis=0)


def joined(rows):
    return rows[0:2] + rows[2:4] + rows[4:6]


def pad_rows(value, count):
    return jnp.concatenate([value, jnp.zeros((count - value.shape[0], LANES), F32)], axis=0)


def place_kernel(tiles, token):
    token[...] = jnp.zeros_like(token)


def turned(value):
    return value.astype(F32).T.astype(BF16)


def pieces_kernel(stage, own, other, *refs):
    out = refs[-1]
    z = lax.axis_index("z")
    half = Z // 2
    if stage == 0:
        mine, theirs = turned(own[...]), turned(other[...])
    else:
        mine, theirs = own[:SLICE], other[:SLICE]
    for target in range(Z):
        use_other = jnp.where(z < half, z <= target - half - 1, z >= target + half)

        @pl.when(use_other)
        def _():
            out[target, :SLICE] = theirs

        @pl.when(jnp.logical_not(use_other))
        def _():
            out[target, :SLICE] = mine

    if stage == 0:
        return
    theirs = other[SLICE:].astype(F32)
    if stage == 1:
        mine = own[SLICE:].astype(F32)
        extra = pad_rows(jnp.concatenate([mine[:6], theirs[:6]], axis=0), EXT)
    else:
        extra = pad_rows(split(refs[0][0:2] + joined(theirs)), EXT)
    extra = extra.astype(BF16)
    for target in range(Z):
        out[target, SLICE:] = extra


def window(stage, own, *parts):
    other = lax.ppermute(own, ALL, x_neighbour_pairs())
    rows = SLICE if stage == 0 else SLICE + EXT
    pieces = call(
        functools.partial(pieces_kernel, stage),
        ((Z, rows, LANES), BF16),
        [VMEM] * (2 + len(parts)),
        own,
        other,
        *parts,
    )
    return lax.all_to_all(pieces, "z", 0, 0)


def multiply(core, steps, tiles, rhs, out, sums):
    y = lax.axis_index("y")
    for i, step in enumerate(steps):
        start = pl.multiple_of((lax.rem(y + step, Y) * CORE + core) * SLICE, SLICE)
        total = jnp.zeros((SLICE, LANES), F32)
        for t in range(tiles.shape[0]):
            total = total + jnp.dot(
                tiles[t, pl.ds(start, SLICE), :], rhs[t], preferred_element_type=F32
            )
        out[i, :SLICE] = total
        if sums is not None:
            out[i, SLICE:] = sums


def send_kernel(stage, tile_row, tile_col, tile_count, tiles, slots, out, rhs, *sums_ref):
    lane = lax.broadcasted_iota(jnp.int32, (SLICE, LANES), 1)
    for t in range(tiles.shape[0]):
        slot = lax.rem(lax.div(tile_col[t], 2), Z)
        first = tile_row[t] * HALF
        vectors = slots[slot, :SLICE].astype(F32)
        other_half = pltpu.roll(vectors, HALF, axis=1)
        vectors = jnp.where(lax.rem(tile_col[t], 2) == tile_row[t], vectors, other_half)
        keep = (lane >= first) & (lane < first + HALF) & (t < tile_count[0])
        rhs[t] = jnp.where(keep, vectors, 0.0).astype(BF16)
    sums = None
    if stage:
        extra = [slots[z, SLICE:].astype(F32) for z in range(Z)]
    if stage == 1:
        low, high = sum(extra[: Z // 2]), sum(extra[Z // 2 :])
        own_low, own_high = joined(low), joined(high)
        next_low, next_high = joined(low[6:12]), joined(high[6:12])
        upper = lax.axis_index("z") >= Z // 2
        gathered = jnp.where(upper, own_high + next_high, own_low + next_low)
        passed = jnp.where(upper, next_high + own_low, next_low + own_high)
        sums = pad_rows(jnp.concatenate([gathered, passed], axis=0), SUMS)
        sums_ref[0][...] = sums
    if stage == 2:
        sums_ref[0][...] = pad_rows(joined(extra[0]) + joined(extra[Z // 2]), SUMS)
    multiply(1 - lax.axis_index("core"), range(Y), tiles, rhs, out, sums)


def keep_kernel(stage, steps, tiles, rhs, *refs):
    sums = refs[0][...] if stage == 1 else None
    multiply(lax.axis_index("core"), steps, tiles, rhs, refs[-1], sums)


def apply_graph(stage, plan, tiles, slots):
    count = tiles.shape[0]
    rows = SLICE + (SUMS if stage == 1 else 0)

    def work(slices):
        return dict(
            limit=20,
            flops=2 * count * slices * SLICE * SLICE * LANES,
            moved=count * slices * SLICE * SLICE * 2,
        )

    outs = (((Y, rows, LANES), F32), ((count, SLICE, LANES), BF16))
    if stage:
        outs += (((SUMS, LANES), F32),)
    sent, rhs, *sums = call(
        functools.partial(send_kernel, stage), outs, [SMEM] * 3 + [VMEM] * 2, *plan, tiles, slots, **work(Y)
    )
    received = lax.ppermute(sent, "core", [(0, 1), (1, 0)])
    passed = sums if stage == 1 else []

    def keep(steps):
        return call(
            functools.partial(keep_kernel, stage, steps),
            ((len(steps), rows, LANES), F32),
            [VMEM] * (2 + len(passed)),
            tiles,
            rhs,
            *passed,
            **work(len(steps)),
        )

    away = keep(range(1, Y))
    parts = []
    for step in (2, 1, 3):
        part = away[step - 1] + received[step]
        parts.append(lax.ppermute(part, "y", [(y, (y + step) % Y) for y in range(Y)]))
    return (keep((0,)), received, *parts), sums


def added(refs):
    own, received, *parts = refs
    value = own[0] + received[0]
    for part in parts:
        value = value + part[...]
    return value


def first_kernel(*refs):
    vectors, first, payload = refs[-3:]
    value = added(refs[:-3])
    first[...] = value
    payload[:SLICE] = value.astype(BF16)
    wide = vectors[...].astype(F32)
    wide = jnp.sum(wide * wide, axis=0, keepdims=True)
    sums = jnp.sum(value * value, axis=0, keepdims=True)
    sums = jnp.concatenate([sums, wide[:, :LANES] + wide[:, LANES:]], axis=0)
    payload[SLICE:] = pad_rows(split(sums), EXT).astype(BF16)


def second_kernel(*refs):
    payload, gathered = refs[-2:]
    value = added(refs[:-2])
    payload[:SLICE] = value[:SLICE].astype(BF16)
    sums = value[SLICE:]
    gathered[...] = sums
    payload[SLICE:] = pad_rows(split(sums[2:4]), EXT).astype(BF16)


def gram_kernel(*refs):
    first, sums, filtered, gram = refs[-4:]
    third = added(refs[:-4])
    totals = jnp.sum(sums[...], axis=1, keepdims=True)
    spread = totals[0:1] / totals[1:2]
    value = 4.0 * third - 3.0 * spread * first[...]
    filtered[...] = value
    full = lax.dot_general(
        value, value, (((0,), (0,)), ((), ())), precision=HIGHEST, preferred_element_type=F32
    )
    gram64 = full[:HALF, :HALF] + full[HALF:, HALF:]
    gram[...] = jnp.concatenate([gram64[: HALF // 2], gram64[HALF // 2 :]], axis=1)


def inverse_factor(work):
    step = 8
    shape = (step, LANES)
    groups = [work[i : i + step] for i in range(0, HALF, step)]
    row = lax.broadcasted_iota(jnp.int32, shape, 0)
    for g in range(len(groups)):
        rest = range(g, len(groups))
        columns = [
            {h: jnp.broadcast_to(groups[h][:, step * g + j : step * g + j + 1], shape) for h in rest}
            for j in range(step)
        ]
        entries = [
            [jnp.broadcast_to(columns[j][g][i : i + 1], shape) for j in range(i + 1)] for i in range(step)
        ]
        rows = [jnp.broadcast_to(groups[g][i : i + 1], shape) for i in range(step)]
        pivots = entries[0][0]
        for j in range(step):
            pivot = entries[j][j]
            pivots = jnp.where(row == j, pivot, pivots)
            reciprocal = 1.0 / pivot
            scaled = rows[j] * reciprocal
            for i in range(j + 1, step):
                factor = entries[i][j] * reciprocal
                rows[i] = rows[i] - factor * rows[j]
                for m in range(j + 1, i + 1):
                    entries[i][m] = entries[i][m] - factor * entries[m][j]
                for h in rest:
                    columns[i][h] = columns[i][h] - factor * columns[j][h]
            for h in rest:
                column = columns[j][h]
                if h == g:
                    column = jnp.where(row > j, column, 0.0)
                groups[h] = groups[h] - column * scaled
        groups[g] = groups[g] / jnp.sqrt(pivots)
    return jnp.concatenate(groups, axis=0)


def finish_kernel(scale, grams, filtered, out):
    packed = grams[0]
    for i in range(1, grams.shape[0]):
        packed = packed + grams[i]
    square = jnp.concatenate([packed[:, :HALF], packed[:, HALF:]], axis=0)
    row = lax.broadcasted_iota(jnp.int32, (HALF, LANES), 0)
    lane = lax.broadcasted_iota(jnp.int32, (HALF, LANES), 1)
    unit = jnp.where(lane - HALF == row, 1.0, 0.0)
    work = jnp.where(lane < HALF, jnp.concatenate([square, square], axis=1), unit)
    inverse = inverse_factor(work)[:, HALF:] * scale
    for block in range(2):
        out[block] = lax.dot_general(
            inverse,
            filtered[:, block * HALF : (block + 1) * HALF],
            (((1,), (1,)), ((), ())),
            precision=HIGHEST,
            preferred_element_type=F32,
        )


def on_device(tiles, tile_row, tile_col, tile_count, block_vectors):
    blocks, rows, vectors = block_vectors.shape
    count = tiles.shape[0]
    plan = (tile_row, tile_col, tile_count)
    vectors_turned = block_vectors.transpose(0, 2, 1).reshape(blocks * vectors, rows)
    slice_shape, payload_shape = (rows, LANES), (rows + EXT, LANES)
    token = call(place_kernel, ((SUMS, LANES), F32), [VMEM], tiles, limit=20, moved=2 * tiles.size)
    parts, _ = apply_graph(0, plan, tiles, window(0, vectors_turned, token))
    first, payload = call(
        first_kernel,
        ((slice_shape, F32), (payload_shape, BF16)),
        [VMEM] * (len(parts) + 1),
        *parts,
        vectors_turned,
    )
    parts, _ = apply_graph(1, plan, tiles, window(1, payload))
    payload, gathered = call(
        second_kernel,
        ((payload_shape, BF16), ((SUMS, LANES), F32)),
        [VMEM] * len(parts),
        *parts,
    )
    parts, sums = apply_graph(2, plan, tiles, window(2, payload, gathered))
    filtered, gram = call(
        gram_kernel,
        ((slice_shape, F32), ((vectors // 2, LANES), F32)),
        [VMEM] * (len(parts) + 2),
        *parts,
        first,
        *sums,
    )

    gram = gram + lax.ppermute(gram, "core", [(0, 1), (1, 0)])
    grams = lax.all_to_all(jnp.broadcast_to(gram[None], (X * Y,) + gram.shape), ("x", "y"), 0, 0)
    gram = jnp.sum(grams, axis=0)
    grams = lax.all_to_all(jnp.broadcast_to(gram[None], (Z,) + gram.shape), "z", 0, 0)
    total_rows = blocks * rows * X * Z * Y * CORE
    out = call(
        functools.partial(finish_kernel, math.sqrt(total_rows)),
        ((blocks, vectors, rows), F32),
        [VMEM, VMEM],
        grams,
        filtered,
    )
    return out.transpose(0, 2, 1)


def solution(mesh):
    grid = Mesh(mesh.devices.reshape(X, Z, Y, CORE), ALL)
    row, col = ("x", "z"), ("y", "core")
    in_specs = (P(row, None, col), P(row), P(row), P(row), P(row, col, None))
    return jax.shard_map(
        on_device, mesh=grid, in_specs=in_specs, out_specs=P(row, col, None), check_vma=False
    )
```

time: 172 us -> 161 us (0.936)
  blocking collectives: 129 us -> 65.6 us
  waiting for transfers between devices: 5.88 us -> 35.3 us
  starting transfers between devices: 7.43 us -> 32.8 us
  Pallas kernels: 22.1 us -> 17 us
  local copies, waits for them, and re-layouts: 5.14 us -> 8.83 us
    all_to_all x3 -> x0, blocking collectives: 39.2 us -> none  [apply_graph(): return (lax.all_to_all(kept + received, 'y', 0, 0), sums)]
    all_to_all x3 -> x2, blocking collectives: 64.4 us -> 38.8 us  [window(): return lax.all_to_all(pieces, 'z', 0, 0)]
    ppermute x0 -> x9, starting transfers between devices: none -> 17.9 us  [apply_graph(): lax.ppermute(part, 'y', [(y, (y + step) % Y) for y in range(Y)])]
    all_to_all x0 -> x1, waiting for transfers between devices: none -> 16.6 us  [window(): return lax.all_to_all(pieces, 'z', 0, 0)]
    ppermute x0 -> x9, waiting for transfers between devices: none -> 10.9 us  [apply_graph(): lax.ppermute(part, 'y', [(y, (y + step) % Y) for y in range(Y)])]
    all_to_all x0 -> x1, starting transfers between devices: none -> 7.2 us  [window(): return lax.all_to_all(pieces, 'z', 0, 0)]
    pallas_call x13 -> x17, Pallas kernels: 22.1 us -> 17 us  [call(): pl.pallas_call(kernel, out_shape=tuple((jax.ShapeDtypeStruct(*s) for s in...]
    unnamed x2 -> x10, local copies, waits for them, and re-layouts: 3.98 us -> 8.8 us
  transfers between devices with their start and end apart: 7 -> 17, of which waited for: 3 -> 14; matrix products, arithmetic and copies ran while one was open for 1% -> 0% of each run, Pallas kernels for 4% -> 3%
where the time goes in v3:
time: 161 us; the launch traced here: 160 us
  blocking collectives  65.6 us (41%)
  waiting for transfers between devices  35.3 us (22%)
  starting transfers between devices  32.8 us (20%)
  Pallas kernels  17 us (11%)
  local copies, waits for them, and re-layouts  8.83 us (5%)
    all_to_all x2, blocking collectives, window(): return lax.all_to_all(pieces, 'z', 0, 0)  38.8 us
    ppermute x9, starting transfers between devices, apply_graph(): lax.ppermute(part, 'y', [(y, (y + step) % Y) for y in range(Y)])  17.9 us
    pallas_call x17, Pallas kernels, call(): pl.pallas_call(kernel, out_shape=tuple((jax.ShapeDtypeStruct(*s) for s in...  17 us
    all_to_all x1, waiting for transfers between devices, window(): return lax.all_to_all(pieces, 'z', 0, 0)  16.6 us
    all_to_all x1, blocking collectives, on_device(): lax.all_to_all(jnp.broadcast_to(gram[None], (X * Y,) + gram.shape), ('x',...  15.4 us
    all_to_all x1, blocking collectives, on_device(): lax.all_to_all(jnp.broadcast_to(gram[None], (Z,) + gram.shape), 'z', 0, 0)  11.5 us
    ppermute x9, waiting for transfers between devices, apply_graph(): lax.ppermute(part, 'y', [(y, (y + step) % Y) for y in range(Y)])  10.9 us
    unnamed x10, local copies, waits for them, and re-layouts  8.8 us
  transfers between devices with their start and end apart: 17, of which 14 were waited for; matrix products, arithmetic and copies ran while one was open for 0% of the time, Pallas kernels for 3%

profile of v3, /device:TPU:8, one launch (start us, length us, event | category | flops | bytes accessed | tf_op | source)
XLA Modules:
  0.0 160.5 jit_solution(15137538665923685380)
XLA Ops:
  0.0 2.8 %collective-permute-start = (bf16[128,256]{1,0:T(8,128)(2,1)}, bf16[128,256]{1,0:T(8,128)(2,1)S(1)}, u32[]{:S(2)}, u32[]{:S(2)}) collective-permute-start(bf16[128,256]{1,0:T(8,128)(2,1)} %bitcast.22), channel_id=1, source_target_pairs={{0,192},{1,193},{2,194},{3,195},{4,196},{5,197},{6,198},{7,199},{8... | collective-permute-start | bytes 196616 | tf_op jit(solution)/shard_map/ppermute | solution.py:105
  2.8 4.0 %copy-done = bf16[10,2048,256]{2,1,0:T(8,128)(2,1)S(1)} copy-done((bf16[10,2048,256]{2,1,0:T(8,128)(2,1)S(1)}, bf16[10,2048,256]{2,1,0:T(8,128)(2,1)}, u32[]{:S(2)}) %copy-start) | copy-done | bytes 10485784
  8.6 7.2 %all-to-all-start = ((bf16[8,256,128]{2,1,0:T(8,128)(2,1)}), bf16[8,256,128]{2,1,0:T(8,128)(2,1)S(1)}, u32[]{:S(2)}, u32[]{:S(2)}) async-start(bf16[8,256,128]{2,1,0:T(8,128)(2,1)} %shard_map.56), calls=%async_computation | async-start | bytes 1048576 | tf_op jit(solution)/shard_map/all_to_all | solution.py:115
  16.4 16.6 %all-to-all-done.slots = bf16[8,256,128]{2,1,0:T(8,128)(2,1)S(1)} async-done(((bf16[8,256,128]{2,1,0:T(8,128)(2,1)}), bf16[8,256,128]{2,1,0:T(8,128)(2,1)S(1)}, u32[]{:S(2)}, u32[]{:S(2)}) %all-to-all-start) | async-done | bytes 524320 | tf_op jit(solution)/shard_map/all_to_all | solution.py:115
  33.0 4.0 %copy-done.1 = bf16[10,2048,256]{2,1,0:T(8,128)(2,1)S(1)} copy-done((bf16[10,2048,256]{2,1,0:T(8,128)(2,1)S(1)}, bf16[10,2048,256]{2,1,0:T(8,128)(2,1)}, u32[]{:S(2)}) %copy-start.1) | copy-done | bytes 10485784
  37.0 2.3 %shard_map.57 = (f32[4,256,128]{2,1,0:T(8,128)S(1)}, bf16[10,256,128]{2,1,0:T(8,128)(2,1)S(1)}) custom-call(s32[10]{0:T(128)S(1)} %copy-done.3, s32[10]{0:T(128)S(1)} %copy-done.4, s32[1]{0:T(128)S(6)} %copy.6.tile_count, bf16[10,2048,256]{2,1,0:T(8,128)(2,1)S(1)} %copy-done.1, bf16[8,256,128]{2,1,0:T(8,128)(2,1)S(1)} %all-to-all-done.slots), custom_call_target="tpu_custom_call" | custom-call | flops 671088640 | bytes 5242880 | tf_op jit(solution)/shard_map/pallas_call | solution.py:27
  39.4 1.2 shard_map.59
  41.8 1.6 collective-permute-start.3
  43.4 3.5 %collective-permute-start.2 = (f32[256,128]{1,0:T(8,128)S(1)}, f32[256,128]{1,0:T(8,128)S(1)}, u32[]{:S(2)}, u32[]{:S(2)}) collective-permute-start(f32[256,128]{1,0:T(8,128)S(1)} %get-tuple-element.41), channel_id=1, source_target_pairs={{0,4},{2,6},{4,0},{6,2},{1,5},{3,7},{5,1},{7,3},{8,12},{10,14},{12... | collective-permute-start | bytes 393224 | tf_op jit(solution)/shard_map/ppermute | solution.py:199
  47.4 1.7 %collective-permute-done.3.refs_3_ = f32[256,128]{1,0:T(8,128)S(1)} collective-permute-done((f32[256,128]{1,0:T(8,128)S(1)}, f32[256,128]{1,0:T(8,128)S(1)}, u32[]{:S(2)}, u32[]{:S(2)}) %collective-permute-start.3) | collective-permute-done | bytes 131104 | tf_op jit(solution)/shard_map/ppermute | solution.py:199
  49.2 1.6 collective-permute-done.2.refs_2_
  50.8 1.8 %collective-permute-start.5 = (bf16[272,128]{1,0:T(8,128)(2,1)S(1)}, bf16[272,128]{1,0:T(8,128)(2,1)S(1)}, u32[]{:S(2)}, u32[]{:S(2)}) collective-permute-start(bf16[272,128]{1,0:T(8,128)(2,1)S(1)} %get-tuple-element.21.own), channel_id=1, source_target_pairs={{0,192},{1,193},{2,194},{3,195},{4,196},{5,197},{6,198},{7,199},{8... | collective-permute-start | bytes 208904 | tf_op jit(solution)/shard_map/ppermute | solution.py:105
  52.6 2.6 %collective-permute-done.5.other = bf16[272,128]{1,0:T(8,128)(2,1)S(1)} collective-permute-done((bf16[272,128]{1,0:T(8,128)(2,1)S(1)}, bf16[272,128]{1,0:T(8,128)(2,1)S(1)}, u32[]{:S(2)}, u32[]{:S(2)}) %collective-permute-start.5) | collective-permute-done | bytes 69664 | tf_op jit(solution)/shard_map/ppermute | solution.py:105
  55.4 19.6 %all_to_all.25.slots = bf16[8,272,128]{2,1,0:T(8,128)(2,1)S(1)} all-to-all(bf16[8,272,128]{2,1,0:T(8,128)(2,1)S(1)} %shard_map.61), channel_id=1, replica_groups=mesh['x'=4,'z'=8,'y'=4,'core'=2] {'z'}, dimensions={0} | all-to-all | bytes 1114112 | tf_op jit(solution)/shard_map/all_to_all | solution.py:115
  75.0 2.3 %shard_map.62 = (f32[4,264,128]{2,1,0:T(8,128)S(1)}, bf16[10,256,128]{2,1,0:T(8,128)(2,1)S(1)}, f32[8,128]{1,0:T(8,128)S(1)}) custom-call(s32[10]{0:T(128)S(1)} %copy-done.3, s32[10]{0:T(128)S(1)} %copy-done.4, s32[1]{0:T(128)S(6)} %copy.6.tile_count, bf16[10,2048,256]{2,1,0:T(8,128)(2,1)S(1)} %copy-done.1, bf16[8,272,128]{2,1,0:T(8,128)(2,1)S(1)} %all_to_all.25.slots), custom_call_target="tpu_custom_call" | custom-call | flops 671088640 | bytes 5242880 | tf_op jit(solution)/shard_map/pallas_call | solution.py:27
  77.4 1.2 shard_map.64
  79.3 3.3 %collective-permute-start.9 = (f32[264,128]{1,0:T(8,128)S(1)}, f32[264,128]{1,0:T(8,128)S(1)}, u32[]{:S(2)}, u32[]{:S(2)}) collective-permute-start(f32[264,128]{1,0:T(8,128)S(1)} %get-tuple-element.33), channel_id=1, source_target_pairs={{0,6},{2,0},{4,2},{6,4},{1,7},{3,1},{5,3},{7,5},{8,14},{10,8},{12,... | collective-permute-start | bytes 405512 | tf_op jit(solution)/shard_map/ppermute | solution.py:199
  82.7 2.2 %collective-permute-start.7 = (f32[264,128]{1,0:T(8,128)S(1)}, f32[264,128]{1,0:T(8,128)S(1)}, u32[]{:S(2)}, u32[]{:S(2)}) collective-permute-start(f32[264,128]{1,0:T(8,128)S(1)} %get-tuple-element.35), channel_id=1, source_target_pairs={{0,4},{2,6},{4,0},{6,2},{1,5},{3,7},{5,1},{7,3},{8,12},{10,14},{12... | collective-permute-start | bytes 405512 | tf_op jit(solution)/shard_map/ppermute | solution.py:199
  85.3 1.3 collective-permute-done.9.refs_4_
  86.6 2.5 %collective-permute-done.8.refs_3_ = f32[264,128]{1,0:T(8,128)S(1)} collective-permute-done((f32[264,128]{1,0:T(8,128)S(1)}, f32[264,128]{1,0:T(8,128)S(1)}, u32[]{:S(2)}, u32[]{:S(2)}) %collective-permute-start.8) | collective-permute-done | bytes 135200 | tf_op jit(solution)/shard_map/ppermute | solution.py:199
  89.6 2.8 %collective-permute-start.10 = (bf16[272,128]{1,0:T(8,128)(2,1)S(1)}, bf16[272,128]{1,0:T(8,128)(2,1)S(1)}, u32[]{:S(2)}, u32[]{:S(2)}) collective-permute-start(bf16[272,128]{1,0:T(8,128)(2,1)S(1)} %get-tuple-element.25.own), channel_id=1, source_target_pairs={{0,192},{1,193},{2,194},{3,195},{4,196},{5,197},{6,198},{7,199},{8... | collective-permute-start | bytes 208904 | tf_op jit(solution)/shard_map/ppermute | solution.py:105
  92.4 1.9 %collective-permute-done.10.other = bf16[272,128]{1,0:T(8,128)(2,1)S(1)} collective-permute-done((bf16[272,128]{1,0:T(8,128)(2,1)S(1)}, bf16[272,128]{1,0:T(8,128)(2,1)S(1)}, u32[]{:S(2)}, u32[]{:S(2)}) %collective-permute-start.10) | collective-permute-done | bytes 69664 | tf_op jit(solution)/shard_map/ppermute | solution.py:105
  94.5 19.1 %all_to_all.26.slots = bf16[8,272,128]{2,1,0:T(8,128)(2,1)S(1)} all-to-all(bf16[8,272,128]{2,1,0:T(8,128)(2,1)S(1)} %shard_map.66), channel_id=1, replica_groups=mesh['x'=4,'z'=8,'y'=4,'core'=2] {'z'}, dimensions={0} | all-to-all | bytes 1114112 | tf_op jit(solution)/shard_map/all_to_all | solution.py:115
  113.7 2.3 %shard_map.67 = (f32[4,256,128]{2,1,0:T(8,128)S(1)}, bf16[10,256,128]{2,1,0:T(8,128)(2,1)S(1)}, f32[8,128]{1,0:T(8,128)S(1)}) custom-call(s32[10]{0:T(128)S(1)} %copy-done.3, s32[10]{0:T(128)S(1)} %copy-done.4, s32[1]{0:T(128)S(6)} %copy.6.tile_count, bf16[10,2048,256]{2,1,0:T(8,128)(2,1)S(1)} %copy-done.1, bf16[8,272,128]{2,1,0:T(8,128)(2,1)S(1)} %all_to_all.26.slots), custom_call_target="tpu_custom_call" | custom-call | flops 671088640 | bytes 5242880 | tf_op jit(solution)/shard_map/pallas_call | solution.py:27
  116.0 1.2 shard_map.69
  118.0 3.4 %collective-permute-start.14 = (f32[256,128]{1,0:T(8,128)S(1)}, f32[256,128]{1,0:T(8,128)S(1)}, u32[]{:S(2)}, u32[]{:S(2)}) collective-permute-start(f32[256,128]{1,0:T(8,128)S(1)} %get-tuple-element.36), channel_id=1, source_target_pairs={{0,6},{2,0},{4,2},{6,4},{1,7},{3,1},{5,3},{7,5},{8,14},{10,8},{12,... | collective-permute-start | bytes 393224 | tf_op jit(solution)/shard_map/ppermute | solution.py:199
  121.4 3.4 %collective-permute-start.12 = (f32[256,128]{1,0:T(8,128)S(1)}, f32[256,128]{1,0:T(8,128)S(1)}, u32[]{:S(2)}, u32[]{:S(2)}) collective-permute-start(f32[256,128]{1,0:T(8,128)S(1)} %get-tuple-element.38), channel_id=1, source_target_pairs={{0,4},{2,6},{4,0},{6,2},{1,5},{3,7},{5,1},{7,3},{8,12},{10,14},{12... | collective-permute-start | bytes 393224 | tf_op jit(solution)/shard_map/ppermute | solution.py:199
  125.3 2.4 %collective-permute-done.13.refs_3_ = f32[256,128]{1,0:T(8,128)S(1)} collective-permute-done((f32[256,128]{1,0:T(8,128)S(1)}, f32[256,128]{1,0:T(8,128)S(1)}, u32[]{:S(2)}, u32[]{:S(2)}) %collective-permute-start.13) | collective-permute-done | bytes 131104 | tf_op jit(solution)/shard_map/ppermute | solution.py:199
  129.3 1.2 collective-permute-done.15
  130.5 15.4 %all_to_all.27 = f32[16,32,128]{2,1,0:T(8,128)S(1)} all-to-all(f32[16,32,128]{2,1,0:T(8,128)S(1)} %broadcast_in_dim.4), channel_id=1, replica_groups=mesh['x'=4,'z'=8,'y'=4,'core'=2] {'x','y'}, dimensions={0} | all-to-all | bytes 524288 | tf_op jit(solution)/shard_map/all_to_all | solution.py:336
  146.0 11.5 %all_to_all.28.grams = f32[8,32,128]{2,1,0:T(8,128)S(1)} all-to-all(f32[8,32,128]{2,1,0:T(8,128)S(1)} %broadcast_in_dim.5), channel_id=1, replica_groups=mesh['x'=4,'z'=8,'y'=4,'core'=2] {'z'}, dimensions={0} | all-to-all | bytes 262144 | tf_op jit(solution)/shard_map/all_to_all | solution.py:338
  157.4 3.1 %shard_map.71 = f32[2,64,256]{2,1,0:T(8,128)} custom-call(f32[8,32,128]{2,1,0:T(8,128)S(1)} %all_to_all.28.grams, f32[256,128]{1,0:T(8,128)S(1)} %get-tuple-element.32.filtered), custom_call_target="tpu_custom_call" | custom-call | tf_op jit(solution)/shard_map/pallas_call | solution.py:27
  (40 shorter events, 8.8 us)
Async XLA Ops:
  0.0 33.0 %copy-start.4 = (s32[10]{0:T(128)S(1)}, s32[10]{0:T(128)}, u32[]{:S(2)}) copy-start(s32[10]{0:T(128)} %tile_col.5) | copy-start | bytes 124
  0.0 33.0 %copy-start.3 = (s32[10]{0:T(128)S(1)}, s32[10]{0:T(128)}, u32[]{:S(2)}) copy-start(s32[10]{0:T(128)} %tile_row.5) | copy-start | bytes 124
  0.0 6.7 %collective-permute-start = (bf16[128,256]{1,0:T(8,128)(2,1)}, bf16[128,256]{1,0:T(8,128)(2,1)S(1)}, u32[]{:S(2)}, u32[]{:S(2)}) collective-permute-start(bf16[128,256]{1,0:T(8,128)(2,1)} %bitcast.22), channel_id=1, source_target_pairs={{0,192},{1,193},{2,194},{3,195},{4,196},{5,197},{6,198},{7,199},{8... | collective-permute-start | bytes 196616 | tf_op jit(solution)/shard_map/ppermute | solution.py:105
  2.8 4.0 %copy-start = (bf16[10,2048,256]{2,1,0:T(8,128)(2,1)S(1)}, bf16[10,2048,256]{2,1,0:T(8,128)(2,1)}, u32[]{:S(2)}) copy-start(bf16[10,2048,256]{2,1,0:T(8,128)(2,1)} %tiles.19) | copy-start | bytes 31457284
  6.7 0.8 copy-start.2
  8.6 24.4 %all-to-all-start = ((bf16[8,256,128]{2,1,0:T(8,128)(2,1)}), bf16[8,256,128]{2,1,0:T(8,128)(2,1)S(1)}, u32[]{:S(2)}, u32[]{:S(2)}) async-start(bf16[8,256,128]{2,1,0:T(8,128)(2,1)} %shard_map.56), calls=%async_computation | async-start | bytes 1048576 | tf_op jit(solution)/shard_map/all_to_all | solution.py:115
  33.0 4.0 %copy-start.1 = (bf16[10,2048,256]{2,1,0:T(8,128)(2,1)S(1)}, bf16[10,2048,256]{2,1,0:T(8,128)(2,1)}, u32[]{:S(2)}) copy-start(bf16[10,2048,256]{2,1,0:T(8,128)(2,1)} %tiles.19) | copy-start | bytes 31457284
  39.3 2.0 %collective-permute-start.1 = (f32[4,256,128]{2,1,0:T(8,128)S(1)}, f32[4,256,128]{2,1,0:T(8,128)S(1)}, u32[]{:S(2)}, u32[]{:S(2)}) collective-permute-start(f32[4,256,128]{2,1,0:T(8,128)S(1)} %get-tuple-element.20), channel_id=1, source_target_pairs={{0,1},{1,0},{2,3},{3,2},{4,5},{5,4},{6,7},{7,6},{8,9},{9,8},{10,11... | collective-permute-start | bytes 1572872 | tf_op jit(solution)/shard_map/ppermute | solution.py:181
  41.3 6.1 %collective-permute-start.4 = (f32[256,128]{1,0:T(8,128)S(1)}, f32[256,128]{1,0:T(8,128)S(1)}, u32[]{:S(2)}, u32[]{:S(2)}) collective-permute-start(f32[256,128]{1,0:T(8,128)S(1)} %get-tuple-element.39), channel_id=1, source_target_pairs={{0,6},{2,0},{4,2},{6,4},{1,7},{3,1},{5,3},{7,5},{8,14},{10,8},{12,... | collective-permute-start | bytes 393224 | tf_op jit(solution)/shard_map/ppermute | solution.py:199
  41.8 7.3 %collective-permute-start.3 = (f32[256,128]{1,0:T(8,128)S(1)}, f32[256,128]{1,0:T(8,128)S(1)}, u32[]{:S(2)}, u32[]{:S(2)}) collective-permute-start(f32[256,128]{1,0:T(8,128)S(1)} %get-tuple-element.40), channel_id=1, source_target_pairs={{0,2},{2,4},{4,6},{6,0},{1,3},{3,5},{5,7},{7,1},{8,10},{10,12},{12... | collective-permute-start | bytes 393224 | tf_op jit(solution)/shard_map/ppermute | solution.py:199
  43.4 7.3 %collective-permute-start.2 = (f32[256,128]{1,0:T(8,128)S(1)}, f32[256,128]{1,0:T(8,128)S(1)}, u32[]{:S(2)}, u32[]{:S(2)}) collective-permute-start(f32[256,128]{1,0:T(8,128)S(1)} %get-tuple-element.41), channel_id=1, source_target_pairs={{0,4},{2,6},{4,0},{6,2},{1,5},{3,7},{5,1},{7,3},{8,12},{10,14},{12... | collective-permute-start | bytes 393224 | tf_op jit(solution)/shard_map/ppermute | solution.py:199
  50.8 4.4 %collective-permute-start.5 = (bf16[272,128]{1,0:T(8,128)(2,1)S(1)}, bf16[272,128]{1,0:T(8,128)(2,1)S(1)}, u32[]{:S(2)}, u32[]{:S(2)}) collective-permute-start(bf16[272,128]{1,0:T(8,128)(2,1)S(1)} %get-tuple-element.21.own), channel_id=1, source_target_pairs={{0,192},{1,193},{2,194},{3,195},{4,196},{5,197},{6,198},{7,199},{8... | collective-permute-start | bytes 208904 | tf_op jit(solution)/shard_map/ppermute | solution.py:105
  77.3 2.0 %collective-permute-start.6 = (f32[4,264,128]{2,1,0:T(8,128)S(1)}, f32[4,264,128]{2,1,0:T(8,128)S(1)}, u32[]{:S(2)}, u32[]{:S(2)}) collective-permute-start(f32[4,264,128]{2,1,0:T(8,128)S(1)} %get-tuple-element.24), channel_id=1, source_target_pairs={{0,1},{1,0},{2,3},{3,2},{4,5},{5,4},{6,7},{7,6},{8,9},{9,8},{10,11... | collective-permute-start | bytes 1622024 | tf_op jit(solution)/shard_map/ppermute | solution.py:181
  79.3 7.3 %collective-permute-start.9 = (f32[264,128]{1,0:T(8,128)S(1)}, f32[264,128]{1,0:T(8,128)S(1)}, u32[]{:S(2)}, u32[]{:S(2)}) collective-permute-start(f32[264,128]{1,0:T(8,128)S(1)} %get-tuple-element.33), channel_id=1, source_target_pairs={{0,6},{2,0},{4,2},{6,4},{1,7},{3,1},{5,3},{7,5},{8,14},{10,8},{12,... | collective-permute-start | bytes 405512 | tf_op jit(solution)/shard_map/ppermute | solution.py:199
  82.7 6.5 %collective-permute-start.8 = (f32[264,128]{1,0:T(8,128)S(1)}, f32[264,128]{1,0:T(8,128)S(1)}, u32[]{:S(2)}, u32[]{:S(2)}) collective-permute-start(f32[264,128]{1,0:T(8,128)S(1)} %get-tuple-element.34), channel_id=1, source_target_pairs={{0,2},{2,4},{4,6},{6,0},{1,3},{3,5},{5,7},{7,1},{8,10},{10,12},{12... | collective-permute-start | bytes 405512 | tf_op jit(solution)/shard_map/ppermute | solution.py:199
  82.7 6.9 %collective-permute-start.7 = (f32[264,128]{1,0:T(8,128)S(1)}, f32[264,128]{1,0:T(8,128)S(1)}, u32[]{:S(2)}, u32[]{:S(2)}) collective-permute-start(f32[264,128]{1,0:T(8,128)S(1)} %get-tuple-element.35), channel_id=1, source_target_pairs={{0,4},{2,6},{4,0},{6,2},{1,5},{3,7},{5,1},{7,3},{8,12},{10,14},{12... | collective-permute-start | bytes 405512 | tf_op jit(solution)/shard_map/ppermute | solution.py:199
  89.6 4.8 %collective-permute-start.10 = (bf16[272,128]{1,0:T(8,128)(2,1)S(1)}, bf16[272,128]{1,0:T(8,128)(2,1)S(1)}, u32[]{:S(2)}, u32[]{:S(2)}) collective-permute-start(bf16[272,128]{1,0:T(8,128)(2,1)S(1)} %get-tuple-element.25.own), channel_id=1, source_target_pairs={{0,192},{1,193},{2,194},{3,195},{4,196},{5,197},{6,198},{7,199},{8... | collective-permute-start | bytes 208904 | tf_op jit(solution)/shard_map/ppermute | solution.py:105
  115.9 2.0 %collective-permute-start.11 = (f32[4,256,128]{2,1,0:T(8,128)S(1)}, f32[4,256,128]{2,1,0:T(8,128)S(1)}, u32[]{:S(2)}, u32[]{:S(2)}) collective-permute-start(f32[4,256,128]{2,1,0:T(8,128)S(1)} %get-tuple-element.28), channel_id=1, source_target_pairs={{0,1},{1,0},{2,3},{3,2},{4,5},{5,4},{6,7},{7,6},{8,9},{9,8},{10,11... | collective-permute-start | bytes 1572872 | tf_op jit(solution)/shard_map/ppermute | solution.py:181
  118.0 7.3 %collective-permute-start.14 = (f32[256,128]{1,0:T(8,128)S(1)}, f32[256,128]{1,0:T(8,128)S(1)}, u32[]{:S(2)}, u32[]{:S(2)}) collective-permute-start(f32[256,128]{1,0:T(8,128)S(1)} %get-tuple-element.36), channel_id=1, source_target_pairs={{0,6},{2,0},{4,2},{6,4},{1,7},{3,1},{5,3},{7,5},{8,14},{10,8},{12,... | collective-permute-start | bytes 393224 | tf_op jit(solution)/shard_map/ppermute | solution.py:199
  121.4 6.4 %collective-permute-start.13 = (f32[256,128]{1,0:T(8,128)S(1)}, f32[256,128]{1,0:T(8,128)S(1)}, u32[]{:S(2)}, u32[]{:S(2)}) collective-permute-start(f32[256,128]{1,0:T(8,128)S(1)} %get-tuple-element.37), channel_id=1, source_target_pairs={{0,2},{2,4},{4,6},{6,0},{1,3},{3,5},{5,7},{7,1},{8,10},{10,12},{12... | collective-permute-start | bytes 393224 | tf_op jit(solution)/shard_map/ppermute | solution.py:199
  121.4 7.3 %collective-permute-start.12 = (f32[256,128]{1,0:T(8,128)S(1)}, f32[256,128]{1,0:T(8,128)S(1)}, u32[]{:S(2)}, u32[]{:S(2)}) collective-permute-start(f32[256,128]{1,0:T(8,128)S(1)} %get-tuple-element.38), channel_id=1, source_target_pairs={{0,4},{2,6},{4,0},{6,2},{1,5},{3,7},{5,1},{7,3},{8,12},{10,14},{12... | collective-permute-start | bytes 393224 | tf_op jit(solution)/shard_map/ppermute | solution.py:199
  129.3 1.2 collective-permute-start.15

commit v4 on v3

--- a/solution.py
+++ b/solution.py
@@ -15,6 +15,7 @@
 HALF = LANES // 2
 EXT = 16
 SUMS = 8
+CORE_SWAP = [(0, 1), (1, 0)]
 HIGHEST = lax.Precision.HIGHEST
 VMEM = pl.BlockSpec(memory_space=pltpu.VMEM)
 SMEM = pl.BlockSpec(memory_space=pltpu.SMEM)
@@ -65,18 +66,15 @@
     token[...] = jnp.zeros_like(token)
 
 
-def turned(value):
-    return value.astype(F32).T.astype(BF16)
+def turn_kernel(vectors, out):
+    out[...] = vectors[...].astype(F32).T.astype(BF16)
 
 
 def pieces_kernel(stage, own, other, *refs):
     out = refs[-1]
     z = lax.axis_index("z")
     half = Z // 2
-    if stage == 0:
-        mine, theirs = turned(own[...]), turned(other[...])
-    else:
-        mine, theirs = own[:SLICE], other[:SLICE]
+    mine, theirs = own[:SLICE], other[:SLICE]
     for target in range(Z):
         use_other = jnp.where(z < half, z <= target - half - 1, z >= target + half)
 
@@ -115,10 +113,10 @@
     return lax.all_to_all(pieces, "z", 0, 0)
 
 
-def multiply(core, steps, tiles, rhs, out, sums):
+def multiply(core, tiles, rhs, out, sums):
     y = lax.axis_index("y")
-    for i, step in enumerate(steps):
-        start = pl.multiple_of((lax.rem(y + step, Y) * CORE + core) * SLICE, SLICE)
+    for i in range(Y):
+        start = pl.multiple_of((lax.rem(y + i, Y) * CORE + core) * SLICE, SLICE)
         total = jnp.zeros((SLICE, LANES), F32)
         for t in range(tiles.shape[0]):
             total = total + jnp.dot(
@@ -132,12 +130,14 @@
 def send_kernel(stage, tile_row, tile_col, tile_count, tiles, slots, out, rhs, *sums_ref):
     lane = lax.broadcasted_iota(jnp.int32, (SLICE, LANES), 1)
     for t in range(tiles.shape[0]):
-        slot = lax.rem(lax.div(tile_col[t], 2), Z)
-        first = tile_row[t] * HALF
+        row, col = tile_row[t], tile_col[t]
+        parity, slot = col & 1, lax.shift_right_logical(col, 1) & (Z - 1)
+        live = t < tile_count[0]
+        first = row * HALF
         vectors = slots[slot, :SLICE].astype(F32)
         other_half = pltpu.roll(vectors, HALF, axis=1)
-        vectors = jnp.where(lax.rem(tile_col[t], 2) == tile_row[t], vectors, other_half)
-        keep = (lane >= first) & (lane < first + HALF) & (t < tile_count[0])
+        vectors = jnp.where(parity == row, vectors, other_half)
+        keep = (lane >= first) & (lane < first + HALF) & live
         rhs[t] = jnp.where(keep, vectors, 0.0).astype(BF16)
     sums = None
     if stage:
@@ -153,51 +153,43 @@
         sums_ref[0][...] = sums
     if stage == 2:
         sums_ref[0][...] = pad_rows(joined(extra[0]) + joined(extra[Z // 2]), SUMS)
-    multiply(1 - lax.axis_index("core"), range(Y), tiles, rhs, out, sums)
-
-
-def keep_kernel(stage, steps, tiles, rhs, *refs):
+    multiply(1 - lax.axis_index("core"), tiles, rhs, out, sums)
+
+
+def keep_kernel(stage, tiles, rhs, *refs):
     sums = refs[0][...] if stage == 1 else None
-    multiply(lax.axis_index("core"), steps, tiles, rhs, refs[-1], sums)
+    multiply(lax.axis_index("core"), tiles, rhs, refs[-1], sums)
 
 
 def apply_graph(stage, plan, tiles, slots):
     count = tiles.shape[0]
     rows = SLICE + (SUMS if stage == 1 else 0)
-
-    def work(slices):
-        return dict(
-            limit=20,
-            flops=2 * count * slices * SLICE * SLICE * LANES,
-            moved=count * slices * SLICE * SLICE * 2,
-        )
-
-    outs = (((Y, rows, LANES), F32), ((count, SLICE, LANES), BF16))
+    slices = ((Y, rows, LANES), F32)
+    outs = (slices, ((count, SLICE, LANES), BF16))
     if stage:
         outs += (((SUMS, LANES), F32),)
+    size = dict(
+        limit=20,
+        flops=2 * count * Y * SLICE * SLICE * LANES,
+        moved=count * Y * SLICE * SLICE * 2,
+    )
     sent, rhs, *sums = call(
-        functools.partial(send_kernel, stage), outs, [SMEM] * 3 + [VMEM] * 2, *plan, tiles, slots, **work(Y)
-    )
-    received = lax.ppermute(sent, "core", [(0, 1), (1, 0)])
-    passed = sums if stage == 1 else []
-
-    def keep(steps):
-        return call(
-            functools.partial(keep_kernel, stage, steps),
-            ((len(steps), rows, LANES), F32),
-            [VMEM] * (2 + len(passed)),
-            tiles,
-            rhs,
-            *passed,
-            **work(len(steps)),
-        )
-
-    away = keep(range(1, Y))
+        functools.partial(send_kernel, stage),
+        outs,
+        [VMEM] * 5,
+        *plan,
+        tiles,
+        slots,
+        **size,
+    )
+    received = lax.ppermute(sent, "core", CORE_SWAP)
+    given = [tiles, rhs] + (sums if stage == 1 else [])
+    kept = call(functools.partial(keep_kernel, stage), slices, [VMEM] * len(given), *given, **size)
     parts = []
-    for step in (2, 1, 3):
-        part = away[step - 1] + received[step]
+    for step in (3, 1, 2):
+        part = kept[step] + received[step]
         parts.append(lax.ppermute(part, "y", [(y, (y + step) % Y) for y in range(Y)]))
-    return (keep((0,)), received, *parts), sums
+    return (kept, received, *parts), sums
 
 
 def added(refs):
@@ -215,8 +207,7 @@
     payload[:SLICE] = value.astype(BF16)
     wide = vectors[...].astype(F32)
     wide = jnp.sum(wide * wide, axis=0, keepdims=True)
-    sums = jnp.sum(value * value, axis=0, keepdims=True)
-    sums = jnp.concatenate([sums, wide[:, :LANES] + wide[:, LANES:]], axis=0)
+    sums = jnp.concatenate([jnp.sum(value * value, axis=0, keepdims=True), wide], axis=0)
     payload[SLICE:] = pad_rows(split(sums), EXT).astype(BF16)
 
 
@@ -240,7 +231,15 @@
         value, value, (((0,), (0,)), ((), ())), precision=HIGHEST, preferred_element_type=F32
     )
     gram64 = full[:HALF, :HALF] + full[HALF:, HALF:]
-    gram[...] = jnp.concatenate([gram64[: HALF // 2], gram64[HALF // 2 :]], axis=1)
+    half = HALF // 2
+    blocks = (gram64[:half, :half], gram64[half:, :half], gram64[half:, half:])
+    gram[...] = jnp.concatenate(
+        [
+            jnp.concatenate([block[i : i + 8] for i in range(0, half, 8)], axis=1)
+            for block in blocks
+        ],
+        axis=0,
+    )
 
 
 def inverse_factor(work):
@@ -284,7 +283,14 @@
     packed = grams[0]
     for i in range(1, grams.shape[0]):
         packed = packed + grams[i]
-    square = jnp.concatenate([packed[:, :HALF], packed[:, HALF:]], axis=0)
+    half = HALF // 2
+    top, corner, bottom = (
+        jnp.concatenate([packed[b : b + 8, i : i + half] for i in range(0, LANES, half)], axis=0)
+        for b in (0, 8, 16)
+    )
+    square = jnp.concatenate(
+        [jnp.concatenate([top, corner.T], axis=1), jnp.concatenate([corner, bottom], axis=1)], axis=0
+    )
     row = lax.broadcasted_iota(jnp.int32, (HALF, LANES), 0)
     lane = lax.broadcasted_iota(jnp.int32, (HALF, LANES), 1)
     unit = jnp.where(lane - HALF == row, 1.0, 0.0)
@@ -304,16 +310,17 @@
     blocks, rows, vectors = block_vectors.shape
     count = tiles.shape[0]
     plan = (tile_row, tile_col, tile_count)
-    vectors_turned = block_vectors.transpose(0, 2, 1).reshape(blocks * vectors, rows)
     slice_shape, payload_shape = (rows, LANES), (rows + EXT, LANES)
+    packed = block_vectors.transpose(0, 2, 1).reshape(blocks * vectors, rows)
+    packed = call(turn_kernel, (slice_shape, BF16), [VMEM], packed)
     token = call(place_kernel, ((SUMS, LANES), F32), [VMEM], tiles, limit=20, moved=2 * tiles.size)
-    parts, _ = apply_graph(0, plan, tiles, window(0, vectors_turned, token))
+    parts, _ = apply_graph(0, plan, tiles, window(0, packed, *plan, token))
     first, payload = call(
         first_kernel,
         ((slice_shape, F32), (payload_shape, BF16)),
         [VMEM] * (len(parts) + 1),
         *parts,
-        vectors_turned,
+        packed,
     )
     parts, _ = apply_graph(1, plan, tiles, window(1, payload))
     payload, gathered = call(
@@ -325,14 +332,14 @@
     parts, sums = apply_graph(2, plan, tiles, window(2, payload, gathered))
     filtered, gram = call(
         gram_kernel,
-        ((slice_shape, F32), ((vectors // 2, LANES), F32)),
+        ((slice_shape, F32), ((24, LANES), F32)),
         [VMEM] * (len(parts) + 2),
         *parts,
         first,
         *sums,
     )
 
-    gram = gram + lax.ppermute(gram, "core", [(0, 1), (1, 0)])
+    gram = gram + lax.ppermute(gram, "core", CORE_SWAP)
     grams = lax.all_to_all(jnp.broadcast_to(gram[None], (X * Y,) + gram.shape), ("x", "y"), 0, 0)
     gram = jnp.sum(grams, axis=0)
     grams = lax.all_to_all(jnp.broadcast_to(gram[None], (Z,) + gram.shape), "z", 0, 0)
@@ -340,7 +347,7 @@
     out = call(
         functools.partial(finish_kernel, math.sqrt(total_rows)),
         ((blocks, vectors, rows), F32),
-        [VMEM, VMEM],
+        [VMEM] * 2,
         grams,
         filtered,
     )

time: 161 us -> 155 us (0.963)
  blocking collectives: 65.6 us -> 88.7 us
  starting transfers between devices: 32.8 us -> 19.7 us
  waiting for transfers between devices: 35.3 us -> 25.3 us
  local copies, waits for them, and re-layouts: 8.83 us -> 4.87 us
  Pallas kernels: 17 us -> 14.9 us
    all_to_all x2 -> x3, blocking collectives: 38.8 us -> 64.3 us  [window(): return lax.all_to_all(pieces, 'z', 0, 0)]
    all_to_all x1 -> x0, waiting for transfers between devices: 16.6 us -> none  [window(): return lax.all_to_all(pieces, 'z', 0, 0)]
    ppermute x9, waiting for transfers between devices: 10.9 us -> 18.5 us  [apply_graph(): lax.ppermute(part, 'y', [(y, (y + step) % Y) for y in range(Y)])]
    all_to_all x1 -> x0, starting transfers between devices: 7.2 us -> none  [window(): return lax.all_to_all(pieces, 'z', 0, 0)]
    ppermute x9, starting transfers between devices: 17.9 us -> 11.7 us  [apply_graph(): lax.ppermute(part, 'y', [(y, (y + step) % Y) for y in range(Y)])]
    unnamed x10 -> x8, local copies, waits for them, and re-layouts: 8.8 us -> 4.84 us
    pallas_call x17 -> x15, Pallas kernels: 17 us -> 14.9 us  [call(): pl.pallas_call(kernel, out_shape=tuple((jax.ShapeDtypeStruct(*s) for s in...]
    all_to_all x1, blocking collectives: 15.4 us -> 13.3 us  [on_device(): lax.all_to_all(jnp.broadcast_to(gram[None], (X * Y,) + gram.shape), ('x',...]
  transfers between devices with their start and end apart: 17 -> 16, of which waited for: 14 -> 14; matrix products, arithmetic and copies ran while one was open for 0% -> 0% of each run, Pallas kernels for 3% -> 3%
where the time goes in v4:
time: 155 us; the launch traced here: 154 us
  blocking collectives  88.7 us (57%)
  waiting for transfers between devices  25.3 us (16%)
  starting transfers between devices  19.7 us (13%)
  Pallas kernels  14.9 us (10%)
  local copies, waits for them, and re-layouts  4.87 us (3%)
    all_to_all x3, blocking collectives, window(): return lax.all_to_all(pieces, 'z', 0, 0)  64.3 us
    ppermute x9, waiting for transfers between devices, apply_graph(): lax.ppermute(part, 'y', [(y, (y + step) % Y) for y in range(Y)])  18.5 us
    pallas_call x15, Pallas kernels, call(): pl.pallas_call(kernel, out_shape=tuple((jax.ShapeDtypeStruct(*s) for s in...  14.9 us
    all_to_all x1, blocking collectives, on_device(): lax.all_to_all(jnp.broadcast_to(gram[None], (X * Y,) + gram.shape), ('x',...  13.3 us
    ppermute x9, starting transfers between devices, apply_graph(): lax.ppermute(part, 'y', [(y, (y + step) % Y) for y in range(Y)])  11.7 us
    all_to_all x1, blocking collectives, on_device(): lax.all_to_all(jnp.broadcast_to(gram[None], (Z,) + gram.shape), 'z', 0, 0)  11.1 us
    ppermute x3, starting transfers between devices, window(): other = lax.ppermute(own, ALL, x_neighbour_pairs())  7.49 us
    unnamed x8, local copies, waits for them, and re-layouts  4.84 us
  transfers between devices with their start and end apart: 16, of which 14 were waited for; matrix products, arithmetic and copies ran while one was open for 0% of the time, Pallas kernels for 3%

profile of v4, /device:TPU:8, one launch (start us, length us, event | category | flops | bytes accessed | tf_op | source)
XLA Modules:
  0.0 154.4 jit_solution(16348101853309099647)
XLA Ops:
  0.0 0.9 copy-done.1
  1.0 2.8 %collective-permute-start = (bf16[256,128]{1,0:T(8,128)(2,1)S(1)}, bf16[256,128]{1,0:T(8,128)(2,1)S(1)}, u32[]{:S(2)}, u32[]{:S(2)}) collective-permute-start(bf16[256,128]{1,0:T(8,128)(2,1)S(1)} %shard_map.55.own.refs_5_), channel_id=1, source_target_pairs={{0,192},{1,193},{2,194},{3,195},{4,196},{5,197},{6,198},{7,199},{8... | collective-permute-start | bytes 196616 | tf_op jit(solution)/shard_map/ppermute | solution.py:103
  4.5 4.0 %copy-done = bf16[10,2048,256]{2,1,0:T(8,128)(2,1)S(1)} copy-done((bf16[10,2048,256]{2,1,0:T(8,128)(2,1)S(1)}, bf16[10,2048,256]{2,1,0:T(8,128)(2,1)}, u32[]{:S(2)}) %copy-start) | copy-done | bytes 10485784
  8.6 24.2 %all_to_all.25.slots = bf16[8,256,128]{2,1,0:T(8,128)(2,1)S(1)} all-to-all(bf16[8,256,128]{2,1,0:T(8,128)(2,1)S(1)} %shard_map.57), channel_id=1, replica_groups=mesh['x'=4,'z'=8,'y'=4,'core'=2] {'z'}, dimensions={0} | all-to-all | bytes 1048576 | tf_op jit(solution)/shard_map/all_to_all | solution.py:113
  32.8 1.9 %shard_map.58 = (f32[4,256,128]{2,1,0:T(8,128)S(1)}, bf16[10,256,128]{2,1,0:T(8,128)(2,1)S(1)}) custom-call(s32[10]{0:T(128)S(1)} %copy-done.2, s32[10]{0:T(128)S(1)} %copy-done.3, s32[1]{0:T(128)S(6)} %copy.6.refs_2_.tile_count, bf16[10,2048,256]{2,1,0:T(8,128)(2,1)S(1)} %copy-done, bf16[8,256,128]{2,1,0:T(8,128)(2,1)S(1)} %all_to_all.25.slots), custom_call_target="tpu_custom_call" | custom-call | flops 671088640 | bytes 5242880 | tf_op jit(solution)/shard_map/pallas_call | solution.py:28
  34.8 1.5 shard_map.59.refs_0_
  36.7 2.4 %collective-permute-start.4 = (f32[256,128]{1,0:T(8,128)S(1)}, f32[256,128]{1,0:T(8,128)S(1)}, u32[]{:S(2)}, u32[]{:S(2)}) collective-permute-start(f32[256,128]{1,0:T(8,128)S(1)} %get-tuple-element.39), channel_id=1, source_target_pairs={{0,4},{2,6},{4,0},{6,2},{1,5},{3,7},{5,1},{7,3},{8,12},{10,14},{12... | collective-permute-start | bytes 393224 | tf_op jit(solution)/shard_map/ppermute | solution.py:191
  39.1 2.0 %collective-permute-start.2 = (f32[256,128]{1,0:T(8,128)S(1)}, f32[256,128]{1,0:T(8,128)S(1)}, u32[]{:S(2)}, u32[]{:S(2)}) collective-permute-start(f32[256,128]{1,0:T(8,128)S(1)} %get-tuple-element.41), channel_id=1, source_target_pairs={{0,6},{2,0},{4,2},{6,4},{1,7},{3,1},{5,3},{7,5},{8,14},{10,8},{12,... | collective-permute-start | bytes 393224 | tf_op jit(solution)/shard_map/ppermute | solution.py:191
  41.1 3.5 %collective-permute-done.4.refs_4_ = f32[256,128]{1,0:T(8,128)S(1)} collective-permute-done((f32[256,128]{1,0:T(8,128)S(1)}, f32[256,128]{1,0:T(8,128)S(1)}, u32[]{:S(2)}, u32[]{:S(2)}) %collective-permute-start.4) | collective-permute-done | bytes 131104 | tf_op jit(solution)/shard_map/ppermute | solution.py:191
  44.7 2.2 %collective-permute-done.3.refs_3_ = f32[256,128]{1,0:T(8,128)S(1)} collective-permute-done((f32[256,128]{1,0:T(8,128)S(1)}, f32[256,128]{1,0:T(8,128)S(1)}, u32[]{:S(2)}, u32[]{:S(2)}) %collective-permute-start.3) | collective-permute-done | bytes 131104 | tf_op jit(solution)/shard_map/ppermute | solution.py:191
  46.9 1.8 %collective-permute-start.5 = (bf16[272,128]{1,0:T(8,128)(2,1)S(1)}, bf16[272,128]{1,0:T(8,128)(2,1)S(1)}, u32[]{:S(2)}, u32[]{:S(2)}) collective-permute-start(bf16[272,128]{1,0:T(8,128)(2,1)S(1)} %get-tuple-element.21.own), channel_id=1, source_target_pairs={{0,192},{1,193},{2,194},{3,195},{4,196},{5,197},{6,198},{7,199},{8... | collective-permute-start | bytes 208904 | tf_op jit(solution)/shard_map/ppermute | solution.py:103
  48.7 2.6 %collective-permute-done.5.other = bf16[272,128]{1,0:T(8,128)(2,1)S(1)} collective-permute-done((bf16[272,128]{1,0:T(8,128)(2,1)S(1)}, bf16[272,128]{1,0:T(8,128)(2,1)S(1)}, u32[]{:S(2)}, u32[]{:S(2)}) %collective-permute-start.5) | collective-permute-done | bytes 69664 | tf_op jit(solution)/shard_map/ppermute | solution.py:103
  51.4 19.9 %all_to_all.26.slots = bf16[8,272,128]{2,1,0:T(8,128)(2,1)S(1)} all-to-all(bf16[8,272,128]{2,1,0:T(8,128)(2,1)S(1)} %shard_map.61), channel_id=1, replica_groups=mesh['x'=4,'z'=8,'y'=4,'core'=2] {'z'}, dimensions={0} | all-to-all | bytes 1114112 | tf_op jit(solution)/shard_map/all_to_all | solution.py:113
  71.4 1.9 %shard_map.62 = (f32[4,264,128]{2,1,0:T(8,128)S(1)}, bf16[10,256,128]{2,1,0:T(8,128)(2,1)S(1)}, f32[8,128]{1,0:T(8,128)S(1)}) custom-call(s32[10]{0:T(128)S(1)} %copy-done.2, s32[10]{0:T(128)S(1)} %copy-done.3, s32[1]{0:T(128)S(6)} %copy.6.refs_2_.tile_count, bf16[10,2048,256]{2,1,0:T(8,128)(2,1)S(1)} %copy-done, bf16[8,272,128]{2,1,0:T(8,128)(2,1)S(1)} %all_to_all.26.slots), custom_call_target="tpu_custom_call" | custom-call | flops 671088640 | bytes 5242880 | tf_op jit(solution)/shard_map/pallas_call | solution.py:28
  73.5 1.5 shard_map.63.refs_0_
  75.5 1.8 %collective-permute-start.9 = (f32[264,128]{1,0:T(8,128)S(1)}, f32[264,128]{1,0:T(8,128)S(1)}, u32[]{:S(2)}, u32[]{:S(2)}) collective-permute-start(f32[264,128]{1,0:T(8,128)S(1)} %get-tuple-element.33), channel_id=1, source_target_pairs={{0,4},{2,6},{4,0},{6,2},{1,5},{3,7},{5,1},{7,3},{8,12},{10,14},{12... | collective-permute-start | bytes 405512 | tf_op jit(solution)/shard_map/ppermute | solution.py:191
  77.3 2.0 %collective-permute-start.7 = (f32[264,128]{1,0:T(8,128)S(1)}, f32[264,128]{1,0:T(8,128)S(1)}, u32[]{:S(2)}, u32[]{:S(2)}) collective-permute-start(f32[264,128]{1,0:T(8,128)S(1)} %get-tuple-element.35), channel_id=1, source_target_pairs={{0,6},{2,0},{4,2},{6,4},{1,7},{3,1},{5,3},{7,5},{8,14},{10,8},{12,... | collective-permute-start | bytes 405512 | tf_op jit(solution)/shard_map/ppermute | solution.py:191
  79.4 4.2 %collective-permute-done.9.refs_4_ = f32[264,128]{1,0:T(8,128)S(1)} collective-permute-done((f32[264,128]{1,0:T(8,128)S(1)}, f32[264,128]{1,0:T(8,128)S(1)}, u32[]{:S(2)}, u32[]{:S(2)}) %collective-permute-start.9) | collective-permute-done | bytes 135200 | tf_op jit(solution)/shard_map/ppermute | solution.py:191
  84.3 1.3 collective-permute-done.7.refs_2_
  85.7 2.8 %collective-permute-start.10 = (bf16[272,128]{1,0:T(8,128)(2,1)S(1)}, bf16[272,128]{1,0:T(8,128)(2,1)S(1)}, u32[]{:S(2)}, u32[]{:S(2)}) collective-permute-start(bf16[272,128]{1,0:T(8,128)(2,1)S(1)} %get-tuple-element.25.own), channel_id=1, source_target_pairs={{0,192},{1,193},{2,194},{3,195},{4,196},{5,197},{6,198},{7,199},{8... | collective-permute-start | bytes 208904 | tf_op jit(solution)/shard_map/ppermute | solution.py:103
  88.5 1.9 %collective-permute-done.10.other = bf16[272,128]{1,0:T(8,128)(2,1)S(1)} collective-permute-done((bf16[272,128]{1,0:T(8,128)(2,1)S(1)}, bf16[272,128]{1,0:T(8,128)(2,1)S(1)}, u32[]{:S(2)}, u32[]{:S(2)}) %collective-permute-start.10) | collective-permute-done | bytes 69664 | tf_op jit(solution)/shard_map/ppermute | solution.py:103
  90.6 20.2 %all_to_all.27.slots = bf16[8,272,128]{2,1,0:T(8,128)(2,1)S(1)} all-to-all(bf16[8,272,128]{2,1,0:T(8,128)(2,1)S(1)} %shard_map.65), channel_id=1, replica_groups=mesh['x'=4,'z'=8,'y'=4,'core'=2] {'z'}, dimensions={0} | all-to-all | bytes 1114112 | tf_op jit(solution)/shard_map/all_to_all | solution.py:113
  110.8 1.9 %shard_map.66 = (f32[4,256,128]{2,1,0:T(8,128)S(1)}, bf16[10,256,128]{2,1,0:T(8,128)(2,1)S(1)}, f32[8,128]{1,0:T(8,128)S(1)}) custom-call(s32[10]{0:T(128)S(1)} %copy-done.2, s32[10]{0:T(128)S(1)} %copy-done.3, s32[1]{0:T(128)S(6)} %copy.6.refs_2_.tile_count, bf16[10,2048,256]{2,1,0:T(8,128)(2,1)S(1)} %copy-done, bf16[8,272,128]{2,1,0:T(8,128)(2,1)S(1)} %all_to_all.27.slots), custom_call_target="tpu_custom_call" | custom-call | flops 671088640 | bytes 5242880 | tf_op jit(solution)/shard_map/pallas_call | solution.py:28
  112.8 1.5 shard_map.67.refs_0_
  114.7 1.4 collective-permute-start.14
  116.4 1.7 %collective-permute-start.12 = (f32[256,128]{1,0:T(8,128)S(1)}, f32[256,128]{1,0:T(8,128)S(1)}, u32[]{:S(2)}, u32[]{:S(2)}) collective-permute-start(f32[256,128]{1,0:T(8,128)S(1)} %get-tuple-element.38), channel_id=1, source_target_pairs={{0,6},{2,0},{4,2},{6,4},{1,7},{3,1},{5,3},{7,5},{8,14},{10,8},{12,... | collective-permute-start | bytes 393224 | tf_op jit(solution)/shard_map/ppermute | solution.py:191
  118.1 4.5 %collective-permute-done.14.refs_4_ = f32[256,128]{1,0:T(8,128)S(1)} collective-permute-done((f32[256,128]{1,0:T(8,128)S(1)}, f32[256,128]{1,0:T(8,128)S(1)}, u32[]{:S(2)}, u32[]{:S(2)}) %collective-permute-start.14) | collective-permute-done | bytes 131104 | tf_op jit(solution)/shard_map/ppermute | solution.py:191
  123.4 1.3 collective-permute-done.12.refs_2_
  125.3 1.2 collective-permute-done.15
  126.5 13.3 %all_to_all.28 = f32[16,24,128]{2,1,0:T(8,128)S(1)} all-to-all(f32[16,24,128]{2,1,0:T(8,128)S(1)} %broadcast_in_dim.4), channel_id=1, replica_groups=mesh['x'=4,'z'=8,'y'=4,'core'=2] {'x','y'}, dimensions={0} | all-to-all | bytes 393216 | tf_op jit(solution)/shard_map/all_to_all | solution.py:343
  139.9 11.1 %all_to_all.29.grams = f32[8,24,128]{2,1,0:T(8,128)S(1)} all-to-all(f32[8,24,128]{2,1,0:T(8,128)S(1)} %broadcast_in_dim.5), channel_id=1, replica_groups=mesh['x'=4,'z'=8,'y'=4,'core'=2] {'z'}, dimensions={0} | all-to-all | bytes 196608 | tf_op jit(solution)/shard_map/all_to_all | solution.py:345
  151.0 3.4 %shard_map.69 = f32[2,64,256]{2,1,0:T(8,128)} custom-call(f32[8,24,128]{2,1,0:T(8,128)S(1)} %all_to_all.29.grams, f32[256,128]{1,0:T(8,128)S(1)} %get-tuple-element.32.filtered), custom_call_target="tpu_custom_call" | custom-call | tf_op jit(solution)/shard_map/pallas_call | solution.py:28
  (35 shorter events, 4.9 us)
Async XLA Ops:
  0.0 8.5 %copy-start.3 = (s32[10]{0:T(128)S(1)}, s32[10]{0:T(128)}, u32[]{:S(2)}) copy-start(s32[10]{0:T(128)} %tile_col.5) | copy-start | bytes 124
  0.0 8.5 %copy-start.2 = (s32[10]{0:T(128)S(1)}, s32[10]{0:T(128)}, u32[]{:S(2)}) copy-start(s32[10]{0:T(128)} %tile_row.5) | copy-start | bytes 124
  0.0 0.9 copy-start.1
  1.0 7.5 %collective-permute-start = (bf16[256,128]{1,0:T(8,128)(2,1)S(1)}, bf16[256,128]{1,0:T(8,128)(2,1)S(1)}, u32[]{:S(2)}, u32[]{:S(2)}) collective-permute-start(bf16[256,128]{1,0:T(8,128)(2,1)S(1)} %shard_map.55.own.refs_5_), channel_id=1, source_target_pairs={{0,192},{1,193},{2,194},{3,195},{4,196},{5,197},{6,198},{7,199},{8... | collective-permute-start | bytes 196616 | tf_op jit(solution)/shard_map/ppermute | solution.py:103
  4.5 4.0 %copy-start = (bf16[10,2048,256]{2,1,0:T(8,128)(2,1)S(1)}, bf16[10,2048,256]{2,1,0:T(8,128)(2,1)}, u32[]{:S(2)}) copy-start(bf16[10,2048,256]{2,1,0:T(8,128)(2,1)} %tiles.13) | copy-start | bytes 31457284
  34.7 2.0 %collective-permute-start.1 = (f32[4,256,128]{2,1,0:T(8,128)S(1)}, f32[4,256,128]{2,1,0:T(8,128)S(1)}, u32[]{:S(2)}, u32[]{:S(2)}) collective-permute-start(f32[4,256,128]{2,1,0:T(8,128)S(1)} %get-tuple-element.20), channel_id=1, source_target_pairs={{0,1},{1,0},{2,3},{3,2},{4,5},{5,4},{6,7},{7,6},{8,9},{9,8},{10,11... | collective-permute-start | bytes 1572872 | tf_op jit(solution)/shard_map/ppermute | solution.py:185
  36.7 7.9 %collective-permute-start.4 = (f32[256,128]{1,0:T(8,128)S(1)}, f32[256,128]{1,0:T(8,128)S(1)}, u32[]{:S(2)}, u32[]{:S(2)}) collective-permute-start(f32[256,128]{1,0:T(8,128)S(1)} %get-tuple-element.39), channel_id=1, source_target_pairs={{0,4},{2,6},{4,0},{6,2},{1,5},{3,7},{5,1},{7,3},{8,12},{10,14},{12... | collective-permute-start | bytes 393224 | tf_op jit(solution)/shard_map/ppermute | solution.py:191
  39.1 7.7 %collective-permute-start.3 = (f32[256,128]{1,0:T(8,128)S(1)}, f32[256,128]{1,0:T(8,128)S(1)}, u32[]{:S(2)}, u32[]{:S(2)}) collective-permute-start(f32[256,128]{1,0:T(8,128)S(1)} %get-tuple-element.40), channel_id=1, source_target_pairs={{0,2},{2,4},{4,6},{6,0},{1,3},{3,5},{5,7},{7,1},{8,10},{10,12},{12... | collective-permute-start | bytes 393224 | tf_op jit(solution)/shard_map/ppermute | solution.py:191
  39.1 7.7 %collective-permute-start.2 = (f32[256,128]{1,0:T(8,128)S(1)}, f32[256,128]{1,0:T(8,128)S(1)}, u32[]{:S(2)}, u32[]{:S(2)}) collective-permute-start(f32[256,128]{1,0:T(8,128)S(1)} %get-tuple-element.41), channel_id=1, source_target_pairs={{0,6},{2,0},{4,2},{6,4},{1,7},{3,1},{5,3},{7,5},{8,14},{10,8},{12,... | collective-permute-start | bytes 393224 | tf_op jit(solution)/shard_map/ppermute | solution.py:191
  46.9 4.4 %collective-permute-start.5 = (bf16[272,128]{1,0:T(8,128)(2,1)S(1)}, bf16[272,128]{1,0:T(8,128)(2,1)S(1)}, u32[]{:S(2)}, u32[]{:S(2)}) collective-permute-start(bf16[272,128]{1,0:T(8,128)(2,1)S(1)} %get-tuple-element.21.own), channel_id=1, source_target_pairs={{0,192},{1,193},{2,194},{3,195},{4,196},{5,197},{6,198},{7,199},{8... | collective-permute-start | bytes 208904 | tf_op jit(solution)/shard_map/ppermute | solution.py:103
  73.3 2.2 %collective-permute-start.6 = (f32[4,264,128]{2,1,0:T(8,128)S(1)}, f32[4,264,128]{2,1,0:T(8,128)S(1)}, u32[]{:S(2)}, u32[]{:S(2)}) collective-permute-start(f32[4,264,128]{2,1,0:T(8,128)S(1)} %get-tuple-element.24), channel_id=1, source_target_pairs={{0,1},{1,0},{2,3},{3,2},{4,5},{5,4},{6,7},{7,6},{8,9},{9,8},{10,11... | collective-permute-start | bytes 1622024 | tf_op jit(solution)/shard_map/ppermute | solution.py:185
  75.5 8.1 %collective-permute-start.9 = (f32[264,128]{1,0:T(8,128)S(1)}, f32[264,128]{1,0:T(8,128)S(1)}, u32[]{:S(2)}, u32[]{:S(2)}) collective-permute-start(f32[264,128]{1,0:T(8,128)S(1)} %get-tuple-element.33), channel_id=1, source_target_pairs={{0,4},{2,6},{4,0},{6,2},{1,5},{3,7},{5,1},{7,3},{8,12},{10,14},{12... | collective-permute-start | bytes 405512 | tf_op jit(solution)/shard_map/ppermute | solution.py:191
  77.3 7.0 %collective-permute-start.8 = (f32[264,128]{1,0:T(8,128)S(1)}, f32[264,128]{1,0:T(8,128)S(1)}, u32[]{:S(2)}, u32[]{:S(2)}) collective-permute-start(f32[264,128]{1,0:T(8,128)S(1)} %get-tuple-element.34), channel_id=1, source_target_pairs={{0,2},{2,4},{4,6},{6,0},{1,3},{3,5},{5,7},{7,1},{8,10},{10,12},{12... | collective-permute-start | bytes 405512 | tf_op jit(solution)/shard_map/ppermute | solution.py:191
  77.3 8.3 %collective-permute-start.7 = (f32[264,128]{1,0:T(8,128)S(1)}, f32[264,128]{1,0:T(8,128)S(1)}, u32[]{:S(2)}, u32[]{:S(2)}) collective-permute-start(f32[264,128]{1,0:T(8,128)S(1)} %get-tuple-element.35), channel_id=1, source_target_pairs={{0,6},{2,0},{4,2},{6,4},{1,7},{3,1},{5,3},{7,5},{8,14},{10,8},{12,... | collective-permute-start | bytes 405512 | tf_op jit(solution)/shard_map/ppermute | solution.py:191
  85.7 4.8 %collective-permute-start.10 = (bf16[272,128]{1,0:T(8,128)(2,1)S(1)}, bf16[272,128]{1,0:T(8,128)(2,1)S(1)}, u32[]{:S(2)}, u32[]{:S(2)}) collective-permute-start(bf16[272,128]{1,0:T(8,128)(2,1)S(1)} %get-tuple-element.25.own), channel_id=1, source_target_pairs={{0,192},{1,193},{2,194},{3,195},{4,196},{5,197},{6,198},{7,199},{8... | collective-permute-start | bytes 208904 | tf_op jit(solution)/shard_map/ppermute | solution.py:103
  112.7 2.0 %collective-permute-start.11 = (f32[4,256,128]{2,1,0:T(8,128)S(1)}, f32[4,256,128]{2,1,0:T(8,128)S(1)}, u32[]{:S(2)}, u32[]{:S(2)}) collective-permute-start(f32[4,256,128]{2,1,0:T(8,128)S(1)} %get-tuple-element.28), channel_id=1, source_target_pairs={{0,1},{1,0},{2,3},{3,2},{4,5},{5,4},{6,7},{7,6},{8,9},{9,8},{10,11... | collective-permute-start | bytes 1572872 | tf_op jit(solution)/shard_map/ppermute | solution.py:185
  114.7 8.0 %collective-permute-start.14 = (f32[256,128]{1,0:T(8,128)S(1)}, f32[256,128]{1,0:T(8,128)S(1)}, u32[]{:S(2)}, u32[]{:S(2)}) collective-permute-start(f32[256,128]{1,0:T(8,128)S(1)} %get-tuple-element.36), channel_id=1, source_target_pairs={{0,4},{2,6},{4,0},{6,2},{1,5},{3,7},{5,1},{7,3},{8,12},{10,14},{12... | collective-permute-start | bytes 393224 | tf_op jit(solution)/shard_map/ppermute | solution.py:191
  116.1 7.3 %collective-permute-start.13 = (f32[256,128]{1,0:T(8,128)S(1)}, f32[256,128]{1,0:T(8,128)S(1)}, u32[]{:S(2)}, u32[]{:S(2)}) collective-permute-start(f32[256,128]{1,0:T(8,128)S(1)} %get-tuple-element.37), channel_id=1, source_target_pairs={{0,2},{2,4},{4,6},{6,0},{1,3},{3,5},{5,7},{7,1},{8,10},{10,12},{12... | collective-permute-start | bytes 393224 | tf_op jit(solution)/shard_map/ppermute | solution.py:191
  116.4 8.2 %collective-permute-start.12 = (f32[256,128]{1,0:T(8,128)S(1)}, f32[256,128]{1,0:T(8,128)S(1)}, u32[]{:S(2)}, u32[]{:S(2)}) collective-permute-start(f32[256,128]{1,0:T(8,128)S(1)} %get-tuple-element.38), channel_id=1, source_target_pairs={{0,6},{2,0},{4,2},{6,4},{1,7},{3,1},{5,3},{7,5},{8,14},{10,8},{12,... | collective-permute-start | bytes 393224 | tf_op jit(solution)/shard_map/ppermute | solution.py:191
  125.2 1.3 collective-permute-start.15

commit v5 on v4

--- a/solution.py
+++ b/solution.py
@@ -188,6 +188,8 @@
     parts = []
     for step in (3, 1, 2):
         part = kept[step] + received[step]
+        if stage == 2:
+            part = part.astype(BF16)
         parts.append(lax.ppermute(part, "y", [(y, (y + step) % Y) for y in range(Y)]))
     return (kept, received, *parts), sums
 
@@ -196,7 +198,7 @@
     own, received, *parts = refs
     value = own[0] + received[0]
     for part in parts:
-        value = value + part[...]
+        value = value + part[...].astype(F32)
     return value
 
 

time: 155 us -> 153 us (0.987)
  waiting for transfers between devices: 25.3 us -> 22.5 us
    ppermute x9, waiting for transfers between devices: 18.5 us -> 15.7 us  [apply_graph(): lax.ppermute(part, 'y', [(y, (y + step) % Y) for y in range(Y)])]
  transfers between devices with their start and end apart: 16 -> 16, of which waited for: 14 -> 13; matrix products, arithmetic and copies ran while one was open for 0% -> 0% of each run, Pallas kernels for 3% -> 3%
where the time goes in v5:
time: 153 us
  blocking collectives  89.9 us (59%)
  waiting for transfers between devices  22.5 us (15%)
  starting transfers between devices  19.7 us (13%)
  Pallas kernels  14.9 us (10%)
  local copies, waits for them, and re-layouts  4.87 us (3%)
    all_to_all x3, blocking collectives, window(): return lax.all_to_all(pieces, 'z', 0, 0)  64.3 us
    ppermute x9, waiting for transfers between devices, apply_graph(): lax.ppermute(part, 'y', [(y, (y + step) % Y) for y in range(Y)])  15.7 us
    pallas_call x15, Pallas kernels, call(): pl.pallas_call(kernel, out_shape=tuple((jax.ShapeDtypeStruct(*s) for s in...  14.9 us
    all_to_all x1, blocking collectives, on_device(): lax.all_to_all(jnp.broadcast_to(gram[None], (X * Y,) + gram.shape), ('x',...  14.5 us
    ppermute x9, starting transfers between devices, apply_graph(): lax.ppermute(part, 'y', [(y, (y + step) % Y) for y in range(Y)])  11.7 us
    all_to_all x1, blocking collectives, on_device(): lax.all_to_all(jnp.broadcast_to(gram[None], (Z,) + gram.shape), 'z', 0, 0)  11.1 us
    ppermute x3, starting transfers between devices, window(): other = lax.ppermute(own, ALL, x_neighbour_pairs())  7.48 us
    unnamed x8, local copies, waits for them, and re-layouts  4.84 us
  transfers between devices with their start and end apart: 16, of which 13 were waited for; matrix products, arithmetic and copies ran while one was open for 0% of the time, Pallas kernels for 3%

profile of v5, /device:TPU:8, one launch (start us, length us, event | category | flops | bytes accessed | tf_op | source)
XLA Modules:
  0.0 152.8 jit_solution(12406150178707561281)
XLA Ops:
  0.0 0.9 copy-done.1
  1.0 2.8 %collective-permute-start = (bf16[256,128]{1,0:T(8,128)(2,1)S(1)}, bf16[256,128]{1,0:T(8,128)(2,1)S(1)}, u32[]{:S(2)}, u32[]{:S(2)}) collective-permute-start(bf16[256,128]{1,0:T(8,128)(2,1)S(1)} %shard_map.55.own.refs_5_), channel_id=1, source_target_pairs={{0,192},{1,193},{2,194},{3,195},{4,196},{5,197},{6,198},{7,199},{8... | collective-permute-start | bytes 196616 | tf_op jit(solution)/shard_map/ppermute | solution.py:103
  4.5 4.0 %copy-done = bf16[10,2048,256]{2,1,0:T(8,128)(2,1)S(1)} copy-done((bf16[10,2048,256]{2,1,0:T(8,128)(2,1)S(1)}, bf16[10,2048,256]{2,1,0:T(8,128)(2,1)}, u32[]{:S(2)}) %copy-start) | copy-done | bytes 10485784
  8.6 24.2 %all_to_all.25.slots = bf16[8,256,128]{2,1,0:T(8,128)(2,1)S(1)} all-to-all(bf16[8,256,128]{2,1,0:T(8,128)(2,1)S(1)} %shard_map.57), channel_id=1, replica_groups=mesh['x'=4,'z'=8,'y'=4,'core'=2] {'z'}, dimensions={0} | all-to-all | bytes 1048576 | tf_op jit(solution)/shard_map/all_to_all | solution.py:113
  32.8 1.9 %shard_map.58 = (f32[4,256,128]{2,1,0:T(8,128)S(1)}, bf16[10,256,128]{2,1,0:T(8,128)(2,1)S(1)}) custom-call(s32[10]{0:T(128)S(1)} %copy-done.2, s32[10]{0:T(128)S(1)} %copy-done.3, s32[1]{0:T(128)S(6)} %copy.6.refs_2_.tile_count, bf16[10,2048,256]{2,1,0:T(8,128)(2,1)S(1)} %copy-done, bf16[8,256,128]{2,1,0:T(8,128)(2,1)S(1)} %all_to_all.25.slots), custom_call_target="tpu_custom_call" | custom-call | flops 671088640 | bytes 5242880 | tf_op jit(solution)/shard_map/pallas_call | solution.py:28
  34.8 1.5 shard_map.59.refs_0_
  36.7 2.4 %collective-permute-start.4 = (f32[256,128]{1,0:T(8,128)S(1)}, f32[256,128]{1,0:T(8,128)S(1)}, u32[]{:S(2)}, u32[]{:S(2)}) collective-permute-start(f32[256,128]{1,0:T(8,128)S(1)} %get-tuple-element.39), channel_id=1, source_target_pairs={{0,4},{2,6},{4,0},{6,2},{1,5},{3,7},{5,1},{7,3},{8,12},{10,14},{12... | collective-permute-start | bytes 393224 | tf_op jit(solution)/shard_map/ppermute | solution.py:193
  39.1 2.0 %collective-permute-start.2 = (f32[256,128]{1,0:T(8,128)S(1)}, f32[256,128]{1,0:T(8,128)S(1)}, u32[]{:S(2)}, u32[]{:S(2)}) collective-permute-start(f32[256,128]{1,0:T(8,128)S(1)} %get-tuple-element.41), channel_id=1, source_target_pairs={{0,6},{2,0},{4,2},{6,4},{1,7},{3,1},{5,3},{7,5},{8,14},{10,8},{12,... | collective-permute-start | bytes 393224 | tf_op jit(solution)/shard_map/ppermute | solution.py:193
  41.1 3.5 %collective-permute-done.4.refs_4_ = f32[256,128]{1,0:T(8,128)S(1)} collective-permute-done((f32[256,128]{1,0:T(8,128)S(1)}, f32[256,128]{1,0:T(8,128)S(1)}, u32[]{:S(2)}, u32[]{:S(2)}) %collective-permute-start.4) | collective-permute-done | bytes 131104 | tf_op jit(solution)/shard_map/ppermute | solution.py:193
  44.7 2.2 %collective-permute-done.3.refs_3_ = f32[256,128]{1,0:T(8,128)S(1)} collective-permute-done((f32[256,128]{1,0:T(8,128)S(1)}, f32[256,128]{1,0:T(8,128)S(1)}, u32[]{:S(2)}, u32[]{:S(2)}) %collective-permute-start.3) | collective-permute-done | bytes 131104 | tf_op jit(solution)/shard_map/ppermute | solution.py:193
  46.9 1.8 %collective-permute-start.5 = (bf16[272,128]{1,0:T(8,128)(2,1)S(1)}, bf16[272,128]{1,0:T(8,128)(2,1)S(1)}, u32[]{:S(2)}, u32[]{:S(2)}) collective-permute-start(bf16[272,128]{1,0:T(8,128)(2,1)S(1)} %get-tuple-element.21.own), channel_id=1, source_target_pairs={{0,192},{1,193},{2,194},{3,195},{4,196},{5,197},{6,198},{7,199},{8... | collective-permute-start | bytes 208904 | tf_op jit(solution)/shard_map/ppermute | solution.py:103
  48.7 2.6 %collective-permute-done.5.other = bf16[272,128]{1,0:T(8,128)(2,1)S(1)} collective-permute-done((bf16[272,128]{1,0:T(8,128)(2,1)S(1)}, bf16[272,128]{1,0:T(8,128)(2,1)S(1)}, u32[]{:S(2)}, u32[]{:S(2)}) %collective-permute-start.5) | collective-permute-done | bytes 69664 | tf_op jit(solution)/shard_map/ppermute | solution.py:103
  51.4 19.9 %all_to_all.26.slots = bf16[8,272,128]{2,1,0:T(8,128)(2,1)S(1)} all-to-all(bf16[8,272,128]{2,1,0:T(8,128)(2,1)S(1)} %shard_map.61), channel_id=1, replica_groups=mesh['x'=4,'z'=8,'y'=4,'core'=2] {'z'}, dimensions={0} | all-to-all | bytes 1114112 | tf_op jit(solution)/shard_map/all_to_all | solution.py:113
  71.4 1.9 %shard_map.62 = (f32[4,264,128]{2,1,0:T(8,128)S(1)}, bf16[10,256,128]{2,1,0:T(8,128)(2,1)S(1)}, f32[8,128]{1,0:T(8,128)S(1)}) custom-call(s32[10]{0:T(128)S(1)} %copy-done.2, s32[10]{0:T(128)S(1)} %copy-done.3, s32[1]{0:T(128)S(6)} %copy.6.refs_2_.tile_count, bf16[10,2048,256]{2,1,0:T(8,128)(2,1)S(1)} %copy-done, bf16[8,272,128]{2,1,0:T(8,128)(2,1)S(1)} %all_to_all.26.slots), custom_call_target="tpu_custom_call" | custom-call | flops 671088640 | bytes 5242880 | tf_op jit(solution)/shard_map/pallas_call | solution.py:28
  73.5 1.5 %shard_map.63.refs_0_ = f32[4,264,128]{2,1,0:T(8,128)S(1)} custom-call(bf16[10,2048,256]{2,1,0:T(8,128)(2,1)S(1)} %copy-done, bf16[10,256,128]{2,1,0:T(8,128)(2,1)S(1)} %get-tuple-element.22.rhs, f32[8,128]{1,0:T(8,128)S(1)} %get-tuple-element.23.refs_0_), custom_call_target="tpu_custom_call" | custom-call | flops 671088640 | bytes 5242880 | tf_op jit(solution)/shard_map/pallas_call | solution.py:28
  75.5 1.8 %collective-permute-start.9 = (f32[264,128]{1,0:T(8,128)S(1)}, f32[264,128]{1,0:T(8,128)S(1)}, u32[]{:S(2)}, u32[]{:S(2)}) collective-permute-start(f32[264,128]{1,0:T(8,128)S(1)} %get-tuple-element.33), channel_id=1, source_target_pairs={{0,4},{2,6},{4,0},{6,2},{1,5},{3,7},{5,1},{7,3},{8,12},{10,14},{12... | collective-permute-start | bytes 405512 | tf_op jit(solution)/shard_map/ppermute | solution.py:193
  77.3 2.0 %collective-permute-start.7 = (f32[264,128]{1,0:T(8,128)S(1)}, f32[264,128]{1,0:T(8,128)S(1)}, u32[]{:S(2)}, u32[]{:S(2)}) collective-permute-start(f32[264,128]{1,0:T(8,128)S(1)} %get-tuple-element.35), channel_id=1, source_target_pairs={{0,6},{2,0},{4,2},{6,4},{1,7},{3,1},{5,3},{7,5},{8,14},{10,8},{12,... | collective-permute-start | bytes 405512 | tf_op jit(solution)/shard_map/ppermute | solution.py:193
  79.4 4.2 %collective-permute-done.9.refs_4_ = f32[264,128]{1,0:T(8,128)S(1)} collective-permute-done((f32[264,128]{1,0:T(8,128)S(1)}, f32[264,128]{1,0:T(8,128)S(1)}, u32[]{:S(2)}, u32[]{:S(2)}) %collective-permute-start.9) | collective-permute-done | bytes 135200 | tf_op jit(solution)/shard_map/ppermute | solution.py:193
  84.3 1.3 collective-permute-done.7.refs_2_
  85.7 2.8 %collective-permute-start.10 = (bf16[272,128]{1,0:T(8,128)(2,1)S(1)}, bf16[272,128]{1,0:T(8,128)(2,1)S(1)}, u32[]{:S(2)}, u32[]{:S(2)}) collective-permute-start(bf16[272,128]{1,0:T(8,128)(2,1)S(1)} %get-tuple-element.25.own), channel_id=1, source_target_pairs={{0,192},{1,193},{2,194},{3,195},{4,196},{5,197},{6,198},{7,199},{8... | collective-permute-start | bytes 208904 | tf_op jit(solution)/shard_map/ppermute | solution.py:103
  88.5 1.9 %collective-permute-done.10.other = bf16[272,128]{1,0:T(8,128)(2,1)S(1)} collective-permute-done((bf16[272,128]{1,0:T(8,128)(2,1)S(1)}, bf16[272,128]{1,0:T(8,128)(2,1)S(1)}, u32[]{:S(2)}, u32[]{:S(2)}) %collective-permute-start.10) | collective-permute-done | bytes 69664 | tf_op jit(solution)/shard_map/ppermute | solution.py:103
  90.6 20.2 %all_to_all.27.slots = bf16[8,272,128]{2,1,0:T(8,128)(2,1)S(1)} all-to-all(bf16[8,272,128]{2,1,0:T(8,128)(2,1)S(1)} %shard_map.65), channel_id=1, replica_groups=mesh['x'=4,'z'=8,'y'=4,'core'=2] {'z'}, dimensions={0} | all-to-all | bytes 1114112 | tf_op jit(solution)/shard_map/all_to_all | solution.py:113
  110.8 1.9 %shard_map.66 = (f32[4,256,128]{2,1,0:T(8,128)S(1)}, bf16[10,256,128]{2,1,0:T(8,128)(2,1)S(1)}, f32[8,128]{1,0:T(8,128)S(1)}) custom-call(s32[10]{0:T(128)S(1)} %copy-done.2, s32[10]{0:T(128)S(1)} %copy-done.3, s32[1]{0:T(128)S(6)} %copy.6.refs_2_.tile_count, bf16[10,2048,256]{2,1,0:T(8,128)(2,1)S(1)} %copy-done, bf16[8,272,128]{2,1,0:T(8,128)(2,1)S(1)} %all_to_all.27.slots), custom_call_target="tpu_custom_call" | custom-call | flops 671088640 | bytes 5242880 | tf_op jit(solution)/shard_map/pallas_call | solution.py:28
  112.8 1.5 %shard_map.67.refs_0_ = f32[4,256,128]{2,1,0:T(8,128)S(1)} custom-call(bf16[10,2048,256]{2,1,0:T(8,128)(2,1)S(1)} %copy-done, bf16[10,256,128]{2,1,0:T(8,128)(2,1)S(1)} %get-tuple-element.27.rhs), custom_call_target="tpu_custom_call" | custom-call | flops 671088640 | bytes 5242880 | tf_op jit(solution)/shard_map/pallas_call | solution.py:28
  114.7 1.4 collective-permute-start.14
  116.4 1.7 %collective-permute-start.12 = (bf16[256,128]{1,0:T(8,128)(2,1)S(1)}, bf16[256,128]{1,0:T(8,128)(2,1)S(1)}, u32[]{:S(2)}, u32[]{:S(2)}) collective-permute-start(bf16[256,128]{1,0:T(8,128)(2,1)S(1)} %get-tuple-element.38), channel_id=1, source_target_pairs={{0,6},{2,0},{4,2},{6,4},{1,7},{3,1},{5,3},{7,5},{8,14},{10,8},{12,... | collective-permute-start | bytes 196616 | tf_op jit(solution)/shard_map/ppermute | solution.py:193
  118.1 2.5 %collective-permute-done.14.refs_4_ = bf16[256,128]{1,0:T(8,128)(2,1)S(1)} collective-permute-done((bf16[256,128]{1,0:T(8,128)(2,1)S(1)}, bf16[256,128]{1,0:T(8,128)(2,1)S(1)}, u32[]{:S(2)}, u32[]{:S(2)}) %collective-permute-start.14) | collective-permute-done | bytes 65568 | tf_op jit(solution)/shard_map/ppermute | solution.py:193
  120.7 1.2 collective-permute-done.12.refs_2_
  122.5 1.2 collective-permute-done.15
  123.7 14.5 %all_to_all.28 = f32[16,24,128]{2,1,0:T(8,128)S(1)} all-to-all(f32[16,24,128]{2,1,0:T(8,128)S(1)} %broadcast_in_dim.4), channel_id=1, replica_groups=mesh['x'=4,'z'=8,'y'=4,'core'=2] {'x','y'}, dimensions={0} | all-to-all | bytes 393216 | tf_op jit(solution)/shard_map/all_to_all | solution.py:345
  138.2 11.1 %all_to_all.29.grams = f32[8,24,128]{2,1,0:T(8,128)S(1)} all-to-all(f32[8,24,128]{2,1,0:T(8,128)S(1)} %broadcast_in_dim.5), channel_id=1, replica_groups=mesh['x'=4,'z'=8,'y'=4,'core'=2] {'z'}, dimensions={0} | all-to-all | bytes 196608 | tf_op jit(solution)/shard_map/all_to_all | solution.py:347
  149.4 3.4 %shard_map.69 = f32[2,64,256]{2,1,0:T(8,128)} custom-call(f32[8,24,128]{2,1,0:T(8,128)S(1)} %all_to_all.29.grams, f32[256,128]{1,0:T(8,128)S(1)} %get-tuple-element.32.filtered), custom_call_target="tpu_custom_call" | custom-call | tf_op jit(solution)/shard_map/pallas_call | solution.py:28
  (35 shorter events, 4.2 us)
Async XLA Ops:
  0.0 8.5 %copy-start.3 = (s32[10]{0:T(128)S(1)}, s32[10]{0:T(128)}, u32[]{:S(2)}) copy-start(s32[10]{0:T(128)} %tile_col.5) | copy-start | bytes 124
  0.0 8.5 %copy-start.2 = (s32[10]{0:T(128)S(1)}, s32[10]{0:T(128)}, u32[]{:S(2)}) copy-start(s32[10]{0:T(128)} %tile_row.5) | copy-start | bytes 124
  0.0 0.9 copy-start.1
  1.0 7.5 %collective-permute-start = (bf16[256,128]{1,0:T(8,128)(2,1)S(1)}, bf16[256,128]{1,0:T(8,128)(2,1)S(1)}, u32[]{:S(2)}, u32[]{:S(2)}) collective-permute-start(bf16[256,128]{1,0:T(8,128)(2,1)S(1)} %shard_map.55.own.refs_5_), channel_id=1, source_target_pairs={{0,192},{1,193},{2,194},{3,195},{4,196},{5,197},{6,198},{7,199},{8... | collective-permute-start | bytes 196616 | tf_op jit(solution)/shard_map/ppermute | solution.py:103
  4.5 4.0 %copy-start = (bf16[10,2048,256]{2,1,0:T(8,128)(2,1)S(1)}, bf16[10,2048,256]{2,1,0:T(8,128)(2,1)}, u32[]{:S(2)}) copy-start(bf16[10,2048,256]{2,1,0:T(8,128)(2,1)} %tiles.13) | copy-start | bytes 31457284
  34.7 2.0 %collective-permute-start.1 = (f32[4,256,128]{2,1,0:T(8,128)S(1)}, f32[4,256,128]{2,1,0:T(8,128)S(1)}, u32[]{:S(2)}, u32[]{:S(2)}) collective-permute-start(f32[4,256,128]{2,1,0:T(8,128)S(1)} %get-tuple-element.20), channel_id=1, source_target_pairs={{0,1},{1,0},{2,3},{3,2},{4,5},{5,4},{6,7},{7,6},{8,9},{9,8},{10,11... | collective-permute-start | bytes 1572872 | tf_op jit(solution)/shard_map/ppermute | solution.py:185
  36.7 7.9 %collective-permute-start.4 = (f32[256,128]{1,0:T(8,128)S(1)}, f32[256,128]{1,0:T(8,128)S(1)}, u32[]{:S(2)}, u32[]{:S(2)}) collective-permute-start(f32[256,128]{1,0:T(8,128)S(1)} %get-tuple-element.39), channel_id=1, source_target_pairs={{0,4},{2,6},{4,0},{6,2},{1,5},{3,7},{5,1},{7,3},{8,12},{10,14},{12... | collective-permute-start | bytes 393224 | tf_op jit(solution)/shard_map/ppermute | solution.py:193
  39.1 7.7 %collective-permute-start.3 = (f32[256,128]{1,0:T(8,128)S(1)}, f32[256,128]{1,0:T(8,128)S(1)}, u32[]{:S(2)}, u32[]{:S(2)}) collective-permute-start(f32[256,128]{1,0:T(8,128)S(1)} %get-tuple-element.40), channel_id=1, source_target_pairs={{0,2},{2,4},{4,6},{6,0},{1,3},{3,5},{5,7},{7,1},{8,10},{10,12},{12... | collective-permute-start | bytes 393224 | tf_op jit(solution)/shard_map/ppermute | solution.py:193
  39.1 7.7 %collective-permute-start.2 = (f32[256,128]{1,0:T(8,128)S(1)}, f32[256,128]{1,0:T(8,128)S(1)}, u32[]{:S(2)}, u32[]{:S(2)}) collective-permute-start(f32[256,128]{1,0:T(8,128)S(1)} %get-tuple-element.41), channel_id=1, source_target_pairs={{0,6},{2,0},{4,2},{6,4},{1,7},{3,1},{5,3},{7,5},{8,14},{10,8},{12,... | collective-permute-start | bytes 393224 | tf_op jit(solution)/shard_map/ppermute | solution.py:193
  46.9 4.4 %collective-permute-start.5 = (bf16[272,128]{1,0:T(8,128)(2,1)S(1)}, bf16[272,128]{1,0:T(8,128)(2,1)S(1)}, u32[]{:S(2)}, u32[]{:S(2)}) collective-permute-start(bf16[272,128]{1,0:T(8,128)(2,1)S(1)} %get-tuple-element.21.own), channel_id=1, source_target_pairs={{0,192},{1,193},{2,194},{3,195},{4,196},{5,197},{6,198},{7,199},{8... | collective-permute-start | bytes 208904 | tf_op jit(solution)/shard_map/ppermute | solution.py:103
  73.3 2.2 %collective-permute-start.6 = (f32[4,264,128]{2,1,0:T(8,128)S(1)}, f32[4,264,128]{2,1,0:T(8,128)S(1)}, u32[]{:S(2)}, u32[]{:S(2)}) collective-permute-start(f32[4,264,128]{2,1,0:T(8,128)S(1)} %get-tuple-element.24), channel_id=1, source_target_pairs={{0,1},{1,0},{2,3},{3,2},{4,5},{5,4},{6,7},{7,6},{8,9},{9,8},{10,11... | collective-permute-start | bytes 1622024 | tf_op jit(solution)/shard_map/ppermute | solution.py:185
  75.5 8.1 %collective-permute-start.9 = (f32[264,128]{1,0:T(8,128)S(1)}, f32[264,128]{1,0:T(8,128)S(1)}, u32[]{:S(2)}, u32[]{:S(2)}) collective-permute-start(f32[264,128]{1,0:T(8,128)S(1)} %get-tuple-element.33), channel_id=1, source_target_pairs={{0,4},{2,6},{4,0},{6,2},{1,5},{3,7},{5,1},{7,3},{8,12},{10,14},{12... | collective-permute-start | bytes 405512 | tf_op jit(solution)/shard_map/ppermute | solution.py:193
  77.3 7.0 %collective-permute-start.8 = (f32[264,128]{1,0:T(8,128)S(1)}, f32[264,128]{1,0:T(8,128)S(1)}, u32[]{:S(2)}, u32[]{:S(2)}) collective-permute-start(f32[264,128]{1,0:T(8,128)S(1)} %get-tuple-element.34), channel_id=1, source_target_pairs={{0,2},{2,4},{4,6},{6,0},{1,3},{3,5},{5,7},{7,1},{8,10},{10,12},{12... | collective-permute-start | bytes 405512 | tf_op jit(solution)/shard_map/ppermute | solution.py:193
  77.3 8.3 %collective-permute-start.7 = (f32[264,128]{1,0:T(8,128)S(1)}, f32[264,128]{1,0:T(8,128)S(1)}, u32[]{:S(2)}, u32[]{:S(2)}) collective-permute-start(f32[264,128]{1,0:T(8,128)S(1)} %get-tuple-element.35), channel_id=1, source_target_pairs={{0,6},{2,0},{4,2},{6,4},{1,7},{3,1},{5,3},{7,5},{8,14},{10,8},{12,... | collective-permute-start | bytes 405512 | tf_op jit(solution)/shard_map/ppermute | solution.py:193
  85.7 4.8 %collective-permute-start.10 = (bf16[272,128]{1,0:T(8,128)(2,1)S(1)}, bf16[272,128]{1,0:T(8,128)(2,1)S(1)}, u32[]{:S(2)}, u32[]{:S(2)}) collective-permute-start(bf16[272,128]{1,0:T(8,128)(2,1)S(1)} %get-tuple-element.25.own), channel_id=1, source_target_pairs={{0,192},{1,193},{2,194},{3,195},{4,196},{5,197},{6,198},{7,199},{8... | collective-permute-start | bytes 208904 | tf_op jit(solution)/shard_map/ppermute | solution.py:103
  112.7 2.0 %collective-permute-start.11 = (f32[4,256,128]{2,1,0:T(8,128)S(1)}, f32[4,256,128]{2,1,0:T(8,128)S(1)}, u32[]{:S(2)}, u32[]{:S(2)}) collective-permute-start(f32[4,256,128]{2,1,0:T(8,128)S(1)} %get-tuple-element.28), channel_id=1, source_target_pairs={{0,1},{1,0},{2,3},{3,2},{4,5},{5,4},{6,7},{7,6},{8,9},{9,8},{10,11... | collective-permute-start | bytes 1572872 | tf_op jit(solution)/shard_map/ppermute | solution.py:185
  114.7 6.0 %collective-permute-start.14 = (bf16[256,128]{1,0:T(8,128)(2,1)S(1)}, bf16[256,128]{1,0:T(8,128)(2,1)S(1)}, u32[]{:S(2)}, u32[]{:S(2)}) collective-permute-start(bf16[256,128]{1,0:T(8,128)(2,1)S(1)} %get-tuple-element.36), channel_id=1, source_target_pairs={{0,4},{2,6},{4,0},{6,2},{1,5},{3,7},{5,1},{7,3},{8,12},{10,14},{12... | collective-permute-start | bytes 196616 | tf_op jit(solution)/shard_map/ppermute | solution.py:193
  116.1 4.6 %collective-permute-start.13 = (bf16[256,128]{1,0:T(8,128)(2,1)S(1)}, bf16[256,128]{1,0:T(8,128)(2,1)S(1)}, u32[]{:S(2)}, u32[]{:S(2)}) collective-permute-start(bf16[256,128]{1,0:T(8,128)(2,1)S(1)} %get-tuple-element.37), channel_id=1, source_target_pairs={{0,2},{2,4},{4,6},{6,0},{1,3},{3,5},{5,7},{7,1},{8,10},{10,12},{12... | collective-permute-start | bytes 196616 | tf_op jit(solution)/shard_map/ppermute | solution.py:193
  116.4 5.4 %collective-permute-start.12 = (bf16[256,128]{1,0:T(8,128)(2,1)S(1)}, bf16[256,128]{1,0:T(8,128)(2,1)S(1)}, u32[]{:S(2)}, u32[]{:S(2)}) collective-permute-start(bf16[256,128]{1,0:T(8,128)(2,1)S(1)} %get-tuple-element.38), channel_id=1, source_target_pairs={{0,6},{2,0},{4,2},{6,4},{1,7},{3,1},{5,3},{7,5},{8,14},{10,8},{12,... | collective-permute-start | bytes 196616 | tf_op jit(solution)/shard_map/ppermute | solution.py:193
  122.4 1.3 collective-permute-start.15

commit v6 on v5

--- a/solution.py
+++ b/solution.py
@@ -186,7 +186,7 @@
     given = [tiles, rhs] + (sums if stage == 1 else [])
     kept = call(functools.partial(keep_kernel, stage), slices, [VMEM] * len(given), *given, **size)
     parts = []
-    for step in (3, 1, 2):
+    for step in (2, 3, 1):
         part = kept[step] + received[step]
         if stage == 2:
             part = part.astype(BF16)

time: 153 us -> 151 us (0.987)
  blocking collectives: 89.9 us -> 87.3 us
    all_to_all x3, blocking collectives: 64.3 us -> 62.4 us  [window(): return lax.all_to_all(pieces, 'z', 0, 0)]
  transfers between devices with their start and end apart: 16 -> 16, of which waited for: 13 -> 14; matrix products, arithmetic and copies ran while one was open for 0% -> 0% of each run, Pallas kernels for 3% -> 3%
where the time goes in v6:
time: 151 us
  blocking collectives  87.3 us (58%)
  waiting for transfers between devices  22.9 us (15%)
  starting transfers between devices  20.2 us (13%)
  Pallas kernels  14.8 us (10%)
  local copies, waits for them, and re-layouts  4.87 us (3%)
    all_to_all x3, blocking collectives, window(): return lax.all_to_all(pieces, 'z', 0, 0)  62.4 us
    ppermute x9, waiting for transfers between devices, apply_graph(): lax.ppermute(part, 'y', [(y, (y + step) % Y) for y in range(Y)])  16.1 us
    pallas_call x15, Pallas kernels, call(): pl.pallas_call(kernel, out_shape=tuple((jax.ShapeDtypeStruct(*s) for s in...  14.8 us
    all_to_all x1, blocking collectives, on_device(): lax.all_to_all(jnp.broadcast_to(gram[None], (X * Y,) + gram.shape), ('x',...  13.8 us
    ppermute x9, starting transfers between devices, apply_graph(): lax.ppermute(part, 'y', [(y, (y + step) % Y) for y in range(Y)])  12.1 us
    all_to_all x1, blocking collectives, on_device(): lax.all_to_all(jnp.broadcast_to(gram[None], (Z,) + gram.shape), 'z', 0, 0)  11.1 us
    ppermute x3, starting transfers between devices, window(): other = lax.ppermute(own, ALL, x_neighbour_pairs())  7.48 us
    unnamed x8, local copies, waits for them, and re-layouts  4.84 us
  transfers between devices with their start and end apart: 16, of which 14 were waited for; matrix products, arithmetic and copies ran while one was open for 0% of the time, Pallas kernels for 3%

profile of v6, /device:TPU:8, one launch (start us, length us, event | category | flops | bytes accessed | tf_op | source)
XLA Modules:
  0.0 151.0 jit_solution(2652430050686544724)
XLA Ops:
  0.0 0.9 copy-done.1
  1.0 2.8 %collective-permute-start = (bf16[256,128]{1,0:T(8,128)(2,1)S(1)}, bf16[256,128]{1,0:T(8,128)(2,1)S(1)}, u32[]{:S(2)}, u32[]{:S(2)}) collective-permute-start(bf16[256,128]{1,0:T(8,128)(2,1)S(1)} %shard_map.55.own.refs_5_), channel_id=1, source_target_pairs={{0,192},{1,193},{2,194},{3,195},{4,196},{5,197},{6,198},{7,199},{8... | collective-permute-start | bytes 196616 | tf_op jit(solution)/shard_map/ppermute | solution.py:103
  4.5 4.0 %copy-done = bf16[10,2048,256]{2,1,0:T(8,128)(2,1)S(1)} copy-done((bf16[10,2048,256]{2,1,0:T(8,128)(2,1)S(1)}, bf16[10,2048,256]{2,1,0:T(8,128)(2,1)}, u32[]{:S(2)}) %copy-start) | copy-done | bytes 10485784
  8.6 24.2 %all_to_all.25.slots = bf16[8,256,128]{2,1,0:T(8,128)(2,1)S(1)} all-to-all(bf16[8,256,128]{2,1,0:T(8,128)(2,1)S(1)} %shard_map.57), channel_id=1, replica_groups=mesh['x'=4,'z'=8,'y'=4,'core'=2] {'z'}, dimensions={0} | all-to-all | bytes 1048576 | tf_op jit(solution)/shard_map/all_to_all | solution.py:113
  32.8 1.9 %shard_map.58 = (f32[4,256,128]{2,1,0:T(8,128)S(1)}, bf16[10,256,128]{2,1,0:T(8,128)(2,1)S(1)}) custom-call(s32[10]{0:T(128)S(1)} %copy-done.2, s32[10]{0:T(128)S(1)} %copy-done.3, s32[1]{0:T(128)S(6)} %copy.6.refs_2_.tile_count, bf16[10,2048,256]{2,1,0:T(8,128)(2,1)S(1)} %copy-done, bf16[8,256,128]{2,1,0:T(8,128)(2,1)S(1)} %all_to_all.25.slots), custom_call_target="tpu_custom_call" | custom-call | flops 671088640 | bytes 5242880 | tf_op jit(solution)/shard_map/pallas_call | solution.py:28
  34.8 1.5 %shard_map.59.refs_0_ = f32[4,256,128]{2,1,0:T(8,128)S(1)} custom-call(bf16[10,2048,256]{2,1,0:T(8,128)(2,1)S(1)} %copy-done, bf16[10,256,128]{2,1,0:T(8,128)(2,1)S(1)} %get-tuple-element.19.rhs), custom_call_target="tpu_custom_call" | custom-call | flops 671088640 | bytes 5242880 | tf_op jit(solution)/shard_map/pallas_call | solution.py:28
  36.7 1.7 %collective-permute-start.4 = (f32[256,128]{1,0:T(8,128)S(1)}, f32[256,128]{1,0:T(8,128)S(1)}, u32[]{:S(2)}, u32[]{:S(2)}) collective-permute-start(f32[256,128]{1,0:T(8,128)S(1)} %get-tuple-element.39), channel_id=1, source_target_pairs={{0,2},{2,4},{4,6},{6,0},{1,3},{3,5},{5,7},{7,1},{8,10},{10,12},{12... | collective-permute-start | bytes 393224 | tf_op jit(solution)/shard_map/ppermute | solution.py:193
  38.8 2.3 %collective-permute-start.2 = (f32[256,128]{1,0:T(8,128)S(1)}, f32[256,128]{1,0:T(8,128)S(1)}, u32[]{:S(2)}, u32[]{:S(2)}) collective-permute-start(f32[256,128]{1,0:T(8,128)S(1)} %get-tuple-element.41), channel_id=1, source_target_pairs={{0,4},{2,6},{4,0},{6,2},{1,5},{3,7},{5,1},{7,3},{8,12},{10,14},{12... | collective-permute-start | bytes 393224 | tf_op jit(solution)/shard_map/ppermute | solution.py:193
  41.1 1.2 collective-permute-done.4.refs_4_
  42.3 1.7 %collective-permute-done.3.refs_3_ = f32[256,128]{1,0:T(8,128)S(1)} collective-permute-done((f32[256,128]{1,0:T(8,128)S(1)}, f32[256,128]{1,0:T(8,128)S(1)}, u32[]{:S(2)}, u32[]{:S(2)}) %collective-permute-start.3) | collective-permute-done | bytes 131104 | tf_op jit(solution)/shard_map/ppermute | solution.py:193
  44.0 3.1 %collective-permute-done.2.refs_2_ = f32[256,128]{1,0:T(8,128)S(1)} collective-permute-done((f32[256,128]{1,0:T(8,128)S(1)}, f32[256,128]{1,0:T(8,128)S(1)}, u32[]{:S(2)}, u32[]{:S(2)}) %collective-permute-start.2) | collective-permute-done | bytes 131104 | tf_op jit(solution)/shard_map/ppermute | solution.py:193
  47.3 1.8 %collective-permute-start.5 = (bf16[272,128]{1,0:T(8,128)(2,1)S(1)}, bf16[272,128]{1,0:T(8,128)(2,1)S(1)}, u32[]{:S(2)}, u32[]{:S(2)}) collective-permute-start(bf16[272,128]{1,0:T(8,128)(2,1)S(1)} %get-tuple-element.21.own), channel_id=1, source_target_pairs={{0,192},{1,193},{2,194},{3,195},{4,196},{5,197},{6,198},{7,199},{8... | collective-permute-start | bytes 208904 | tf_op jit(solution)/shard_map/ppermute | solution.py:103
  49.1 2.6 %collective-permute-done.5.other = bf16[272,128]{1,0:T(8,128)(2,1)S(1)} collective-permute-done((bf16[272,128]{1,0:T(8,128)(2,1)S(1)}, bf16[272,128]{1,0:T(8,128)(2,1)S(1)}, u32[]{:S(2)}, u32[]{:S(2)}) %collective-permute-start.5) | collective-permute-done | bytes 69664 | tf_op jit(solution)/shard_map/ppermute | solution.py:103
  51.8 19.0 %all_to_all.26.slots = bf16[8,272,128]{2,1,0:T(8,128)(2,1)S(1)} all-to-all(bf16[8,272,128]{2,1,0:T(8,128)(2,1)S(1)} %shard_map.61), channel_id=1, replica_groups=mesh['x'=4,'z'=8,'y'=4,'core'=2] {'z'}, dimensions={0} | all-to-all | bytes 1114112 | tf_op jit(solution)/shard_map/all_to_all | solution.py:113
  70.8 1.9 %shard_map.62 = (f32[4,264,128]{2,1,0:T(8,128)S(1)}, bf16[10,256,128]{2,1,0:T(8,128)(2,1)S(1)}, f32[8,128]{1,0:T(8,128)S(1)}) custom-call(s32[10]{0:T(128)S(1)} %copy-done.2, s32[10]{0:T(128)S(1)} %copy-done.3, s32[1]{0:T(128)S(6)} %copy.6.refs_2_.tile_count, bf16[10,2048,256]{2,1,0:T(8,128)(2,1)S(1)} %copy-done, bf16[8,272,128]{2,1,0:T(8,128)(2,1)S(1)} %all_to_all.26.slots), custom_call_target="tpu_custom_call" | custom-call | flops 671088640 | bytes 5242880 | tf_op jit(solution)/shard_map/pallas_call | solution.py:28
  73.0 1.5 %shard_map.63.refs_0_ = f32[4,264,128]{2,1,0:T(8,128)S(1)} custom-call(bf16[10,2048,256]{2,1,0:T(8,128)(2,1)S(1)} %copy-done, bf16[10,256,128]{2,1,0:T(8,128)(2,1)S(1)} %get-tuple-element.22.rhs, f32[8,128]{1,0:T(8,128)S(1)} %get-tuple-element.23.refs_0_), custom_call_target="tpu_custom_call" | custom-call | flops 671088640 | bytes 5242880 | tf_op jit(solution)/shard_map/pallas_call | solution.py:28
  75.1 2.0 %collective-permute-start.8 = (f32[264,128]{1,0:T(8,128)S(1)}, f32[264,128]{1,0:T(8,128)S(1)}, u32[]{:S(2)}, u32[]{:S(2)}) collective-permute-start(f32[264,128]{1,0:T(8,128)S(1)} %get-tuple-element.34), channel_id=1, source_target_pairs={{0,6},{2,0},{4,2},{6,4},{1,7},{3,1},{5,3},{7,5},{8,14},{10,8},{12,... | collective-permute-start | bytes 405512 | tf_op jit(solution)/shard_map/ppermute | solution.py:193
  77.1 1.6 %collective-permute-start.7 = (f32[264,128]{1,0:T(8,128)S(1)}, f32[264,128]{1,0:T(8,128)S(1)}, u32[]{:S(2)}, u32[]{:S(2)}) collective-permute-start(f32[264,128]{1,0:T(8,128)S(1)} %get-tuple-element.35), channel_id=1, source_target_pairs={{0,4},{2,6},{4,0},{6,2},{1,5},{3,7},{5,1},{7,3},{8,12},{10,14},{12... | collective-permute-start | bytes 405512 | tf_op jit(solution)/shard_map/ppermute | solution.py:193
  78.6 2.8 %collective-permute-done.9.refs_4_ = f32[264,128]{1,0:T(8,128)S(1)} collective-permute-done((f32[264,128]{1,0:T(8,128)S(1)}, f32[264,128]{1,0:T(8,128)S(1)}, u32[]{:S(2)}, u32[]{:S(2)}) %collective-permute-start.9) | collective-permute-done | bytes 135200 | tf_op jit(solution)/shard_map/ppermute | solution.py:193
  81.4 3.5 %collective-permute-done.7.refs_2_ = f32[264,128]{1,0:T(8,128)S(1)} collective-permute-done((f32[264,128]{1,0:T(8,128)S(1)}, f32[264,128]{1,0:T(8,128)S(1)}, u32[]{:S(2)}, u32[]{:S(2)}) %collective-permute-start.7) | collective-permute-done | bytes 135200 | tf_op jit(solution)/shard_map/ppermute | solution.py:193
  84.9 2.8 %collective-permute-start.10 = (bf16[272,128]{1,0:T(8,128)(2,1)S(1)}, bf16[272,128]{1,0:T(8,128)(2,1)S(1)}, u32[]{:S(2)}, u32[]{:S(2)}) collective-permute-start(bf16[272,128]{1,0:T(8,128)(2,1)S(1)} %get-tuple-element.25.own), channel_id=1, source_target_pairs={{0,192},{1,193},{2,194},{3,195},{4,196},{5,197},{6,198},{7,199},{8... | collective-permute-start | bytes 208904 | tf_op jit(solution)/shard_map/ppermute | solution.py:103
  87.7 1.9 %collective-permute-done.10.other = bf16[272,128]{1,0:T(8,128)(2,1)S(1)} collective-permute-done((bf16[272,128]{1,0:T(8,128)(2,1)S(1)}, bf16[272,128]{1,0:T(8,128)(2,1)S(1)}, u32[]{:S(2)}, u32[]{:S(2)}) %collective-permute-start.10) | collective-permute-done | bytes 69664 | tf_op jit(solution)/shard_map/ppermute | solution.py:103
  89.8 19.1 %all_to_all.27.slots = bf16[8,272,128]{2,1,0:T(8,128)(2,1)S(1)} all-to-all(bf16[8,272,128]{2,1,0:T(8,128)(2,1)S(1)} %shard_map.65), channel_id=1, replica_groups=mesh['x'=4,'z'=8,'y'=4,'core'=2] {'z'}, dimensions={0} | all-to-all | bytes 1114112 | tf_op jit(solution)/shard_map/all_to_all | solution.py:113
  109.0 1.9 %shard_map.66 = (f32[4,256,128]{2,1,0:T(8,128)S(1)}, bf16[10,256,128]{2,1,0:T(8,128)(2,1)S(1)}, f32[8,128]{1,0:T(8,128)S(1)}) custom-call(s32[10]{0:T(128)S(1)} %copy-done.2, s32[10]{0:T(128)S(1)} %copy-done.3, s32[1]{0:T(128)S(6)} %copy.6.refs_2_.tile_count, bf16[10,2048,256]{2,1,0:T(8,128)(2,1)S(1)} %copy-done, bf16[8,272,128]{2,1,0:T(8,128)(2,1)S(1)} %all_to_all.27.slots), custom_call_target="tpu_custom_call" | custom-call | flops 671088640 | bytes 5242880 | tf_op jit(solution)/shard_map/pallas_call | solution.py:28
  111.0 1.5 %shard_map.67.refs_0_ = f32[4,256,128]{2,1,0:T(8,128)S(1)} custom-call(bf16[10,2048,256]{2,1,0:T(8,128)(2,1)S(1)} %copy-done, bf16[10,256,128]{2,1,0:T(8,128)(2,1)S(1)} %get-tuple-element.27.rhs), custom_call_target="tpu_custom_call" | custom-call | flops 671088640 | bytes 5242880 | tf_op jit(solution)/shard_map/pallas_call | solution.py:28
  113.6 1.4 collective-permute-start.13
  115.0 2.0 %collective-permute-start.12 = (bf16[256,128]{1,0:T(8,128)(2,1)S(1)}, bf16[256,128]{1,0:T(8,128)(2,1)S(1)}, u32[]{:S(2)}, u32[]{:S(2)}) collective-permute-start(bf16[256,128]{1,0:T(8,128)(2,1)S(1)} %get-tuple-element.38), channel_id=1, source_target_pairs={{0,4},{2,6},{4,0},{6,2},{1,5},{3,7},{5,1},{7,3},{8,12},{10,14},{12... | collective-permute-start | bytes 196616 | tf_op jit(solution)/shard_map/ppermute | solution.py:193
  117.8 2.9 %collective-permute-done.12.refs_2_ = bf16[256,128]{1,0:T(8,128)(2,1)S(1)} collective-permute-done((bf16[256,128]{1,0:T(8,128)(2,1)S(1)}, bf16[256,128]{1,0:T(8,128)(2,1)S(1)}, u32[]{:S(2)}, u32[]{:S(2)}) %collective-permute-start.12) | collective-permute-done | bytes 65568 | tf_op jit(solution)/shard_map/ppermute | solution.py:193
  121.4 1.2 collective-permute-done.15
  122.6 13.8 %all_to_all.28 = f32[16,24,128]{2,1,0:T(8,128)S(1)} all-to-all(f32[16,24,128]{2,1,0:T(8,128)S(1)} %broadcast_in_dim.4), channel_id=1, replica_groups=mesh['x'=4,'z'=8,'y'=4,'core'=2] {'x','y'}, dimensions={0} | all-to-all | bytes 393216 | tf_op jit(solution)/shard_map/all_to_all | solution.py:345
  136.5 11.1 %all_to_all.29.grams = f32[8,24,128]{2,1,0:T(8,128)S(1)} all-to-all(f32[8,24,128]{2,1,0:T(8,128)S(1)} %broadcast_in_dim.5), channel_id=1, replica_groups=mesh['x'=4,'z'=8,'y'=4,'core'=2] {'z'}, dimensions={0} | all-to-all | bytes 196608 | tf_op jit(solution)/shard_map/all_to_all | solution.py:347
  147.6 3.4 %shard_map.69 = f32[2,64,256]{2,1,0:T(8,128)} custom-call(f32[8,24,128]{2,1,0:T(8,128)S(1)} %all_to_all.29.grams, f32[256,128]{1,0:T(8,128)S(1)} %get-tuple-element.32.filtered), custom_call_target="tpu_custom_call" | custom-call | tf_op jit(solution)/shard_map/pallas_call | solution.py:28
  (35 shorter events, 5.2 us)
Async XLA Ops:
  0.0 8.5 %copy-start.3 = (s32[10]{0:T(128)S(1)}, s32[10]{0:T(128)}, u32[]{:S(2)}) copy-start(s32[10]{0:T(128)} %tile_col.5) | copy-start | bytes 124
  0.0 8.5 %copy-start.2 = (s32[10]{0:T(128)S(1)}, s32[10]{0:T(128)}, u32[]{:S(2)}) copy-start(s32[10]{0:T(128)} %tile_row.5) | copy-start | bytes 124
  0.0 0.9 copy-start.1
  1.0 7.5 %collective-permute-start = (bf16[256,128]{1,0:T(8,128)(2,1)S(1)}, bf16[256,128]{1,0:T(8,128)(2,1)S(1)}, u32[]{:S(2)}, u32[]{:S(2)}) collective-permute-start(bf16[256,128]{1,0:T(8,128)(2,1)S(1)} %shard_map.55.own.refs_5_), channel_id=1, source_target_pairs={{0,192},{1,193},{2,194},{3,195},{4,196},{5,197},{6,198},{7,199},{8... | collective-permute-start | bytes 196616 | tf_op jit(solution)/shard_map/ppermute | solution.py:103
  4.5 4.0 %copy-start = (bf16[10,2048,256]{2,1,0:T(8,128)(2,1)S(1)}, bf16[10,2048,256]{2,1,0:T(8,128)(2,1)}, u32[]{:S(2)}) copy-start(bf16[10,2048,256]{2,1,0:T(8,128)(2,1)} %tiles.13) | copy-start | bytes 31457284
  34.7 2.0 %collective-permute-start.1 = (f32[4,256,128]{2,1,0:T(8,128)S(1)}, f32[4,256,128]{2,1,0:T(8,128)S(1)}, u32[]{:S(2)}, u32[]{:S(2)}) collective-permute-start(f32[4,256,128]{2,1,0:T(8,128)S(1)} %get-tuple-element.20), channel_id=1, source_target_pairs={{0,1},{1,0},{2,3},{3,2},{4,5},{5,4},{6,7},{7,6},{8,9},{9,8},{10,11... | collective-permute-start | bytes 1572872 | tf_op jit(solution)/shard_map/ppermute | solution.py:185
  36.7 5.6 %collective-permute-start.4 = (f32[256,128]{1,0:T(8,128)S(1)}, f32[256,128]{1,0:T(8,128)S(1)}, u32[]{:S(2)}, u32[]{:S(2)}) collective-permute-start(f32[256,128]{1,0:T(8,128)S(1)} %get-tuple-element.39), channel_id=1, source_target_pairs={{0,2},{2,4},{4,6},{6,0},{1,3},{3,5},{5,7},{7,1},{8,10},{10,12},{12... | collective-permute-start | bytes 393224 | tf_op jit(solution)/shard_map/ppermute | solution.py:193
  38.4 5.7 %collective-permute-start.3 = (f32[256,128]{1,0:T(8,128)S(1)}, f32[256,128]{1,0:T(8,128)S(1)}, u32[]{:S(2)}, u32[]{:S(2)}) collective-permute-start(f32[256,128]{1,0:T(8,128)S(1)} %get-tuple-element.40), channel_id=1, source_target_pairs={{0,6},{2,0},{4,2},{6,4},{1,7},{3,1},{5,3},{7,5},{8,14},{10,8},{12,... | collective-permute-start | bytes 393224 | tf_op jit(solution)/shard_map/ppermute | solution.py:193
  38.8 8.3 %collective-permute-start.2 = (f32[256,128]{1,0:T(8,128)S(1)}, f32[256,128]{1,0:T(8,128)S(1)}, u32[]{:S(2)}, u32[]{:S(2)}) collective-permute-start(f32[256,128]{1,0:T(8,128)S(1)} %get-tuple-element.41), channel_id=1, source_target_pairs={{0,4},{2,6},{4,0},{6,2},{1,5},{3,7},{5,1},{7,3},{8,12},{10,14},{12... | collective-permute-start | bytes 393224 | tf_op jit(solution)/shard_map/ppermute | solution.py:193
  47.3 4.4 %collective-permute-start.5 = (bf16[272,128]{1,0:T(8,128)(2,1)S(1)}, bf16[272,128]{1,0:T(8,128)(2,1)S(1)}, u32[]{:S(2)}, u32[]{:S(2)}) collective-permute-start(bf16[272,128]{1,0:T(8,128)(2,1)S(1)} %get-tuple-element.21.own), channel_id=1, source_target_pairs={{0,192},{1,193},{2,194},{3,195},{4,196},{5,197},{6,198},{7,199},{8... | collective-permute-start | bytes 208904 | tf_op jit(solution)/shard_map/ppermute | solution.py:103
  72.7 2.2 %collective-permute-start.6 = (f32[4,264,128]{2,1,0:T(8,128)S(1)}, f32[4,264,128]{2,1,0:T(8,128)S(1)}, u32[]{:S(2)}, u32[]{:S(2)}) collective-permute-start(f32[4,264,128]{2,1,0:T(8,128)S(1)} %get-tuple-element.24), channel_id=1, source_target_pairs={{0,1},{1,0},{2,3},{3,2},{4,5},{5,4},{6,7},{7,6},{8,9},{9,8},{10,11... | collective-permute-start | bytes 1622024 | tf_op jit(solution)/shard_map/ppermute | solution.py:185
  75.0 6.4 %collective-permute-start.9 = (f32[264,128]{1,0:T(8,128)S(1)}, f32[264,128]{1,0:T(8,128)S(1)}, u32[]{:S(2)}, u32[]{:S(2)}) collective-permute-start(f32[264,128]{1,0:T(8,128)S(1)} %get-tuple-element.33), channel_id=1, source_target_pairs={{0,2},{2,4},{4,6},{6,0},{1,3},{3,5},{5,7},{7,1},{8,10},{10,12},{12... | collective-permute-start | bytes 405512 | tf_op jit(solution)/shard_map/ppermute | solution.py:193
  75.1 6.3 %collective-permute-start.8 = (f32[264,128]{1,0:T(8,128)S(1)}, f32[264,128]{1,0:T(8,128)S(1)}, u32[]{:S(2)}, u32[]{:S(2)}) collective-permute-start(f32[264,128]{1,0:T(8,128)S(1)} %get-tuple-element.34), channel_id=1, source_target_pairs={{0,6},{2,0},{4,2},{6,4},{1,7},{3,1},{5,3},{7,5},{8,14},{10,8},{12,... | collective-permute-start | bytes 405512 | tf_op jit(solution)/shard_map/ppermute | solution.py:193
  77.1 7.8 %collective-permute-start.7 = (f32[264,128]{1,0:T(8,128)S(1)}, f32[264,128]{1,0:T(8,128)S(1)}, u32[]{:S(2)}, u32[]{:S(2)}) collective-permute-start(f32[264,128]{1,0:T(8,128)S(1)} %get-tuple-element.35), channel_id=1, source_target_pairs={{0,4},{2,6},{4,0},{6,2},{1,5},{3,7},{5,1},{7,3},{8,12},{10,14},{12... | collective-permute-start | bytes 405512 | tf_op jit(solution)/shard_map/ppermute | solution.py:193
  84.9 4.8 %collective-permute-start.10 = (bf16[272,128]{1,0:T(8,128)(2,1)S(1)}, bf16[272,128]{1,0:T(8,128)(2,1)S(1)}, u32[]{:S(2)}, u32[]{:S(2)}) collective-permute-start(bf16[272,128]{1,0:T(8,128)(2,1)S(1)} %get-tuple-element.25.own), channel_id=1, source_target_pairs={{0,192},{1,193},{2,194},{3,195},{4,196},{5,197},{6,198},{7,199},{8... | collective-permute-start | bytes 208904 | tf_op jit(solution)/shard_map/ppermute | solution.py:103
  110.9 2.0 %collective-permute-start.11 = (f32[4,256,128]{2,1,0:T(8,128)S(1)}, f32[4,256,128]{2,1,0:T(8,128)S(1)}, u32[]{:S(2)}, u32[]{:S(2)}) collective-permute-start(f32[4,256,128]{2,1,0:T(8,128)S(1)} %get-tuple-element.28), channel_id=1, source_target_pairs={{0,1},{1,0},{2,3},{3,2},{4,5},{5,4},{6,7},{7,6},{8,9},{9,8},{10,11... | collective-permute-start | bytes 1572872 | tf_op jit(solution)/shard_map/ppermute | solution.py:185
  112.9 4.3 %collective-permute-start.14 = (bf16[256,128]{1,0:T(8,128)(2,1)S(1)}, bf16[256,128]{1,0:T(8,128)(2,1)S(1)}, u32[]{:S(2)}, u32[]{:S(2)}) collective-permute-start(bf16[256,128]{1,0:T(8,128)(2,1)S(1)} %get-tuple-element.36), channel_id=1, source_target_pairs={{0,2},{2,4},{4,6},{6,0},{1,3},{3,5},{5,7},{7,1},{8,10},{10,12},{12... | collective-permute-start | bytes 196616 | tf_op jit(solution)/shard_map/ppermute | solution.py:193
  113.6 4.3 %collective-permute-start.13 = (bf16[256,128]{1,0:T(8,128)(2,1)S(1)}, bf16[256,128]{1,0:T(8,128)(2,1)S(1)}, u32[]{:S(2)}, u32[]{:S(2)}) collective-permute-start(bf16[256,128]{1,0:T(8,128)(2,1)S(1)} %get-tuple-element.37), channel_id=1, source_target_pairs={{0,6},{2,0},{4,2},{6,4},{1,7},{3,1},{5,3},{7,5},{8,14},{10,8},{12,... | collective-permute-start | bytes 196616 | tf_op jit(solution)/shard_map/ppermute | solution.py:193
  115.0 5.8 %collective-permute-start.12 = (bf16[256,128]{1,0:T(8,128)(2,1)S(1)}, bf16[256,128]{1,0:T(8,128)(2,1)S(1)}, u32[]{:S(2)}, u32[]{:S(2)}) collective-permute-start(bf16[256,128]{1,0:T(8,128)(2,1)S(1)} %get-tuple-element.38), channel_id=1, source_target_pairs={{0,4},{2,6},{4,0},{6,2},{1,5},{3,7},{5,1},{7,3},{8,12},{10,14},{12... | collective-permute-start | bytes 196616 | tf_op jit(solution)/shard_map/ppermute | solution.py:193
  121.3 1.3 collective-permute-start.15

commit v7 on v6

--- a/solution.py
+++ b/solution.py
@@ -298,14 +298,12 @@
     unit = jnp.where(lane - HALF == row, 1.0, 0.0)
     work = jnp.where(lane < HALF, jnp.concatenate([square, square], axis=1), unit)
     inverse = inverse_factor(work)[:, HALF:] * scale
-    for block in range(2):
-        out[block] = lax.dot_general(
-            inverse,
-            filtered[:, block * HALF : (block + 1) * HALF],
-            (((1,), (1,)), ((), ())),
-            precision=HIGHEST,
-            preferred_element_type=F32,
-        )
+    rows = filtered.shape[0]
+    both = jnp.concatenate([filtered[:, :HALF], filtered[:, HALF:]], axis=0)
+    basis = lax.dot_general(
+        inverse, both, (((1,), (1,)), ((), ())), precision=HIGHEST, preferred_element_type=F32
+    )
+    out[0], out[1] = basis[:, :rows], basis[:, rows:]
 
 
 def on_device(tiles, tile_row, tile_col, tile_count, block_vectors):

time: 151 us -> 151 us (level)
  no operation moved by 1% of the time
where the time goes in v7:
time: 151 us
  blocking collectives  87.3 us (58%)
  waiting for transfers between devices  22.8 us (15%)
  starting transfers between devices  20.2 us (13%)
  Pallas kernels  14.9 us (10%)
  local copies, waits for them, and re-layouts  4.87 us (3%)
    all_to_all x3, blocking collectives, window(): return lax.all_to_all(pieces, 'z', 0, 0)  62.4 us
    ppermute x9, waiting for transfers between devices, apply_graph(): lax.ppermute(part, 'y', [(y, (y + step) % Y) for y in range(Y)])  16 us
    pallas_call x15, Pallas kernels, call(): pl.pallas_call(kernel, out_shape=tuple((jax.ShapeDtypeStruct(*s) for s in...  14.9 us
    all_to_all x1, blocking collectives, on_device(): lax.all_to_all(jnp.broadcast_to(gram[None], (X * Y,) + gram.shape), ('x',...  13.8 us
    ppermute x9, starting transfers between devices, apply_graph(): lax.ppermute(part, 'y', [(y, (y + step) % Y) for y in range(Y)])  12.1 us
    all_to_all x1, blocking collectives, on_device(): lax.all_to_all(jnp.broadcast_to(gram[None], (Z,) + gram.shape), 'z', 0, 0)  11.1 us
    ppermute x3, starting transfers between devices, window(): other = lax.ppermute(own, ALL, x_neighbour_pairs())  7.47 us
    unnamed x8, local copies, waits for them, and re-layouts  4.84 us
  transfers between devices with their start and end apart: 16, of which 14 were waited for; matrix products, arithmetic and copies ran while one was open for 0% of the time, Pallas kernels for 3%

profile of v7, /device:TPU:8, one launch (start us, length us, event | category | flops | bytes accessed | tf_op | source)
XLA Modules:
  0.0 151.0 jit_solution(12833619387204130226)
XLA Ops:
  0.0 0.9 copy-done.1
  1.0 2.8 %collective-permute-start = (bf16[256,128]{1,0:T(8,128)(2,1)S(1)}, bf16[256,128]{1,0:T(8,128)(2,1)S(1)}, u32[]{:S(2)}, u32[]{:S(2)}) collective-permute-start(bf16[256,128]{1,0:T(8,128)(2,1)S(1)} %shard_map.55.own.refs_5_), channel_id=1, source_target_pairs={{0,192},{1,193},{2,194},{3,195},{4,196},{5,197},{6,198},{7,199},{8... | collective-permute-start | bytes 196616 | tf_op jit(solution)/shard_map/ppermute | solution.py:103
  4.5 4.0 %copy-done = bf16[10,2048,256]{2,1,0:T(8,128)(2,1)S(1)} copy-done((bf16[10,2048,256]{2,1,0:T(8,128)(2,1)S(1)}, bf16[10,2048,256]{2,1,0:T(8,128)(2,1)}, u32[]{:S(2)}) %copy-start) | copy-done | bytes 10485784
  8.6 24.2 %all_to_all.25.slots = bf16[8,256,128]{2,1,0:T(8,128)(2,1)S(1)} all-to-all(bf16[8,256,128]{2,1,0:T(8,128)(2,1)S(1)} %shard_map.57), channel_id=1, replica_groups=mesh['x'=4,'z'=8,'y'=4,'core'=2] {'z'}, dimensions={0} | all-to-all | bytes 1048576 | tf_op jit(solution)/shard_map/all_to_all | solution.py:113
  32.8 1.9 %shard_map.58 = (f32[4,256,128]{2,1,0:T(8,128)S(1)}, bf16[10,256,128]{2,1,0:T(8,128)(2,1)S(1)}) custom-call(s32[10]{0:T(128)S(1)} %copy-done.2, s32[10]{0:T(128)S(1)} %copy-done.3, s32[1]{0:T(128)S(6)} %copy.6.refs_2_.tile_count, bf16[10,2048,256]{2,1,0:T(8,128)(2,1)S(1)} %copy-done, bf16[8,256,128]{2,1,0:T(8,128)(2,1)S(1)} %all_to_all.25.slots), custom_call_target="tpu_custom_call" | custom-call | flops 671088640 | bytes 5242880 | tf_op jit(solution)/shard_map/pallas_call | solution.py:28
  34.8 1.5 %shard_map.59.refs_0_ = f32[4,256,128]{2,1,0:T(8,128)S(1)} custom-call(bf16[10,2048,256]{2,1,0:T(8,128)(2,1)S(1)} %copy-done, bf16[10,256,128]{2,1,0:T(8,128)(2,1)S(1)} %get-tuple-element.19.rhs), custom_call_target="tpu_custom_call" | custom-call | flops 671088640 | bytes 5242880 | tf_op jit(solution)/shard_map/pallas_call | solution.py:28
  36.7 1.7 %collective-permute-start.4 = (f32[256,128]{1,0:T(8,128)S(1)}, f32[256,128]{1,0:T(8,128)S(1)}, u32[]{:S(2)}, u32[]{:S(2)}) collective-permute-start(f32[256,128]{1,0:T(8,128)S(1)} %get-tuple-element.39), channel_id=1, source_target_pairs={{0,2},{2,4},{4,6},{6,0},{1,3},{3,5},{5,7},{7,1},{8,10},{10,12},{12... | collective-permute-start | bytes 393224 | tf_op jit(solution)/shard_map/ppermute | solution.py:193
  38.8 2.3 %collective-permute-start.2 = (f32[256,128]{1,0:T(8,128)S(1)}, f32[256,128]{1,0:T(8,128)S(1)}, u32[]{:S(2)}, u32[]{:S(2)}) collective-permute-start(f32[256,128]{1,0:T(8,128)S(1)} %get-tuple-element.41), channel_id=1, source_target_pairs={{0,4},{2,6},{4,0},{6,2},{1,5},{3,7},{5,1},{7,3},{8,12},{10,14},{12... | collective-permute-start | bytes 393224 | tf_op jit(solution)/shard_map/ppermute | solution.py:193
  41.1 1.2 collective-permute-done.4.refs_4_
  42.3 1.7 %collective-permute-done.3.refs_3_ = f32[256,128]{1,0:T(8,128)S(1)} collective-permute-done((f32[256,128]{1,0:T(8,128)S(1)}, f32[256,128]{1,0:T(8,128)S(1)}, u32[]{:S(2)}, u32[]{:S(2)}) %collective-permute-start.3) | collective-permute-done | bytes 131104 | tf_op jit(solution)/shard_map/ppermute | solution.py:193
  44.0 3.1 %collective-permute-done.2.refs_2_ = f32[256,128]{1,0:T(8,128)S(1)} collective-permute-done((f32[256,128]{1,0:T(8,128)S(1)}, f32[256,128]{1,0:T(8,128)S(1)}, u32[]{:S(2)}, u32[]{:S(2)}) %collective-permute-start.2) | collective-permute-done | bytes 131104 | tf_op jit(solution)/shard_map/ppermute | solution.py:193
  47.3 1.8 %collective-permute-start.5 = (bf16[272,128]{1,0:T(8,128)(2,1)S(1)}, bf16[272,128]{1,0:T(8,128)(2,1)S(1)}, u32[]{:S(2)}, u32[]{:S(2)}) collective-permute-start(bf16[272,128]{1,0:T(8,128)(2,1)S(1)} %get-tuple-element.21.own), channel_id=1, source_target_pairs={{0,192},{1,193},{2,194},{3,195},{4,196},{5,197},{6,198},{7,199},{8... | collective-permute-start | bytes 208904 | tf_op jit(solution)/shard_map/ppermute | solution.py:103
  49.1 2.6 %collective-permute-done.5.other = bf16[272,128]{1,0:T(8,128)(2,1)S(1)} collective-permute-done((bf16[272,128]{1,0:T(8,128)(2,1)S(1)}, bf16[272,128]{1,0:T(8,128)(2,1)S(1)}, u32[]{:S(2)}, u32[]{:S(2)}) %collective-permute-start.5) | collective-permute-done | bytes 69664 | tf_op jit(solution)/shard_map/ppermute | solution.py:103
  51.8 19.0 %all_to_all.26.slots = bf16[8,272,128]{2,1,0:T(8,128)(2,1)S(1)} all-to-all(bf16[8,272,128]{2,1,0:T(8,128)(2,1)S(1)} %shard_map.61), channel_id=1, replica_groups=mesh['x'=4,'z'=8,'y'=4,'core'=2] {'z'}, dimensions={0} | all-to-all | bytes 1114112 | tf_op jit(solution)/shard_map/all_to_all | solution.py:113
  70.8 1.9 %shard_map.62 = (f32[4,264,128]{2,1,0:T(8,128)S(1)}, bf16[10,256,128]{2,1,0:T(8,128)(2,1)S(1)}, f32[8,128]{1,0:T(8,128)S(1)}) custom-call(s32[10]{0:T(128)S(1)} %copy-done.2, s32[10]{0:T(128)S(1)} %copy-done.3, s32[1]{0:T(128)S(6)} %copy.6.refs_2_.tile_count, bf16[10,2048,256]{2,1,0:T(8,128)(2,1)S(1)} %copy-done, bf16[8,272,128]{2,1,0:T(8,128)(2,1)S(1)} %all_to_all.26.slots), custom_call_target="tpu_custom_call" | custom-call | flops 671088640 | bytes 5242880 | tf_op jit(solution)/shard_map/pallas_call | solution.py:28
  73.0 1.5 %shard_map.63.refs_0_ = f32[4,264,128]{2,1,0:T(8,128)S(1)} custom-call(bf16[10,2048,256]{2,1,0:T(8,128)(2,1)S(1)} %copy-done, bf16[10,256,128]{2,1,0:T(8,128)(2,1)S(1)} %get-tuple-element.22.rhs, f32[8,128]{1,0:T(8,128)S(1)} %get-tuple-element.23.refs_0_), custom_call_target="tpu_custom_call" | custom-call | flops 671088640 | bytes 5242880 | tf_op jit(solution)/shard_map/pallas_call | solution.py:28
  75.1 2.0 %collective-permute-start.8 = (f32[264,128]{1,0:T(8,128)S(1)}, f32[264,128]{1,0:T(8,128)S(1)}, u32[]{:S(2)}, u32[]{:S(2)}) collective-permute-start(f32[264,128]{1,0:T(8,128)S(1)} %get-tuple-element.34), channel_id=1, source_target_pairs={{0,6},{2,0},{4,2},{6,4},{1,7},{3,1},{5,3},{7,5},{8,14},{10,8},{12,... | collective-permute-start | bytes 405512 | tf_op jit(solution)/shard_map/ppermute | solution.py:193
  77.1 1.6 %collective-permute-start.7 = (f32[264,128]{1,0:T(8,128)S(1)}, f32[264,128]{1,0:T(8,128)S(1)}, u32[]{:S(2)}, u32[]{:S(2)}) collective-permute-start(f32[264,128]{1,0:T(8,128)S(1)} %get-tuple-element.35), channel_id=1, source_target_pairs={{0,4},{2,6},{4,0},{6,2},{1,5},{3,7},{5,1},{7,3},{8,12},{10,14},{12... | collective-permute-start | bytes 405512 | tf_op jit(solution)/shard_map/ppermute | solution.py:193
  78.6 2.8 %collective-permute-done.9.refs_4_ = f32[264,128]{1,0:T(8,128)S(1)} collective-permute-done((f32[264,128]{1,0:T(8,128)S(1)}, f32[264,128]{1,0:T(8,128)S(1)}, u32[]{:S(2)}, u32[]{:S(2)}) %collective-permute-start.9) | collective-permute-done | bytes 135200 | tf_op jit(solution)/shard_map/ppermute | solution.py:193
  81.4 3.5 %collective-permute-done.7.refs_2_ = f32[264,128]{1,0:T(8,128)S(1)} collective-permute-done((f32[264,128]{1,0:T(8,128)S(1)}, f32[264,128]{1,0:T(8,128)S(1)}, u32[]{:S(2)}, u32[]{:S(2)}) %collective-permute-start.7) | collective-permute-done | bytes 135200 | tf_op jit(solution)/shard_map/ppermute | solution.py:193
  84.9 2.8 %collective-permute-start.10 = (bf16[272,128]{1,0:T(8,128)(2,1)S(1)}, bf16[272,128]{1,0:T(8,128)(2,1)S(1)}, u32[]{:S(2)}, u32[]{:S(2)}) collective-permute-start(bf16[272,128]{1,0:T(8,128)(2,1)S(1)} %get-tuple-element.25.own), channel_id=1, source_target_pairs={{0,192},{1,193},{2,194},{3,195},{4,196},{5,197},{6,198},{7,199},{8... | collective-permute-start | bytes 208904 | tf_op jit(solution)/shard_map/ppermute | solution.py:103
  87.7 1.9 %collective-permute-done.10.other = bf16[272,128]{1,0:T(8,128)(2,1)S(1)} collective-permute-done((bf16[272,128]{1,0:T(8,128)(2,1)S(1)}, bf16[272,128]{1,0:T(8,128)(2,1)S(1)}, u32[]{:S(2)}, u32[]{:S(2)}) %collective-permute-start.10) | collective-permute-done | bytes 69664 | tf_op jit(solution)/shard_map/ppermute | solution.py:103
  89.8 19.1 %all_to_all.27.slots = bf16[8,272,128]{2,1,0:T(8,128)(2,1)S(1)} all-to-all(bf16[8,272,128]{2,1,0:T(8,128)(2,1)S(1)} %shard_map.65), channel_id=1, replica_groups=mesh['x'=4,'z'=8,'y'=4,'core'=2] {'z'}, dimensions={0} | all-to-all | bytes 1114112 | tf_op jit(solution)/shard_map/all_to_all | solution.py:113
  109.0 1.9 %shard_map.66 = (f32[4,256,128]{2,1,0:T(8,128)S(1)}, bf16[10,256,128]{2,1,0:T(8,128)(2,1)S(1)}, f32[8,128]{1,0:T(8,128)S(1)}) custom-call(s32[10]{0:T(128)S(1)} %copy-done.2, s32[10]{0:T(128)S(1)} %copy-done.3, s32[1]{0:T(128)S(6)} %copy.6.refs_2_.tile_count, bf16[10,2048,256]{2,1,0:T(8,128)(2,1)S(1)} %copy-done, bf16[8,272,128]{2,1,0:T(8,128)(2,1)S(1)} %all_to_all.27.slots), custom_call_target="tpu_custom_call" | custom-call | flops 671088640 | bytes 5242880 | tf_op jit(solution)/shard_map/pallas_call | solution.py:28
  111.0 1.5 %shard_map.67.refs_0_ = f32[4,256,128]{2,1,0:T(8,128)S(1)} custom-call(bf16[10,2048,256]{2,1,0:T(8,128)(2,1)S(1)} %copy-done, bf16[10,256,128]{2,1,0:T(8,128)(2,1)S(1)} %get-tuple-element.27.rhs), custom_call_target="tpu_custom_call" | custom-call | flops 671088640 | bytes 5242880 | tf_op jit(solution)/shard_map/pallas_call | solution.py:28
  113.6 1.4 collective-permute-start.13
  115.0 2.0 %collective-permute-start.12 = (bf16[256,128]{1,0:T(8,128)(2,1)S(1)}, bf16[256,128]{1,0:T(8,128)(2,1)S(1)}, u32[]{:S(2)}, u32[]{:S(2)}) collective-permute-start(bf16[256,128]{1,0:T(8,128)(2,1)S(1)} %get-tuple-element.38), channel_id=1, source_target_pairs={{0,4},{2,6},{4,0},{6,2},{1,5},{3,7},{5,1},{7,3},{8,12},{10,14},{12... | collective-permute-start | bytes 196616 | tf_op jit(solution)/shard_map/ppermute | solution.py:193
  117.8 2.9 %collective-permute-done.12.refs_2_ = bf16[256,128]{1,0:T(8,128)(2,1)S(1)} collective-permute-done((bf16[256,128]{1,0:T(8,128)(2,1)S(1)}, bf16[256,128]{1,0:T(8,128)(2,1)S(1)}, u32[]{:S(2)}, u32[]{:S(2)}) %collective-permute-start.12) | collective-permute-done | bytes 65568 | tf_op jit(solution)/shard_map/ppermute | solution.py:193
  121.5 1.2 collective-permute-done.15
  122.6 13.8 %all_to_all.28 = f32[16,24,128]{2,1,0:T(8,128)S(1)} all-to-all(f32[16,24,128]{2,1,0:T(8,128)S(1)} %broadcast_in_dim.4), channel_id=1, replica_groups=mesh['x'=4,'z'=8,'y'=4,'core'=2] {'x','y'}, dimensions={0} | all-to-all | bytes 393216 | tf_op jit(solution)/shard_map/all_to_all | solution.py:343
  136.5 11.1 %all_to_all.29.grams = f32[8,24,128]{2,1,0:T(8,128)S(1)} all-to-all(f32[8,24,128]{2,1,0:T(8,128)S(1)} %broadcast_in_dim.5), channel_id=1, replica_groups=mesh['x'=4,'z'=8,'y'=4,'core'=2] {'z'}, dimensions={0} | all-to-all | bytes 196608 | tf_op jit(solution)/shard_map/all_to_all | solution.py:345
  147.6 3.4 %shard_map.69 = f32[2,64,256]{2,1,0:T(8,128)} custom-call(f32[8,24,128]{2,1,0:T(8,128)S(1)} %all_to_all.29.grams, f32[256,128]{1,0:T(8,128)S(1)} %get-tuple-element.32.filtered), custom_call_target="tpu_custom_call" | custom-call | tf_op jit(solution)/shard_map/pallas_call | solution.py:28
  (35 shorter events, 5.2 us)
Async XLA Ops:
  0.0 8.5 %copy-start.3 = (s32[10]{0:T(128)S(1)}, s32[10]{0:T(128)}, u32[]{:S(2)}) copy-start(s32[10]{0:T(128)} %tile_col.5) | copy-start | bytes 124
  0.0 8.5 %copy-start.2 = (s32[10]{0:T(128)S(1)}, s32[10]{0:T(128)}, u32[]{:S(2)}) copy-start(s32[10]{0:T(128)} %tile_row.5) | copy-start | bytes 124
  0.0 0.9 copy-start.1
  1.0 7.5 %collective-permute-start = (bf16[256,128]{1,0:T(8,128)(2,1)S(1)}, bf16[256,128]{1,0:T(8,128)(2,1)S(1)}, u32[]{:S(2)}, u32[]{:S(2)}) collective-permute-start(bf16[256,128]{1,0:T(8,128)(2,1)S(1)} %shard_map.55.own.refs_5_), channel_id=1, source_target_pairs={{0,192},{1,193},{2,194},{3,195},{4,196},{5,197},{6,198},{7,199},{8... | collective-permute-start | bytes 196616 | tf_op jit(solution)/shard_map/ppermute | solution.py:103
  4.5 4.0 %copy-start = (bf16[10,2048,256]{2,1,0:T(8,128)(2,1)S(1)}, bf16[10,2048,256]{2,1,0:T(8,128)(2,1)}, u32[]{:S(2)}) copy-start(bf16[10,2048,256]{2,1,0:T(8,128)(2,1)} %tiles.13) | copy-start | bytes 31457284
  34.7 2.0 %collective-permute-start.1 = (f32[4,256,128]{2,1,0:T(8,128)S(1)}, f32[4,256,128]{2,1,0:T(8,128)S(1)}, u32[]{:S(2)}, u32[]{:S(2)}) collective-permute-start(f32[4,256,128]{2,1,0:T(8,128)S(1)} %get-tuple-element.20), channel_id=1, source_target_pairs={{0,1},{1,0},{2,3},{3,2},{4,5},{5,4},{6,7},{7,6},{8,9},{9,8},{10,11... | collective-permute-start | bytes 1572872 | tf_op jit(solution)/shard_map/ppermute | solution.py:185
  36.7 5.6 %collective-permute-start.4 = (f32[256,128]{1,0:T(8,128)S(1)}, f32[256,128]{1,0:T(8,128)S(1)}, u32[]{:S(2)}, u32[]{:S(2)}) collective-permute-start(f32[256,128]{1,0:T(8,128)S(1)} %get-tuple-element.39), channel_id=1, source_target_pairs={{0,2},{2,4},{4,6},{6,0},{1,3},{3,5},{5,7},{7,1},{8,10},{10,12},{12... | collective-permute-start | bytes 393224 | tf_op jit(solution)/shard_map/ppermute | solution.py:193
  38.4 5.7 %collective-permute-start.3 = (f32[256,128]{1,0:T(8,128)S(1)}, f32[256,128]{1,0:T(8,128)S(1)}, u32[]{:S(2)}, u32[]{:S(2)}) collective-permute-start(f32[256,128]{1,0:T(8,128)S(1)} %get-tuple-element.40), channel_id=1, source_target_pairs={{0,6},{2,0},{4,2},{6,4},{1,7},{3,1},{5,3},{7,5},{8,14},{10,8},{12,... | collective-permute-start | bytes 393224 | tf_op jit(solution)/shard_map/ppermute | solution.py:193
  38.8 8.3 %collective-permute-start.2 = (f32[256,128]{1,0:T(8,128)S(1)}, f32[256,128]{1,0:T(8,128)S(1)}, u32[]{:S(2)}, u32[]{:S(2)}) collective-permute-start(f32[256,128]{1,0:T(8,128)S(1)} %get-tuple-element.41), channel_id=1, source_target_pairs={{0,4},{2,6},{4,0},{6,2},{1,5},{3,7},{5,1},{7,3},{8,12},{10,14},{12... | collective-permute-start | bytes 393224 | tf_op jit(solution)/shard_map/ppermute | solution.py:193
  47.3 4.4 %collective-permute-start.5 = (bf16[272,128]{1,0:T(8,128)(2,1)S(1)}, bf16[272,128]{1,0:T(8,128)(2,1)S(1)}, u32[]{:S(2)}, u32[]{:S(2)}) collective-permute-start(bf16[272,128]{1,0:T(8,128)(2,1)S(1)} %get-tuple-element.21.own), channel_id=1, source_target_pairs={{0,192},{1,193},{2,194},{3,195},{4,196},{5,197},{6,198},{7,199},{8... | collective-permute-start | bytes 208904 | tf_op jit(solution)/shard_map/ppermute | solution.py:103
  72.7 2.2 %collective-permute-start.6 = (f32[4,264,128]{2,1,0:T(8,128)S(1)}, f32[4,264,128]{2,1,0:T(8,128)S(1)}, u32[]{:S(2)}, u32[]{:S(2)}) collective-permute-start(f32[4,264,128]{2,1,0:T(8,128)S(1)} %get-tuple-element.24), channel_id=1, source_target_pairs={{0,1},{1,0},{2,3},{3,2},{4,5},{5,4},{6,7},{7,6},{8,9},{9,8},{10,11... | collective-permute-start | bytes 1622024 | tf_op jit(solution)/shard_map/ppermute | solution.py:185
  75.0 6.4 %collective-permute-start.9 = (f32[264,128]{1,0:T(8,128)S(1)}, f32[264,128]{1,0:T(8,128)S(1)}, u32[]{:S(2)}, u32[]{:S(2)}) collective-permute-start(f32[264,128]{1,0:T(8,128)S(1)} %get-tuple-element.33), channel_id=1, source_target_pairs={{0,2},{2,4},{4,6},{6,0},{1,3},{3,5},{5,7},{7,1},{8,10},{10,12},{12... | collective-permute-start | bytes 405512 | tf_op jit(solution)/shard_map/ppermute | solution.py:193
  75.1 6.3 %collective-permute-start.8 = (f32[264,128]{1,0:T(8,128)S(1)}, f32[264,128]{1,0:T(8,128)S(1)}, u32[]{:S(2)}, u32[]{:S(2)}) collective-permute-start(f32[264,128]{1,0:T(8,128)S(1)} %get-tuple-element.34), channel_id=1, source_target_pairs={{0,6},{2,0},{4,2},{6,4},{1,7},{3,1},{5,3},{7,5},{8,14},{10,8},{12,... | collective-permute-start | bytes 405512 | tf_op jit(solution)/shard_map/ppermute | solution.py:193
  77.1 7.8 %collective-permute-start.7 = (f32[264,128]{1,0:T(8,128)S(1)}, f32[264,128]{1,0:T(8,128)S(1)}, u32[]{:S(2)}, u32[]{:S(2)}) collective-permute-start(f32[264,128]{1,0:T(8,128)S(1)} %get-tuple-element.35), channel_id=1, source_target_pairs={{0,4},{2,6},{4,0},{6,2},{1,5},{3,7},{5,1},{7,3},{8,12},{10,14},{12... | collective-permute-start | bytes 405512 | tf_op jit(solution)/shard_map/ppermute | solution.py:193
  84.9 4.8 %collective-permute-start.10 = (bf16[272,128]{1,0:T(8,128)(2,1)S(1)}, bf16[272,128]{1,0:T(8,128)(2,1)S(1)}, u32[]{:S(2)}, u32[]{:S(2)}) collective-permute-start(bf16[272,128]{1,0:T(8,128)(2,1)S(1)} %get-tuple-element.25.own), channel_id=1, source_target_pairs={{0,192},{1,193},{2,194},{3,195},{4,196},{5,197},{6,198},{7,199},{8... | collective-permute-start | bytes 208904 | tf_op jit(solution)/shard_map/ppermute | solution.py:103
  110.9 2.0 %collective-permute-start.11 = (f32[4,256,128]{2,1,0:T(8,128)S(1)}, f32[4,256,128]{2,1,0:T(8,128)S(1)}, u32[]{:S(2)}, u32[]{:S(2)}) collective-permute-start(f32[4,256,128]{2,1,0:T(8,128)S(1)} %get-tuple-element.28), channel_id=1, source_target_pairs={{0,1},{1,0},{2,3},{3,2},{4,5},{5,4},{6,7},{7,6},{8,9},{9,8},{10,11... | collective-permute-start | bytes 1572872 | tf_op jit(solution)/shard_map/ppermute | solution.py:185
  112.9 4.3 %collective-permute-start.14 = (bf16[256,128]{1,0:T(8,128)(2,1)S(1)}, bf16[256,128]{1,0:T(8,128)(2,1)S(1)}, u32[]{:S(2)}, u32[]{:S(2)}) collective-permute-start(bf16[256,128]{1,0:T(8,128)(2,1)S(1)} %get-tuple-element.36), channel_id=1, source_target_pairs={{0,2},{2,4},{4,6},{6,0},{1,3},{3,5},{5,7},{7,1},{8,10},{10,12},{12... | collective-permute-start | bytes 196616 | tf_op jit(solution)/shard_map/ppermute | solution.py:193
  113.6 4.3 %collective-permute-start.13 = (bf16[256,128]{1,0:T(8,128)(2,1)S(1)}, bf16[256,128]{1,0:T(8,128)(2,1)S(1)}, u32[]{:S(2)}, u32[]{:S(2)}) collective-permute-start(bf16[256,128]{1,0:T(8,128)(2,1)S(1)} %get-tuple-element.37), channel_id=1, source_target_pairs={{0,6},{2,0},{4,2},{6,4},{1,7},{3,1},{5,3},{7,5},{8,14},{10,8},{12,... | collective-permute-start | bytes 196616 | tf_op jit(solution)/shard_map/ppermute | solution.py:193
  115.0 5.8 %collective-permute-start.12 = (bf16[256,128]{1,0:T(8,128)(2,1)S(1)}, bf16[256,128]{1,0:T(8,128)(2,1)S(1)}, u32[]{:S(2)}, u32[]{:S(2)}) collective-permute-start(bf16[256,128]{1,0:T(8,128)(2,1)S(1)} %get-tuple-element.38), channel_id=1, source_target_pairs={{0,4},{2,6},{4,0},{6,2},{1,5},{3,7},{5,1},{7,3},{8,12},{10,14},{12... | collective-permute-start | bytes 196616 | tf_op jit(solution)/shard_map/ppermute | solution.py:193
  121.4 1.3 collective-permute-start.15
